TPU v7x, 32 devices: a whole 2x2x4 slice. The times are simulated.
32 devices in a mesh: section: 2 (over core), head: 4 (over z), ctx: 4 (over y, x).
Axes of the slice: x: 2, y: 2, z: 4, core: 2. Of those that a mesh axis runs over, the one named last changes fastest.
Arguments:
- layer_input: bfloat16 [4, 512, 1536], P(None, ('ctx', 'head')), may hold values from -6 to 6
- out_cotangent: bfloat16 [4, 512, 1536], P(None, ('ctx', 'head')), may hold values from -6 to 6
- block_order: int32 [4, 8], replicated, may hold values from 0 to 7, each once within a row
- gain_attn: bfloat16 [2, 1536], P('section', 'ctx'), may hold values from 0.099609375 to 1.8984375
- w_query: bfloat16 [2, 1536, 1536], P('section', 'ctx', 'head'), may hold values from -0.15625 to 0.15625
- w_key: bfloat16 [2, 1536, 768], P('section', 'ctx', 'head'), may hold values from -0.15625 to 0.15625
- w_value: bfloat16 [2, 1536, 768], P('section', 'ctx', 'head'), may hold values from -0.15625 to 0.15625
- w_out: bfloat16 [2, 1536, 1536], P('section', 'head', 'ctx'), may hold values from -0.625 to 0.625
- gain_ffn: bfloat16 [2, 1536], P('section', 'ctx'), may hold values from 0.099609375 to 1.8984375
- w_gate: bfloat16 [2, 1536, 4096], P('section', 'ctx', 'head'), may hold values from -0.15625 to 0.15625
- w_up: bfloat16 [2, 1536, 4096], P('section', 'ctx', 'head'), may hold values from -0.15625 to 0.15625
- w_down: bfloat16 [2, 4096, 1536], P('section', 'head', 'ctx'), may hold values from -0.125 to 0.125
Outputs:
- layer_out: bfloat16 [2, 4, 512, 1536], P('section', None, ('ctx', 'head'))
- in_grad: float32 [2, 4, 512, 1536], P('section', None, ('ctx', 'head'))
- grad_gain_attn: float32 [2, 1536], P('section', 'ctx')
- grad_w_query: float32 [2, 1536, 1536], P('section', 'ctx', 'head')
- grad_w_key: float32 [2, 1536, 768], P('section', 'ctx', 'head')
- grad_w_value: float32 [2, 1536, 768], P('section', 'ctx', 'head')
- grad_w_out: float32 [2, 1536, 1536], P('section', 'head', 'ctx')
- grad_gain_ffn: float32 [2, 1536], P('section', 'ctx')
- grad_w_gate: float32 [2, 1536, 4096], P('section', 'ctx', 'head')
- grad_w_up: float32 [2, 1536, 4096], P('section', 'ctx', 'head')
- grad_w_down: float32 [2, 4096, 1536], P('section', 'head', 'ctx')
Inputs may be any that keep to these rules, and one draw needn't show every extreme that they name: `block_order`: row m gives, for each of the 8 stored blocks of sequence m, its block of positions; each row is a permutation.
All inputs are finite; a program needn't handle non-finite values.
Results may differ from a plain program's by a relative error of at most 0.035.
Values may be sent and summed in bfloat16 or wider, within the bound.
No kernel may reach another device: no remote copies, remote signals or barrier semaphores. Data moves between devices by JAX's collectives and lax.ppermute only.
A program may use at most 128 MiB of HBM per device.

v0:
```python
import jax
import jax.numpy as jnp
from jax import lax
from jax.sharding import PartitionSpec as P

HEAD_DIM = 96


epsilon = 1e-05
rope_base = 100000.0
masked = -1e30


def shifted(value, axis, steps):
    count = lax.axis_size(axis)
    first, last = (max(0, -steps), min(count, count - steps))
    return lax.ppermute(value, axis, [(source, source + steps) for source in range(first, last)])


def rotation(positions, half_dim):
    steps_f = jnp.arange(half_dim, dtype=jnp.float32)
    frequency = jnp.power(rope_base, steps_f * (-2.0 / (2 * half_dim)))
    angles = positions.astype(jnp.float32)[:, None] * frequency[None, :]
    return (jnp.cos(angles), jnp.sin(angles))


def rotate(values, cosine, sine_tab):
    half_dim = values.shape[-1] // 2
    first_half = values[..., :half_dim]
    second_half = values[..., half_dim:]
    return jnp.concatenate(
        [
            first_half * cosine - second_half * sine_tab,
            second_half * cosine + first_half * sine_tab,
        ],
        axis=-1,
    )


def rotate_back(grad_vals, cosine, sine_tab):
    half_dim = grad_vals.shape[-1] // 2
    first_half = grad_vals[..., :half_dim]
    second_half = grad_vals[..., half_dim:]
    return jnp.concatenate(
        [
            first_half * cosine + second_half * sine_tab,
            second_half * cosine - first_half * sine_tab,
        ],
        axis=-1,
    )


def row_places(order_row, offset, amount, block_rows):
    stored = offset + jnp.arange(amount, dtype=jnp.int32)
    owner_block = stored // block_rows
    matches = owner_block[:, None] == jnp.arange(order_row.shape[0], dtype=jnp.int32)[None, :]
    base_block = jnp.sum(jnp.where(matches, order_row[None, :], 0), axis=1)
    return base_block * block_rows + stored % block_rows


def spread(row_block):
    return lax.all_gather(row_block, "head", axis=0, tiled=True)


def spread_grads(row_block):
    return lax.all_gather(row_block, "head", axis=0, tiled=True)


def settle_rows(partial_terms):
    return lax.psum_scatter(
        partial_terms.astype(jnp.bfloat16), "head", scatter_dimension=0, tiled=True
    ).astype(jnp.float32)


def branch_total(left_rows, right_mat):
    return lax.psum_scatter(
        jnp.dot(left_rows, right_mat, preferred_element_type=jnp.float32).astype(jnp.bfloat16),
        "head",
        scatter_dimension=0,
        tiled=True,
    ).astype(jnp.float32)


def norm_back(d_normed, residual, scale_rows, gain, carried):
    unit_rows = residual * scale_rows
    grad_gain = jnp.sum(d_normed * unit_rows, axis=0)
    d_unit = d_normed * gain
    d_resid = carried + scale_rows * (
        d_unit - unit_rows * jnp.mean(d_unit * unit_rows, axis=1, keepdims=True)
    )
    return (grad_gain, d_resid)


def forward(weights, layer_in, order_row):
    gain_attn, w_query, w_key, w_value, w_out, gain_ffn, w_gate, w_up, w_down = weights
    residual = layer_in.astype(jnp.float32)
    scale_attn = lax.rsqrt(jnp.mean(residual * residual, axis=1, keepdims=True) + epsilon)
    normed_a = spread((residual * scale_attn * gain_attn).astype(jnp.bfloat16))
    span_rows = normed_a.shape[0]
    block_rows = span_rows // 2
    places_q = row_places(order_row, lax.axis_index("ctx") * span_rows, span_rows, block_rows)
    cosine, sine_tab = rotation(places_q, HEAD_DIM // 2)
    cosine = cosine[:, None, :]
    sine_tab = sine_tab[:, None, :]
    q_lin = jnp.dot(normed_a, w_query, preferred_element_type=jnp.float32).reshape(
        span_rows, -1, HEAD_DIM
    )
    k_lin = jnp.dot(normed_a, w_key, preferred_element_type=jnp.float32).reshape(
        span_rows, -1, HEAD_DIM
    )
    value_rows = (
        jnp.dot(normed_a, w_value, preferred_element_type=jnp.float32)
        .astype(jnp.bfloat16)
        .reshape(span_rows, -1, HEAD_DIM)
    )
    kv_heads = k_lin.shape[1]
    group_size = q_lin.shape[1] // kv_heads
    query_rows = (
        rotate(q_lin, cosine, sine_tab)
        .astype(jnp.bfloat16)
        .reshape(span_rows, kv_heads, group_size, HEAD_DIM)
    )
    key_rows = rotate(k_lin, cosine, sine_tab).astype(jnp.bfloat16)
    inv_root = HEAD_DIM ** (-0.5)
    start_max = jnp.full((kv_heads, group_size, span_rows), masked, jnp.float32)
    key_piece = lax.all_gather(key_rows, "ctx", axis=0, tiled=True)
    value_piece = lax.all_gather(value_rows, "ctx", axis=0, tiled=True)
    places_k = row_places(order_row, jnp.int32(0), key_piece.shape[0], block_rows)
    allowed = places_k[None, None, None, :] <= places_q[None, None, :, None]
    scores = (
        jnp.einsum("sagd,kad->agsk", query_rows, key_piece, preferred_element_type=jnp.float32)
        * inv_root
    )
    scores = jnp.where(allowed, scores, masked)
    new_max = jnp.maximum(start_max, jnp.max(scores, axis=-1))
    weight = jnp.where(allowed, jnp.exp(scores - new_max[..., None]), 0.0)
    running_sum = jnp.sum(weight, axis=-1)
    running_out = jnp.einsum(
        "agsk,kad->sagd",
        weight.astype(jnp.bfloat16),
        value_piece,
        preferred_element_type=jnp.float32,
    )
    log_total = new_max + jnp.log(running_sum)
    attn_mix = (
        (running_out / jnp.transpose(running_sum, (2, 0, 1))[..., None])
        .astype(jnp.bfloat16)
        .reshape(span_rows, -1)
    )
    mid_stream = residual + branch_total(attn_mix, w_out)
    scale_ffn = lax.rsqrt(jnp.mean(mid_stream * mid_stream, axis=1, keepdims=True) + epsilon)
    normed_b = spread((mid_stream * scale_ffn * gain_ffn).astype(jnp.bfloat16))
    gate_pre = jnp.dot(normed_b, w_gate, preferred_element_type=jnp.float32)
    up_pre = jnp.dot(normed_b, w_up, preferred_element_type=jnp.float32)
    hidden = (jax.nn.silu(gate_pre) * up_pre).astype(jnp.bfloat16)
    result = (mid_stream + branch_total(hidden, w_down)).astype(jnp.bfloat16)
    stored = (
        residual,
        scale_attn,
        normed_a,
        places_q,
        cosine,
        sine_tab,
        query_rows,
        key_rows,
        value_rows,
        log_total,
        attn_mix,
        mid_stream,
        scale_ffn,
        normed_b,
        gate_pre,
        up_pre,
        hidden,
        order_row,
    )
    return (result, stored)


def backward(weights, stored, out_grad):
    gain_attn, w_query, w_key, w_value, w_out, gain_ffn, w_gate, w_up, w_down = weights
    (
        residual,
        scale_attn,
        normed_a,
        places_q,
        cosine,
        sine_tab,
        query_rows,
        key_rows,
        value_rows,
        log_total,
        attn_mix,
        mid_stream,
        scale_ffn,
        normed_b,
        gate_pre,
        up_pre,
        hidden,
        order_row,
    ) = stored
    span_rows = normed_a.shape[0]
    kv_heads = key_rows.shape[1]
    group_size = query_rows.shape[2]
    inv_root = HEAD_DIM ** (-0.5)
    d_ffn = spread_grads(out_grad.astype(jnp.bfloat16))
    grad_down = jnp.einsum("sf,sd->fd", hidden, d_ffn, preferred_element_type=jnp.float32)
    d_hidden = jnp.einsum("sd,fd->sf", d_ffn, w_down, preferred_element_type=jnp.float32)
    sigma_gate = jax.nn.sigmoid(gate_pre)
    d_gate = (d_hidden * up_pre * sigma_gate * (1.0 + gate_pre * (1.0 - sigma_gate))).astype(
        jnp.bfloat16
    )
    d_up = (d_hidden * gate_pre * sigma_gate).astype(jnp.bfloat16)
    grad_gate = jnp.einsum("sd,sf->df", normed_b, d_gate, preferred_element_type=jnp.float32)
    grad_up = jnp.einsum("sd,sf->df", normed_b, d_up, preferred_element_type=jnp.float32)
    d_joined_b = jnp.einsum(
        "sf,df->sd", d_gate, w_gate, preferred_element_type=jnp.float32
    ) + jnp.einsum("sf,df->sd", d_up, w_up, preferred_element_type=jnp.float32)
    d_normed_b = settle_rows(d_joined_b)
    grad_gain_ffn, d_mid = norm_back(d_normed_b, mid_stream, scale_ffn, gain_ffn, out_grad)
    d_attn = spread_grads(d_mid.astype(jnp.bfloat16))
    grad_out = jnp.einsum("sq,sd->qd", attn_mix, d_attn, preferred_element_type=jnp.float32)
    d_mix = jnp.einsum("sd,qd->sq", d_attn, w_out, preferred_element_type=jnp.float32).astype(
        jnp.bfloat16
    )
    key_all, value_all = (
        lax.all_gather(key_rows, "ctx", axis=0, tiled=True),
        lax.all_gather(value_rows, "ctx", axis=0, tiled=True),
    )
    seq_len = key_all.shape[0]
    key_block = min(512, seq_len)
    d_grouped = d_mix.reshape(span_rows, kv_heads, group_size, HEAD_DIM)
    mix_grouped = attn_mix.reshape(span_rows, kv_heads, group_size, HEAD_DIM)
    row_delta = jnp.transpose(
        jnp.sum(d_grouped.astype(jnp.float32) * mix_grouped.astype(jnp.float32), axis=-1), (1, 2, 0)
    )
    places_all = row_places(order_row, 0, seq_len, span_rows // 2).reshape(-1, key_block)

    def back_block(d_query, inputs):
        key_piece, value_piece, places_k = inputs
        allowed = places_k[None, None, None, :] <= places_q[None, None, :, None]
        scores = (
            jnp.einsum("sagd,kad->agsk", query_rows, key_piece, preferred_element_type=jnp.float32)
            * inv_root
        )
        scores = jnp.where(allowed, scores, masked)
        attn_prob = jnp.where(allowed, jnp.exp(scores - log_total[..., None]), 0.0)
        d_prob = jnp.einsum(
            "sagd,kad->agsk", d_grouped, value_piece, preferred_element_type=jnp.float32
        )
        d_score = (attn_prob * (d_prob - row_delta[..., None])).astype(jnp.bfloat16)
        d_query = d_query + jnp.einsum(
            "agsk,kad->sagd", d_score, key_piece, preferred_element_type=jnp.float32
        )
        d_key = jnp.einsum(
            "agsk,sagd->kad", d_score, query_rows, preferred_element_type=jnp.float32
        )
        d_value = jnp.einsum(
            "agsk,sagd->kad",
            attn_prob.astype(jnp.bfloat16),
            d_grouped,
            preferred_element_type=jnp.float32,
        )
        return (d_query, (d_key, d_value))

    start_query = jnp.zeros((span_rows, kv_heads, group_size, HEAD_DIM), jnp.float32)
    key_blocks = key_all.reshape(-1, key_block, kv_heads, HEAD_DIM)
    value_blocks = value_all.reshape(-1, key_block, kv_heads, HEAD_DIM)
    d_query, (key_terms, value_terms) = lax.scan(
        back_block, start_query, (key_blocks, value_blocks, places_all)
    )
    d_key, d_value = (
        lax.psum_scatter(
            key_terms.reshape(seq_len, kv_heads, HEAD_DIM).astype(jnp.bfloat16),
            "ctx",
            scatter_dimension=0,
            tiled=True,
        ).astype(jnp.float32),
        lax.psum_scatter(
            value_terms.reshape(seq_len, kv_heads, HEAD_DIM).astype(jnp.bfloat16),
            "ctx",
            scatter_dimension=0,
            tiled=True,
        ).astype(jnp.float32),
    )
    d_q_lin = (
        rotate_back(d_query.reshape(span_rows, -1, HEAD_DIM) * inv_root, cosine, sine_tab)
        .astype(jnp.bfloat16)
        .reshape(span_rows, -1)
    )
    d_k_lin = (
        rotate_back(d_key * inv_root, cosine, sine_tab).astype(jnp.bfloat16).reshape(span_rows, -1)
    )
    d_v_lin = d_value.astype(jnp.bfloat16).reshape(span_rows, -1)
    grad_query = jnp.einsum("sd,sq->dq", normed_a, d_q_lin, preferred_element_type=jnp.float32)
    grad_key = jnp.einsum("sd,sq->dq", normed_a, d_k_lin, preferred_element_type=jnp.float32)
    grad_value = jnp.einsum("sd,sq->dq", normed_a, d_v_lin, preferred_element_type=jnp.float32)
    d_joined_a = jnp.einsum("sq,dq->sd", d_q_lin, w_query, preferred_element_type=jnp.float32)
    d_joined_a = d_joined_a + jnp.einsum(
        "sq,dq->sd", d_k_lin, w_key, preferred_element_type=jnp.float32
    )
    d_joined_a = d_joined_a + jnp.einsum(
        "sq,dq->sd", d_v_lin, w_value, preferred_element_type=jnp.float32
    )
    d_normed_a = settle_rows(d_joined_a)
    grad_gain_attn, d_input = norm_back(d_normed_a, residual, scale_attn, gain_attn, d_mid)
    return (
        d_input,
        (
            grad_gain_attn,
            grad_query,
            grad_key,
            grad_value,
            grad_out,
            grad_gain_ffn,
            grad_gate,
            grad_up,
            grad_down,
        ),
    )


def local(
    layer_input,
    out_cotangent,
    block_order,
    gain_attn,
    w_query,
    w_key,
    w_value,
    w_out,
    gain_ffn,
    w_gate,
    w_up,
    w_down,
):
    section_index = lax.axis_index("section")
    first_section = section_index == 0
    micro_count = layer_input.shape[0]

    def fetch():
        return (
            lax.all_gather(gain_attn[0], "ctx", axis=0, tiled=True),
            lax.all_gather(w_query[0], "ctx", axis=0, tiled=True),
            lax.all_gather(w_key[0], "ctx", axis=0, tiled=True),
            lax.all_gather(w_value[0], "ctx", axis=0, tiled=True),
            lax.all_gather(w_out[0], "ctx", axis=1, tiled=True),
            lax.all_gather(gain_ffn[0], "ctx", axis=0, tiled=True),
            lax.all_gather(w_gate[0], "ctx", axis=0, tiled=True),
            lax.all_gather(w_up[0], "ctx", axis=0, tiled=True),
            lax.all_gather(w_down[0], "ctx", axis=1, tiled=True),
        )

    weights = fetch()
    received = jnp.zeros_like(layer_input[0])
    results = []
    keep_list = []
    for step_index in range(micro_count + 1):
        source = layer_input[min(step_index, micro_count - 1)]
        current = jnp.where(first_section, source, received)
        micro_index = jnp.clip(step_index - section_index, 0, micro_count - 1)
        order_row = lax.dynamic_index_in_dim(block_order, micro_index, 0, keepdims=False)
        result, stored = forward(weights, current, order_row)
        results.append(result)
        keep_list.append((current, order_row))
        if step_index < micro_count:
            received = shifted(result, "section", 1)
    layer_out = jnp.where(first_section, jnp.stack(results[:micro_count]), jnp.stack(results[1:]))[
        None
    ]
    weights_back = fetch()
    totals = tuple((jnp.zeros(item.shape, jnp.float32) for item in weights_back))
    back_received = jnp.zeros_like(out_cotangent[0])
    in_grads = []
    for step_index in range(micro_count + 1):
        cotangent_row = out_cotangent[max(micro_count - 1 - step_index, 0)]
        grad_rows = jnp.where(first_section, back_received, cotangent_row).astype(jnp.float32)
        live_flag = jnp.where(first_section, step_index > 0, step_index < micro_count).astype(
            jnp.float32
        )
        current, order_row = keep_list[micro_count - step_index]
        unused, stored = forward(weights_back, current, order_row)
        d_input, grad_terms = backward(weights_back, stored, grad_rows)
        in_grads.append(d_input)
        weighted = tuple((live_flag * item for item in grad_terms))
        totals = tuple((older + newer for older, newer in zip(totals, weighted)))
        if step_index < micro_count:
            back_received = shifted(d_input.astype(jnp.bfloat16), "section", -1)
    totals = (
        lax.psum_scatter(
            totals[0].astype(jnp.bfloat16), "ctx", scatter_dimension=0, tiled=True
        ).astype(jnp.float32),
        lax.psum_scatter(
            totals[1].astype(jnp.bfloat16), "ctx", scatter_dimension=0, tiled=True
        ).astype(jnp.float32),
        lax.psum_scatter(
            totals[2].astype(jnp.bfloat16), "ctx", scatter_dimension=0, tiled=True
        ).astype(jnp.float32),
        lax.psum_scatter(
            totals[3].astype(jnp.bfloat16), "ctx", scatter_dimension=0, tiled=True
        ).astype(jnp.float32),
        lax.psum_scatter(
            totals[4].astype(jnp.bfloat16), "ctx", scatter_dimension=1, tiled=True
        ).astype(jnp.float32),
        lax.psum_scatter(
            totals[5].astype(jnp.bfloat16), "ctx", scatter_dimension=0, tiled=True
        ).astype(jnp.float32),
        lax.psum_scatter(
            totals[6].astype(jnp.bfloat16), "ctx", scatter_dimension=0, tiled=True
        ).astype(jnp.float32),
        lax.psum_scatter(
            totals[7].astype(jnp.bfloat16), "ctx", scatter_dimension=0, tiled=True
        ).astype(jnp.float32),
        lax.psum_scatter(
            totals[8].astype(jnp.bfloat16), "ctx", scatter_dimension=1, tiled=True
        ).astype(jnp.float32),
    )
    gain_one, gain_two = lax.psum((totals[0], totals[5]), "head")
    upper_rows = jnp.stack(
        [in_grads[micro_count - slot_index] for slot_index in range(micro_count)]
    )
    lower_rows = jnp.stack(
        [in_grads[micro_count - 1 - slot_index] for slot_index in range(micro_count)]
    )
    lower_rows = lax.optimization_barrier(lower_rows.astype(jnp.bfloat16)).astype(jnp.float32)
    in_grad = jnp.where(first_section, upper_rows, lower_rows)[None]
    return (
        layer_out,
        in_grad,
        gain_one[None],
        totals[1][None],
        totals[2][None],
        totals[3][None],
        totals[4][None],
        gain_two[None],
        totals[6][None],
        totals[7][None],
        totals[8][None],
    )


def solution(mesh):
    placed = (
        P(None, ("ctx", "head"), None),
        P(None, ("ctx", "head"), None),
        P(),
        P("section", "ctx"),
        P("section", "ctx", "head"),
        P("section", "ctx", "head"),
        P("section", "ctx", "head"),
        P("section", "head", "ctx"),
        P("section", "ctx"),
        P("section", "ctx", "head"),
        P("section", "ctx", "head"),
        P("section", "head", "ctx"),
    )
    return jax.shard_map(
        local,
        mesh=mesh,
        in_specs=placed,
        out_specs=(
            P("section", None, ("ctx", "head"), None),
            P("section", None, ("ctx", "head"), None),
            P("section", "ctx"),
            P("section", "ctx", "head"),
            P("section", "ctx", "head"),
            P("section", "ctx", "head"),
            P("section", "head", "ctx"),
            P("section", "ctx"),
            P("section", "ctx", "head"),
            P("section", "ctx", "head"),
            P("section", "head", "ctx"),
        ),
        check_vma=False,
    )
```

profile of v0, /device:TPU:0, one launch (start us, length us, event | category | flops | bytes accessed | tf_op | source)
XLA Modules:
  0.0 1691.3 jit_solution(16196692559533378661)
XLA Ops:
  20.5 14.9 all_gather.157
  111.5 14.8 all_gather.165
  126.4 26.7 %all-gather.20.cloned.1.call-done = bf16[1,1536,1024]{2,1,0:T(8,128)(2,1)} async-done(((bf16[1,384,1024]{2,1,0:T(8,128)(2,1)}), bf16[1,1536,1024]{2,1,0:T(8,128)(2,1)}) %all-gather.20.cloned.1.call-update) | async-done | bytes 3145744 | tf_op jit(solution)/shard_map/all_gather | solution.py:349
  155.6 43.4 %all-gather.22.cloned.1.call-done = bf16[1,1536,1024]{2,1,0:T(8,128)(2,1)} async-done(((bf16[1,384,1024]{2,1,0:T(8,128)(2,1)}), bf16[1,1536,1024]{2,1,0:T(8,128)(2,1)}) %all-gather.22.cloned.1.call-update) | async-done | bytes 3145744 | tf_op jit(solution)/shard_map/all_gather | solution.py:350
  202.3 42.3 %all-gather.24.cloned.1.call-done = bf16[1,1024,1536]{2,1,0:T(8,128)(2,1)} async-done(((bf16[1,1024,384]{2,1,0:T(8,128)(2,1)}), bf16[1,1024,1536]{2,1,0:T(8,128)(2,1)}) %all-gather.24.cloned.1.call-update) | async-done | bytes 3145744 | tf_op jit(solution)/shard_map/all_gather | solution.py:351
  248.1 20.7 %reduce-scatter.68.cloned.1.call-done = bf16[32,1536]{1,0:T(8,128)(2,1)} async-done(((bf16[128,1536]{1,0:T(8,128)(2,1)}), bf16[32,1536]{1,0:T(8,128)(2,1)}) %reduce-scatter.68.cloned.1.call-update) | async-done | bytes 98320 | tf_op jit(solution)/shard_map/reduce_scatter | solution.py:76
  272.9 15.4 all_gather.169
  311.8 18.1 %reduce-scatter.70.cloned.1.call-done = bf16[32,1536]{1,0:T(8,128)(2,1)} async-done(((bf16[128,1536]{1,0:T(8,128)(2,1)}), bf16[32,1536]{1,0:T(8,128)(2,1)}) %reduce-scatter.70.cloned.1.call-update) | async-done | bytes 98320 | tf_op jit(solution)/shard_map/reduce_scatter | solution.py:76
  332.2 14.8 all_gather.172
  352.6 17.2 %reduce-scatter.72.cloned.1.call-done = bf16[32,1536]{1,0:T(8,128)(2,1)} async-done(((bf16[128,1536]{1,0:T(8,128)(2,1)}), bf16[32,1536]{1,0:T(8,128)(2,1)}) %reduce-scatter.72.cloned.1.call-update) | async-done | bytes 98320 | tf_op jit(solution)/shard_map/reduce_scatter | solution.py:76
  374.9 15.5 all_gather.173
  415.1 17.9 %reduce-scatter.74.cloned.1.call-done = bf16[32,1536]{1,0:T(8,128)(2,1)} async-done(((bf16[128,1536]{1,0:T(8,128)(2,1)}), bf16[32,1536]{1,0:T(8,128)(2,1)}) %reduce-scatter.74.cloned.1.call-update) | async-done | bytes 98320 | tf_op jit(solution)/shard_map/reduce_scatter | solution.py:76
  435.3 14.8 all_gather.176
  455.7 17.6 %reduce-scatter.76.cloned.1.call-done = bf16[32,1536]{1,0:T(8,128)(2,1)} async-done(((bf16[128,1536]{1,0:T(8,128)(2,1)}), bf16[32,1536]{1,0:T(8,128)(2,1)}) %reduce-scatter.76.cloned.1.call-update) | async-done | bytes 98320 | tf_op jit(solution)/shard_map/reduce_scatter | solution.py:76
  478.4 15.4 all_gather.177
  518.6 17.9 %reduce-scatter.78.cloned.1.call-done = bf16[32,1536]{1,0:T(8,128)(2,1)} async-done(((bf16[128,1536]{1,0:T(8,128)(2,1)}), bf16[32,1536]{1,0:T(8,128)(2,1)}) %reduce-scatter.78.cloned.1.call-update) | async-done | bytes 98320 | tf_op jit(solution)/shard_map/reduce_scatter | solution.py:76
  538.8 14.7 all_gather.180
  559.1 17.3 %reduce-scatter.80.cloned.1.call-done = bf16[32,1536]{1,0:T(8,128)(2,1)} async-done(((bf16[128,1536]{1,0:T(8,128)(2,1)}), bf16[32,1536]{1,0:T(8,128)(2,1)}) %reduce-scatter.80.cloned.1.call-update) | async-done | bytes 98320 | tf_op jit(solution)/shard_map/reduce_scatter | solution.py:76
  581.5 15.4 all_gather.181
  622.5 16.5 all-gather.9
  645.7 14.9 all_gather.184
  669.7 16.6 reduce-scatter.86.cloned.1.call-done
  689.7 14.8 all_gather.186
  746.2 21.2 %reduce-scatter.114.cloned.1.call-done = bf16[128,192]{1,0:T(8,128)(2,1)} async-done(((bf16[512,192]{1,0:T(8,128)(2,1)}), bf16[128,192]{1,0:T(8,128)(2,1)}) %reduce-scatter.114.cloned.1.call-update) | async-done | bytes 49168 | tf_op jit(solution)/shard_map/reshape | solution.py:294
  773.3 17.5 %reduce-scatter.88.cloned.1.call-done = bf16[32,1536]{1,0:T(8,128)(2,1)} async-done(((bf16[128,1536]{1,0:T(8,128)(2,1)}), bf16[32,1536]{1,0:T(8,128)(2,1)}) %reduce-scatter.88.cloned.1.call-update) | async-done | bytes 98320 | tf_op jit(solution)/shard_map/reduce_scatter | solution.py:70
  793.0 19.7 %reduce-scatter.84.cloned.1.call-done = bf16[32,1536]{1,0:T(8,128)(2,1)} async-done(((bf16[128,1536]{1,0:T(8,128)(2,1)}), bf16[32,1536]{1,0:T(8,128)(2,1)}) %reduce-scatter.84.cloned.1.call-update) | async-done | bytes 98320 | tf_op jit(solution)/shard_map/reduce_scatter | solution.py:76
  818.7 15.3 all_gather.187
  842.1 17.7 %reduce-scatter.90.cloned.1.call-done = bf16[32,1536]{1,0:T(8,128)(2,1)} async-done(((bf16[128,1536]{1,0:T(8,128)(2,1)}), bf16[32,1536]{1,0:T(8,128)(2,1)}) %reduce-scatter.90.cloned.1.call-update) | async-done | bytes 98320 | tf_op jit(solution)/shard_map/reduce_scatter | solution.py:70
  863.1 14.8 all_gather.188
  920.0 21.2 %reduce-scatter.118.cloned.1.call-done = bf16[128,192]{1,0:T(8,128)(2,1)} async-done(((bf16[512,192]{1,0:T(8,128)(2,1)}), bf16[128,192]{1,0:T(8,128)(2,1)}) %reduce-scatter.118.cloned.1.call-update) | async-done | bytes 49168 | tf_op jit(solution)/shard_map/reshape | solution.py:294
  943.6 21.2 %reduce-scatter.92.cloned.1.call-done = bf16[32,1536]{1,0:T(8,128)(2,1)} async-done(((bf16[128,1536]{1,0:T(8,128)(2,1)}), bf16[32,1536]{1,0:T(8,128)(2,1)}) %reduce-scatter.92.cloned.1.call-update) | async-done | bytes 98320 | tf_op jit(solution)/shard_map/reduce_scatter | solution.py:70
  972.5 15.3 all_gather.189
  995.9 17.7 %reduce-scatter.94.cloned.1.call-done = bf16[32,1536]{1,0:T(8,128)(2,1)} async-done(((bf16[128,1536]{1,0:T(8,128)(2,1)}), bf16[32,1536]{1,0:T(8,128)(2,1)}) %reduce-scatter.94.cloned.1.call-update) | async-done | bytes 98320 | tf_op jit(solution)/shard_map/reduce_scatter | solution.py:70
  1017.0 14.7 all_gather.190
  1073.8 21.0 %reduce-scatter.122.cloned.1.call-done = bf16[128,192]{1,0:T(8,128)(2,1)} async-done(((bf16[512,192]{1,0:T(8,128)(2,1)}), bf16[128,192]{1,0:T(8,128)(2,1)}) %reduce-scatter.122.cloned.1.call-update) | async-done | bytes 49168 | tf_op jit(solution)/shard_map/reshape | solution.py:294
  1097.3 21.0 %reduce-scatter.96.cloned.1.call-done = bf16[32,1536]{1,0:T(8,128)(2,1)} async-done(((bf16[128,1536]{1,0:T(8,128)(2,1)}), bf16[32,1536]{1,0:T(8,128)(2,1)}) %reduce-scatter.96.cloned.1.call-update) | async-done | bytes 98320 | tf_op jit(solution)/shard_map/reduce_scatter | solution.py:70
  1126.0 15.3 all_gather.191
  1149.4 17.7 %reduce-scatter.98.cloned.1.call-done = bf16[32,1536]{1,0:T(8,128)(2,1)} async-done(((bf16[128,1536]{1,0:T(8,128)(2,1)}), bf16[32,1536]{1,0:T(8,128)(2,1)}) %reduce-scatter.98.cloned.1.call-update) | async-done | bytes 98320 | tf_op jit(solution)/shard_map/reduce_scatter | solution.py:70
  1227.4 21.1 %reduce-scatter.126.cloned.1.call-done = bf16[128,192]{1,0:T(8,128)(2,1)} async-done(((bf16[512,192]{1,0:T(8,128)(2,1)}), bf16[128,192]{1,0:T(8,128)(2,1)}) %reduce-scatter.126.cloned.1.call-update) | async-done | bytes 49168 | tf_op jit(solution)/shard_map/reshape | solution.py:294
  1250.8 21.1 %reduce-scatter.100.cloned.1.call-done = bf16[32,1536]{1,0:T(8,128)(2,1)} async-done(((bf16[128,1536]{1,0:T(8,128)(2,1)}), bf16[32,1536]{1,0:T(8,128)(2,1)}) %reduce-scatter.100.cloned.1.call-update) | async-done | bytes 98320 | tf_op jit(solution)/shard_map/reduce_scatter | solution.py:70
  1279.7 15.4 all_gather.193
  1323.5 14.7 all_gather.194
  1354.7 15.3 reduce-scatter.128.cloned.1.call-done
  1373.8 23.0 %reduce-scatter.130.cloned.1.call-done = bf16[128,192]{1,0:T(8,128)(2,1)} async-done(((bf16[512,192]{1,0:T(8,128)(2,1)}), bf16[128,192]{1,0:T(8,128)(2,1)}) %reduce-scatter.130.cloned.1.call-update) | async-done | bytes 49168 | tf_op jit(solution)/shard_map/reshape | solution.py:294
  1511.1 29.9 %reduce-scatter.106.cloned.1.call-done = bf16[384,384]{1,0:T(8,128)(2,1)} async-done(((bf16[1536,384]{1,0:T(8,128)(2,1)}), bf16[384,384]{1,0:T(8,128)(2,1)}) %reduce-scatter.106.cloned.1.call-update) | async-done | bytes 294928 | tf_op jit(solution)/shard_map/reduce_scatter | solution.py:393
  1542.8 45.1 %reduce-scatter.138.cloned.1.call-done = bf16[384,1024]{1,0:T(8,128)(2,1)} async-done(((bf16[1536,1024]{1,0:T(8,128)(2,1)}), bf16[384,1024]{1,0:T(8,128)(2,1)}) %reduce-scatter.138.cloned.1.call-update) | async-done | bytes 786448
  1590.7 44.2 %reduce-scatter.108.cloned.1.call-done = bf16[384,1024]{1,0:T(8,128)(2,1)} async-done(((bf16[1536,1024]{1,0:T(8,128)(2,1)}), bf16[384,1024]{1,0:T(8,128)(2,1)}) %reduce-scatter.108.cloned.1.call-update) | async-done | bytes 786448 | tf_op jit(solution)/shard_map/reduce_scatter | solution.py:408
  1637.4 44.5 %reduce-scatter.110.cloned.1.call-done = bf16[384,1024]{1,0:T(8,128)(2,1)} async-done(((bf16[1536,1024]{1,0:T(8,128)(2,1)}), bf16[384,1024]{1,0:T(8,128)(2,1)}) %reduce-scatter.110.cloned.1.call-update) | async-done | bytes 786448 | tf_op jit(solution)/shard_map/reduce_scatter | solution.py:411
  (970 shorter events, 689.2 us)
Async XLA Ops:
  7.2 76.2 %all-gather.16.cloned.1.call-start = ((), (), s32[]{:S(2)}) async-start(), calls=%async_computation.60 | async-start | bytes 1474560 | tf_op jit(solution)/shard_map/all_gather | solution.py:344
  7.9 78.5 %all-gather.18.cloned.1.call-start = ((), (), s32[]{:S(2)}) async-start(), calls=%async_computation.61 | async-start | bytes 1474560 | tf_op jit(solution)/shard_map/all_gather | solution.py:347
  8.7 100.3 %reduce-scatter.66.cloned.1.call-start = ((), (), s32[]{:S(2)}) async-start(), calls=%async_computation.37 | async-start | bytes 491520 | tf_op jit(solution)/shard_map/reduce_scatter | solution.py:76
  88.9 64.2 %all-gather.20.cloned.1.call-start = ((), (), s32[]{:S(2)}) async-start(), calls=%async_computation.62 | async-start | bytes 3932160 | tf_op jit(solution)/shard_map/all_gather | solution.py:349
  89.5 109.5 %all-gather.22.cloned.1.call-start = ((), (), s32[]{:S(2)}) async-start(), calls=%async_computation.63 | async-start | bytes 3932160 | tf_op jit(solution)/shard_map/all_gather | solution.py:350
  90.1 154.5 %all-gather.24.cloned.1.call-start = ((), (), s32[]{:S(2)}) async-start(), calls=%async_computation.64 | async-start | bytes 3932160 | tf_op jit(solution)/shard_map/all_gather | solution.py:351
  90.7 178.2 %reduce-scatter.68.cloned.1.call-start = ((), (), s32[]{:S(2)}) async-start(), calls=%async_computation.38 | async-start | bytes 491520 | tf_op jit(solution)/shard_map/reduce_scatter | solution.py:76
  248.1 81.8 %reduce-scatter.70.cloned.1.call-start = ((), (), s32[]{:S(2)}) async-start(), calls=%async_computation.39 | async-start | bytes 491520 | tf_op jit(solution)/shard_map/reduce_scatter | solution.py:76
  311.7 58.0 %reduce-scatter.72.cloned.1.call-start = ((), (), s32[]{:S(2)}) async-start(), calls=%async_computation.40 | async-start | bytes 491520 | tf_op jit(solution)/shard_map/reduce_scatter | solution.py:76
  351.2 81.8 %reduce-scatter.74.cloned.1.call-start = ((), (), s32[]{:S(2)}) async-start(), calls=%async_computation.41 | async-start | bytes 491520 | tf_op jit(solution)/shard_map/reduce_scatter | solution.py:76
  370.9 2.2 collective-permute-start.1
  415.1 58.2 %reduce-scatter.76.cloned.1.call-start = ((), (), s32[]{:S(2)}) async-start(), calls=%async_computation.42 | async-start | bytes 491520 | tf_op jit(solution)/shard_map/reduce_scatter | solution.py:76
  454.4 82.1 %reduce-scatter.78.cloned.1.call-start = ((), (), s32[]{:S(2)}) async-start(), calls=%async_computation.43 | async-start | bytes 491520 | tf_op jit(solution)/shard_map/reduce_scatter | solution.py:76
  474.4 2.2 collective-permute-start.2
  518.5 57.8 %reduce-scatter.80.cloned.1.call-start = ((), (), s32[]{:S(2)}) async-start(), calls=%async_computation.44 | async-start | bytes 491520 | tf_op jit(solution)/shard_map/reduce_scatter | solution.py:76
  557.8 85.8 %reduce-scatter.82.cloned.1.call-start = ((), (), s32[]{:S(2)}) async-start(), calls=%async_computation.45 | async-start | bytes 491520 | tf_op jit(solution)/shard_map/reduce_scatter | solution.py:76
  621.5 64.8 %reduce-scatter.86.cloned.1.call-start = ((), (), s32[]{:S(2)}) async-start(), calls=%async_computation.47 | async-start | bytes 491520 | tf_op jit(solution)/shard_map/reduce_scatter | solution.py:70
  668.4 71.6 %reduce-scatter.112.cloned.1.call-start = ((), (), s32[]{:S(2)}) async-start(), calls=%async_computation.65 | async-start | bytes 327680
  717.9 49.5 %reduce-scatter.114.cloned.1.call-start = ((), (), s32[]{:S(2)}) async-start(), calls=%async_computation.66 | async-start | bytes 327680 | tf_op jit(solution)/shard_map/reshape | solution.py:294
  723.5 67.3 %reduce-scatter.88.cloned.1.call-start = ((), (), s32[]{:S(2)}) async-start(), calls=%async_computation.48 | async-start | bytes 491520 | tf_op jit(solution)/shard_map/reduce_scatter | solution.py:70
  769.8 42.8 %reduce-scatter.84.cloned.1.call-start = ((), (), s32[]{:S(2)}) async-start(), calls=%async_computation.46 | async-start | bytes 491520 | tf_op jit(solution)/shard_map/reduce_scatter | solution.py:76
  773.2 86.6 %reduce-scatter.90.cloned.1.call-start = ((), (), s32[]{:S(2)}) async-start(), calls=%async_computation.49 | async-start | bytes 491520 | tf_op jit(solution)/shard_map/reduce_scatter | solution.py:70
  814.6 3.2 collective-permute-start.4
  840.8 73.0 %reduce-scatter.116.cloned.1.call-start = ((), (), s32[]{:S(2)}) async-start(), calls=%async_computation.67 | async-start | bytes 327680
  891.4 49.8 %reduce-scatter.118.cloned.1.call-start = ((), (), s32[]{:S(2)}) async-start(), calls=%async_computation.68 | async-start | bytes 327680 | tf_op jit(solution)/shard_map/reshape | solution.py:294
  897.3 67.5 %reduce-scatter.92.cloned.1.call-start = ((), (), s32[]{:S(2)}) async-start(), calls=%async_computation.50 | async-start | bytes 491520 | tf_op jit(solution)/shard_map/reduce_scatter | solution.py:70
  943.6 70.0 %reduce-scatter.94.cloned.1.call-start = ((), (), s32[]{:S(2)}) async-start(), calls=%async_computation.51 | async-start | bytes 491520 | tf_op jit(solution)/shard_map/reduce_scatter | solution.py:70
  968.4 3.2 collective-permute-start.5
  994.6 73.0 %reduce-scatter.120.cloned.1.call-start = ((), (), s32[]{:S(2)}) async-start(), calls=%async_computation.69 | async-start | bytes 327680
  1045.1 49.7 %reduce-scatter.122.cloned.1.call-start = ((), (), s32[]{:S(2)}) async-start(), calls=%async_computation.70 | async-start | bytes 327680 | tf_op jit(solution)/shard_map/reshape | solution.py:294
  1050.7 67.6 %reduce-scatter.96.cloned.1.call-start = ((), (), s32[]{:S(2)}) async-start(), calls=%async_computation.52 | async-start | bytes 491520 | tf_op jit(solution)/shard_map/reduce_scatter | solution.py:70
  1097.2 69.8 %reduce-scatter.98.cloned.1.call-start = ((), (), s32[]{:S(2)}) async-start(), calls=%async_computation.53 | async-start | bytes 491520 | tf_op jit(solution)/shard_map/reduce_scatter | solution.py:70
  1121.9 3.2 collective-permute-start.6
  1148.1 73.0 %reduce-scatter.124.cloned.1.call-start = ((), (), s32[]{:S(2)}) async-start(), calls=%async_computation.71 | async-start | bytes 327680
  1198.6 49.8 %reduce-scatter.126.cloned.1.call-start = ((), (), s32[]{:S(2)}) async-start(), calls=%async_computation.72 | async-start | bytes 327680 | tf_op jit(solution)/shard_map/reshape | solution.py:294
  1204.3 67.6 %reduce-scatter.100.cloned.1.call-start = ((), (), s32[]{:S(2)}) async-start(), calls=%async_computation.54 | async-start | bytes 491520 | tf_op jit(solution)/shard_map/reduce_scatter | solution.py:70
  1250.8 70.0 %reduce-scatter.102.cloned.1.call-start = ((), (), s32[]{:S(2)}) async-start(), calls=%async_computation.55 | async-start | bytes 491520 | tf_op jit(solution)/shard_map/reduce_scatter | solution.py:70
  1275.5 3.2 collective-permute-start.7
  1301.8 68.1 %reduce-scatter.128.cloned.1.call-start = ((), (), s32[]{:S(2)}) async-start(), calls=%async_computation.73 | async-start | bytes 327680
  1347.5 49.3 %reduce-scatter.130.cloned.1.call-start = ((), (), s32[]{:S(2)}) async-start(), calls=%async_computation.74 | async-start | bytes 327680 | tf_op jit(solution)/shard_map/reshape | solution.py:294
  1352.3 124.0 %reduce-scatter.104.cloned.1.call-start = ((), (), s32[]{:S(2)}) async-start(), calls=%async_computation.56 | async-start | bytes 491520 | tf_op jit(solution)/shard_map/reduce_scatter | solution.py:70
  1398.7 102.4 %reduce-scatter.132.cloned.1.call-start = ((), (), s32[]{:S(2)}) async-start(), calls=%async_computation.75 | async-start | bytes 983040
  1404.1 98.1 %reduce-scatter.134.cloned.1.call-start = ((), (), s32[]{:S(2)}) async-start(), calls=%async_computation.76 | async-start | bytes 983040
  1409.2 99.9 %reduce-scatter.136.cloned.1.call-start = ((), (), s32[]{:S(2)}) async-start(), calls=%async_computation.77 | async-start | bytes 1474560
  1415.6 125.3 %reduce-scatter.106.cloned.1.call-start = ((), (), s32[]{:S(2)}) async-start(), calls=%async_computation.57 | async-start | bytes 1474560 | tf_op jit(solution)/shard_map/reduce_scatter | solution.py:393
  1420.5 167.5 %reduce-scatter.138.cloned.1.call-start = ((), (), s32[]{:S(2)}) async-start(), calls=%async_computation.78 | async-start | bytes 3932160
  1438.7 196.2 %reduce-scatter.108.cloned.1.call-start = ((), (), s32[]{:S(2)}) async-start(), calls=%async_computation.58 | async-start | bytes 3932160 | tf_op jit(solution)/shard_map/reduce_scatter | solution.py:408
  1456.1 225.7 %reduce-scatter.110.cloned.1.call-start = ((), (), s32[]{:S(2)}) async-start(), calls=%async_computation.59 | async-start | bytes 3932160 | tf_op jit(solution)/shard_map/reduce_scatter | solution.py:411
  (255 other events, 2870.6 us)
Sparse Core Ops, SparseCore 0:
  9.8 31.7 all-gather.15
  43.5 30.6 all-gather.17
  89.0 19.8 reduce-scatter.65
  110.8 42.2 all-gather.19
  154.9 43.9 all-gather.21
  200.7 43.8 all-gather.23
  248.2 20.5 reduce-scatter.67
  311.8 18.0 reduce-scatter.69
  351.4 18.3 reduce-scatter.71
  415.2 17.7 reduce-scatter.73
  454.5 18.7 reduce-scatter.75
  518.6 17.8 reduce-scatter.77
  557.9 18.4 reduce-scatter.79
  621.6 18.7 reduce-scatter.81
  668.5 17.7 reduce-scatter.85
  718.1 21.8 reduce-scatter.111
  743.4 24.0 reduce-scatter.113
  770.2 20.5 reduce-scatter.87
  793.7 18.8 reduce-scatter.83
  840.9 18.8 reduce-scatter.89
  891.5 22.2 reduce-scatter.115
  917.1 24.0 reduce-scatter.117
  944.2 20.5 reduce-scatter.91
  994.7 18.8 reduce-scatter.93
  1045.3 22.2 reduce-scatter.119
  1070.8 24.0 reduce-scatter.121
  1097.7 20.5 reduce-scatter.95
  1148.2 18.8 reduce-scatter.97
  1198.7 22.3 reduce-scatter.123
  1224.3 24.0 reduce-scatter.125
  1251.4 20.5 reduce-scatter.99
  1301.9 18.8 reduce-scatter.101
  1347.7 22.2 reduce-scatter.127
  1372.7 24.0 reduce-scatter.129
  1399.8 20.5 reduce-scatter.103
  1423.7 24.3 reduce-scatter.131
  1450.9 26.0 reduce-scatter.133
  1480.5 28.5 reduce-scatter.135
  1512.4 28.5 reduce-scatter.105
  1544.0 43.9 reduce-scatter.137
  1590.9 43.9 reduce-scatter.107
  1637.9 43.9 reduce-scatter.109
where the time goes:
time: 1710 us; the launch traced here: 1690 us
  waiting for transfers between devices  791 us (46%)
  blocking collectives  454 us (27%)
  matrix products  231 us (14%)
  other arithmetic  108 us (6%)
  local copies, waits for them, and re-layouts  74.8 us (4%)
  between operations  19 us (1%)
    reduce_scatter x10, waiting for transfers between devices, settle_rows(): lax.psum_scatter(partial_terms.astype(jnp.bfloat16), 'head', scatter_dime...  164 us
    reduce_scatter x10, waiting for transfers between devices, branch_total(): lax.psum_scatter(jnp.dot(left_rows, right_mat, preferred_element_type=jnp...  157 us
    all_gather x10, blocking collectives, spread_grads(): return lax.all_gather(row_block, 'head', axis=0, tiled=True)  152 us
    all_gather x10, blocking collectives, spread(): return lax.all_gather(row_block, 'head', axis=0, tiled=True)  151 us
    unnamed x51, waiting for transfers between devices  124 us
    reshape x5, waiting for transfers between devices, backward(): d_v_lin = d_value.astype(jnp.bfloat16).reshape(span_rows, -1)  108 us
    unnamed x530, local copies, waits for them, and re-layouts  66.3 us
    all_gather x5, blocking collectives, forward(): key_piece = lax.all_gather(key_rows, 'ctx', axis=0, tiled=True)  45.8 us
  transfers between devices with their start and end apart: 50, of which 44 were waited for; matrix products, arithmetic and copies ran while one was open for 12% of the time, Pallas kernels for 0%

commit v1 on v0

v1 whole, which is shorter than its diff:
```python
import jax
import jax.numpy as jnp
import numpy as np
from jax import lax
from jax.experimental import pallas as pl
from jax.experimental.pallas import tpu as pltpu
from jax.sharding import PartitionSpec as P

HEAD_DIM = 96
HALF = HEAD_DIM // 2
INV_ROOT = HEAD_DIM ** (-0.5)
EPSILON = 1e-05
ROPE_BASE = 100000.0
MASKED = -1e30
LANES = 128
UNIT_BLOCK = 256
F32 = jnp.float32
BF16 = jnp.bfloat16
GROUPS = 1
VMEM_LIMIT = 48 * 1024 * 1024


def swap(value, axis, step):
    count = lax.axis_size(axis)
    return lax.ppermute(value, axis, [(i, i ^ step) for i in range(count)])


def swap_from(value, source):
    return lax.ppermute(value, "section", [(source, 1 - source)])


def after(value, earlier):
    return lax.optimization_barrier((value, earlier))[0]


def dot(left, right):
    return jnp.dot(left, right, preferred_element_type=F32)


def dot_nt(left, right):
    return lax.dot_general(left, right, (((1,), (1,)), ((), ())), preferred_element_type=F32)


def dot_tn(left, right):
    return lax.dot_general(left, right, (((0,), (0,)), ((), ())), preferred_element_type=F32)


def split_terms(value):
    high = value.astype(BF16)
    return high, (value - high.astype(F32)).astype(BF16)


def shape(dims, dtype=BF16):
    return jax.ShapeDtypeStruct(dims, dtype)


def kept(dims, dtype=BF16):
    return pltpu.HBM(dims, dtype)


class View:
    def __init__(self, array, width=None, block=0):
        self.array = array
        self.width = array.shape[-1] if width is None else width
        self.block = block


def call(kernel, name, args, outs, scratch=(), flops=0):
    specs, arrays = [], []
    size = 0
    for arg in args:
        if isinstance(arg, View):
            block = arg.block
            specs.append(
                pl.BlockSpec((arg.array.shape[0], arg.width), lambda i, block=block: (0, block))
            )
            arrays.append(arg.array)
            size += arg.array.shape[0] * arg.width * arg.array.dtype.itemsize
        else:
            zeros = (0,) * arg.ndim
            specs.append(pl.BlockSpec(arg.shape, lambda i, zeros=zeros: zeros))
            arrays.append(arg)
            size += arg.size * arg.dtype.itemsize
    out_specs = [
        pl.BlockSpec(out.shape, lambda i, zeros=(0,) * len(out.shape): zeros) for out in outs
    ]
    size += sum(int(np.prod(out.shape)) * jnp.dtype(out.dtype).itemsize for out in outs)
    return pl.pallas_call(
        kernel,
        grid=(1,),
        in_specs=specs,
        out_specs=out_specs,
        out_shape=outs,
        scratch_shapes=list(scratch),
        compiler_params=pltpu.CompilerParams(vmem_limit_bytes=VMEM_LIMIT),
        cost_estimate=pl.CostEstimate(flops=flops, bytes_accessed=size, transcendentals=0),
        name=name,
    )(*arrays)


def place(pieces, ctx):
    count = len(pieces)
    size, width = pieces[0].shape

    def kernel(*refs):
        whole = refs[count]
        mine = lax.axis_index("ctx")
        for k in range(count):
            at = pl.multiple_of((mine ^ k) * size, size)
            whole[pl.ds(at, size), :] = refs[k][...]

    return call(kernel, "place", pieces, [shape((count * size, width))])[0]


def write_pieces(outs, value, micros, start=0, width=None):
    heads = len(outs)
    piece = outs[0].shape[1]
    for m in range(micros):
        for k in range(heads):
            at = (m * heads + k) * piece
            outs[k][m] = value[at : at + piece].astype(BF16)


def read_pieces(whole, pieces, micros):
    heads = len(pieces)
    piece = pieces[0].shape[1]
    for m in range(micros):
        for k in range(heads):
            at = (m * heads + k) * piece
            whole[at : at + piece, :] = pieces[k][m]


def project(pieces, queries, kvs, gain_views, cosine, sine, turn):
    heads = len(pieces)
    micros, piece, d_model = pieces[0].shape
    rows = micros * heads * piece
    half = d_model // 2
    width = queries[0].width

    def kernel(*refs):
        xs = refs[:heads]
        q_own, q_other, kv_own, kv_other, g_own, g_other, cos, sin, turns, eye = refs[heads : heads + 10]
        na, q_out, kv_out, gains = refs[heads + 10 :]
        gains[:, :half] = dot_nt(eye[...], g_own[...])
        gains[:, half:] = dot_nt(eye[...], g_other[...])
        gain = gains[0:1, :]
        for m in range(micros):
            for k in range(heads):
                x = xs[k][m].astype(F32)
                scale = lax.rsqrt(jnp.mean(x * x, axis=-1, keepdims=True) + EPSILON)
                at = (m * heads + k) * piece
                na[at : at + piece, :] = (x * scale * gain).astype(BF16)
        low, high = na[:, :half], na[:, half:]
        for part, (own, other, out) in enumerate(
            ((q_own, q_other, q_out), (kv_own, kv_other, kv_out))
        ):
            lin = dot(low, own[...]) + dot(high, other[...])
            a, b = split_terms(lin)
            turned = dot(a, turns[part]) + dot(b, turns[part])
            at = part * width
            out[...] = (
                lin * cos[:, at : at + width] + turned * sin[:, at : at + width]
            ).astype(BF16)

    eye = jnp.asarray(np.eye(8, LANES), BF16)
    return call(
        kernel,
        "project",
        [*pieces, *queries, *kvs, *gain_views, cosine, sine, turn, eye],
        [kept((rows, d_model)), kept((rows, width)), shape((rows, width)), shape((8, d_model), F32)],
        flops=4 * rows * d_model * width,
    )


def attend(query, pieces, place_q, place_k, pad, outs_w, heads, piece, group):
    ctxs = len(pieces)
    micros, span, width = pieces[0].shape
    keys = ctxs * span
    rows = micros * span
    half = outs_w[0].array.shape[0]
    kv_heads = pad.shape[1] // LANES // 2

    def kernel(*refs):
        q_ref = refs[0]
        kvs = refs[1 : 1 + ctxs]
        pq, pk, pads, w_own, w_other = refs[1 + ctxs : 6 + ctxs]
        prob, mix = refs[6 + ctxs : 8 + ctxs]
        outs = refs[8 + ctxs : 8 + ctxs + heads]
        kv_rows, mixed = refs[8 + ctxs + heads :]
        for m in range(micros):
            for j in range(ctxs):
                kv_rows[j * span : (j + 1) * span, :] = kvs[j][m]
            kv = dot(kv_rows[...], pads[...]).astype(BF16)
            q = dot(q_ref[m * span : (m + 1) * span, :], pads[...]).astype(BF16)
            allowed = pk[m] <= pq[m]
            allowed = jnp.concatenate([allowed] * group, axis=0)
            for a in range(kv_heads):
                q2 = jnp.concatenate(
                    [q[:, (a * group + g) * LANES : (a * group + g + 1) * LANES] for g in range(group)],
                    axis=0,
                )
                key = kv[:, a * LANES : (a + 1) * LANES]
                value = kv[:, (kv_heads + a) * LANES : (kv_heads + a + 1) * LANES]
                scores = jnp.where(allowed, dot_nt(q2, key) * INV_ROOT, MASKED)
                top = jnp.max(scores, axis=-1, keepdims=True)
                weight = jnp.exp(scores - top)
                share = (weight / jnp.sum(weight, axis=-1, keepdims=True)).astype(BF16)
                prob[m * kv_heads + a] = share
                got = dot(share, value).astype(BF16)
                for g in range(group):
                    at = (a * group + g) * LANES
                    mixed[:, at : at + LANES] = got[g * span : (g + 1) * span]
            mix[m * span : (m + 1) * span, :] = dot_nt(mixed[...], pads[...]).astype(BF16)
        for t, w in enumerate((w_own, w_other)):
            branch = dot_nt(mix[...], w[...]).astype(BF16)
            for m in range(micros):
                for k in range(heads):
                    at = (m * heads + k) * piece
                    outs[k][m, :, t * half : (t + 1) * half] = branch[at : at + piece]

    return call(
        kernel,
        "attend",
        [query, *pieces, place_q, place_k, pad, *outs_w],
        [
            kept((micros * kv_heads, group * span, keys)),
            kept((rows, width)),
            *[shape((micros, piece, 2 * half)) for _ in range(heads)],
        ],
        [pltpu.VMEM((keys, width), BF16), pltpu.VMEM((span, pad.shape[1]), BF16)],
        flops=4 * rows * width * (keys + half),
    )


def add_mid(x, terms, gains):
    def kernel(*refs):
        x_ref, gain = refs[0], refs[1]
        parts = refs[2 : 2 + len(terms)]
        mid, nb = refs[2 + len(terms) :]
        total = x_ref[...].astype(F32)
        for part in parts:
            total = total + part[...].astype(F32)
        mid[...] = total
        scale = lax.rsqrt(jnp.mean(total * total, axis=-1, keepdims=True) + EPSILON)
        nb[...] = (total * scale * gain[1:2, :]).astype(BF16)

    return call(
        kernel, "add_mid", [x, gains, *terms], [shape(x.shape, F32), shape(x.shape)]
    )


def add_out(mid, terms):
    def kernel(*refs):
        total = refs[0][...]
        for part in refs[1:-1]:
            total = total + part[...].astype(F32)
        refs[-1][...] = total.astype(BF16)

    return call(kernel, "add_out", [mid, *terms], [shape(mid.shape)])[0]


def blocks_of(pair, units):
    specs, arrays = [], []
    count = units // UNIT_BLOCK
    for part in range(3):
        for array in pair:
            specs.append(
                pl.BlockSpec(
                    (array.shape[0], UNIT_BLOCK), lambda j, part=part: (0, part * count + j)
                )
            )
            arrays.append(array)
    return specs, arrays


def pack_places(half, units, width):
    hidden_at = 2 * half
    mix_at = -(-(hidden_at + units) // width) * width
    return hidden_at, mix_at


def feed(pieces, pair, units, na, mix):
    heads = len(pieces)
    micros, piece, d_model = pieces[0].shape
    rows = micros * heads * piece
    half = d_model // 2
    count = units // UNIT_BLOCK
    width = mix.shape[1]
    hidden_at, mix_at = pack_places(half, units, width)

    def kernel(*refs):
        xs = refs[:heads]
        gate_w = refs[heads : heads + 2]
        up_w = refs[heads + 2 : heads + 4]
        down_w = refs[heads + 4 : heads + 6]
        na_in, mix_in = refs[heads + 6 : heads + 8]
        gate_out, up_out, hidden_out, nb, packed = refs[heads + 8 : heads + 13]
        outs = refs[heads + 13 : 2 * heads + 13]
        total = refs[-1]
        j = pl.program_id(0)

        @pl.when(j == 0)
        def _():
            read_pieces(nb, xs, micros)
            total[...] = jnp.zeros_like(total)
            packed[:, :half] = na_in[...]
            packed[:, half : 2 * half] = nb[:, half:]
            packed[:, mix_at : mix_at + width] = mix_in[...]

        low, high = nb[:, :half], nb[:, half:]
        gate = dot(low, gate_w[0][...]) + dot(high, gate_w[1][...])
        up = dot(low, up_w[0][...]) + dot(high, up_w[1][...])
        gate_out[...] = gate
        up_out[...] = up
        hidden = (gate * jax.nn.sigmoid(gate) * up).astype(BF16)
        hidden_out[...] = hidden
        at = pl.multiple_of(hidden_at + j * UNIT_BLOCK, UNIT_BLOCK)
        packed[:, pl.ds(at, UNIT_BLOCK)] = hidden
        total[:, :half] += dot_nt(hidden, down_w[0][...])
        total[:, half:] += dot_nt(hidden, down_w[1][...])

        @pl.when(j == count - 1)
        def _():
            write_pieces(outs, total, micros)

    specs, arrays = blocks_of(pair, units)
    whole = pl.BlockSpec((rows, d_model), lambda j: (0, 0))
    block = pl.BlockSpec((rows, UNIT_BLOCK), lambda j: (0, j))
    rows_spec = pl.BlockSpec((micros, piece, d_model), lambda j: (0, 0, 0))
    return pl.pallas_call(
        kernel,
        grid=(count,),
        in_specs=[rows_spec] * heads
        + specs
        + [pl.BlockSpec((rows, half), lambda j: (0, 1)), pl.BlockSpec(mix.shape, lambda j: (0, 0))],
        out_specs=[block, block, block, whole]
        + [pl.BlockSpec((rows, mix_at + width), lambda j: (0, 0))]
        + [rows_spec] * heads,
        out_shape=[
            kept((rows, units), F32),
            kept((rows, units), F32),
            kept((rows, units)),
            kept((rows, d_model)),
            kept((rows, mix_at + width)),
            *[shape((micros, piece, d_model)) for _ in range(heads)],
        ],
        scratch_shapes=[pltpu.VMEM((rows, d_model), F32)],
        compiler_params=pltpu.CompilerParams(vmem_limit_bytes=VMEM_LIMIT),
        cost_estimate=pl.CostEstimate(
            flops=6 * rows * d_model * units, bytes_accessed=6 * d_model * units, transcendentals=0
        ),
        name="feed",
    )(*pieces, *arrays, na, mix)


def feed_back(pieces, pair, gate, up):
    heads = len(pieces)
    micros, piece, d_model = pieces[0].shape
    rows, units = gate.shape
    half = d_model // 2
    count = units // UNIT_BLOCK

    def kernel(*refs):
        xs = refs[:heads]
        gate_w = refs[heads : heads + 2]
        up_w = refs[heads + 2 : heads + 4]
        down_w = refs[heads + 4 : heads + 6]
        gate_in, up_in = refs[heads + 6 : heads + 8]
        d_gate_out, d_up_out, gf, packed = refs[heads + 8 : heads + 12]
        outs = refs[heads + 12 : 2 * heads + 12]
        total = refs[-1]
        j = pl.program_id(0)

        @pl.when(j == 0)
        def _():
            read_pieces(gf, xs, micros)
            total[...] = jnp.zeros_like(total)
            packed[:, :half] = gf[:, half:]

        d_hidden = dot(gf[:, :half], down_w[0][...]) + dot(gf[:, half:], down_w[1][...])
        gate_v, up_v = gate_in[...], up_in[...]
        sigma = jax.nn.sigmoid(gate_v)
        d_gate = (d_hidden * up_v * sigma * (1.0 + gate_v * (1.0 - sigma))).astype(BF16)
        d_up = (d_hidden * gate_v * sigma).astype(BF16)
        d_gate_out[...] = d_gate
        d_up_out[...] = d_up
        at = pl.multiple_of(half + j * UNIT_BLOCK, UNIT_BLOCK)
        packed[:, pl.ds(at, UNIT_BLOCK)] = d_gate
        at = pl.multiple_of(half + units + j * UNIT_BLOCK, UNIT_BLOCK)
        packed[:, pl.ds(at, UNIT_BLOCK)] = d_up
        total[:, :half] += dot_nt(d_gate, gate_w[0][...]) + dot_nt(d_up, up_w[0][...])
        total[:, half:] += dot_nt(d_gate, gate_w[1][...]) + dot_nt(d_up, up_w[1][...])

        @pl.when(j == count - 1)
        def _():
            write_pieces(outs, total, micros)

    specs, arrays = blocks_of(pair, units)
    whole = pl.BlockSpec((rows, d_model), lambda j: (0, 0))
    block = pl.BlockSpec((rows, UNIT_BLOCK), lambda j: (0, j))
    rows_spec = pl.BlockSpec((micros, piece, d_model), lambda j: (0, 0, 0))
    return pl.pallas_call(
        kernel,
        grid=(count,),
        in_specs=[rows_spec] * heads + specs + [block, block],
        out_specs=[block, block, whole]
        + [pl.BlockSpec((rows, half + 2 * units), lambda j: (0, 0))]
        + [rows_spec] * heads,
        out_shape=[
            kept((rows, units)),
            kept((rows, units)),
            kept((rows, d_model)),
            kept((rows, half + 2 * units)),
            *[shape((micros, piece, d_model)) for _ in range(heads)],
        ],
        scratch_shapes=[pltpu.VMEM((rows, d_model), F32)],
        compiler_params=pltpu.CompilerParams(vmem_limit_bytes=VMEM_LIMIT),
        cost_estimate=pl.CostEstimate(
            flops=6 * rows * d_model * units, bytes_accessed=6 * d_model * units, transcendentals=0
        ),
        name="feed_back",
    )(*pieces, *arrays, gate, up)


def norm_back(terms, residual, gains, row, carried):
    d_model = residual.shape[-1]

    def kernel(*refs):
        res, gain, carry = refs[:3]
        parts = refs[3 : 3 + len(terms)]
        d_out, d_low, d_gain = refs[3 + len(terms) :]
        d_normed = parts[0][...].astype(F32)
        for part in parts[1:]:
            d_normed = d_normed + part[...].astype(F32)
        rows = res[...].astype(F32)
        scale = lax.rsqrt(jnp.mean(rows * rows, axis=-1, keepdims=True) + EPSILON)
        unit = rows * scale
        d_gain[...] = jnp.sum(jnp.sum(d_normed * unit, axis=0), axis=0, keepdims=True)
        d_unit = d_normed * gain[row : row + 1, :]
        total = carry[...].astype(F32) + scale * (
            d_unit - unit * jnp.mean(d_unit * unit, axis=-1, keepdims=True)
        )
        d_out[...] = total
        d_low[...] = total.astype(BF16)

    return call(
        kernel,
        "norm_back",
        [residual, gains, carried, *terms],
        [shape(residual.shape, F32), shape(residual.shape), shape((1, d_model), F32)],
    )


def attend_back(pieces, outs_w, mix, prob, query, kv_pieces, pad, turn, cosine, sine, group):
    heads = len(pieces)
    micros, piece, d_model = pieces[0].shape
    span = heads * piece
    rows = micros * span
    half = d_model // 2
    ctxs = len(kv_pieces)
    width = query.shape[1]
    keys = ctxs * span
    kv_heads = pad.shape[1] // LANES // 2

    def kernel(*refs):
        xs = refs[:heads]
        w_own, w_other, mix_in, prob_in, q_ref = refs[heads : heads + 5]
        kvs = refs[heads + 5 : heads + 5 + ctxs]
        pads, turns, cos, sin = refs[heads + 5 + ctxs : heads + 9 + ctxs]
        ga, ga_other, dq_out = refs[heads + 9 + ctxs : heads + 12 + ctxs]
        outs = refs[heads + 12 + ctxs : heads + 12 + 2 * ctxs]
        kv_rows, d_kv, d_q = refs[heads + 12 + 2 * ctxs :]
        read_pieces(ga, xs, micros)
        ga_other[...] = ga[:, half:]
        d_mix = (dot(ga[:, :half], w_own[...]) + dot(ga[:, half:], w_other[...])).astype(BF16)
        for m in range(micros):
            for j in range(ctxs):
                kv_rows[j * span : (j + 1) * span, :] = kvs[j][m]
            here = slice(m * span, (m + 1) * span)
            kv = dot(kv_rows[...], pads[...]).astype(BF16)
            q = dot(q_ref[here, :], pads[...]).astype(BF16)
            d = dot(d_mix[here], pads[...])
            product = d * dot(mix_in[here, :], pads[...])
            d = d.astype(BF16)
            for a in range(kv_heads):
                cuts = [slice((a * group + g) * LANES, (a * group + g + 1) * LANES) for g in range(group)]
                q2 = jnp.concatenate([q[:, cut] for cut in cuts], axis=0)
                d2 = jnp.concatenate([d[:, cut] for cut in cuts], axis=0)
                delta = jnp.concatenate(
                    [jnp.sum(product[:, cut], axis=-1, keepdims=True) for cut in cuts], axis=0
                )
                key = kv[:, a * LANES : (a + 1) * LANES]
                value = kv[:, (kv_heads + a) * LANES : (kv_heads + a + 1) * LANES]
                share = prob_in[m * kv_heads + a]
                d_prob = dot_nt(d2, value)
                d_score = (share.astype(F32) * (d_prob - delta)).astype(BF16)
                back = dot(d_score, key)
                for g, cut in enumerate(cuts):
                    d_q[:, cut] = back[g * span : (g + 1) * span]
                d_kv[:, a * LANES : (a + 1) * LANES] = dot_tn(d_score, q2).astype(BF16)
                d_kv[:, (kv_heads + a) * LANES : (kv_heads + a + 1) * LANES] = dot_tn(
                    share, d2
                ).astype(BF16)
            packed = dot_nt(d_kv[...], pads[...]).astype(BF16)
            for j in range(ctxs):
                outs[j][m] = packed[j * span : (j + 1) * span]
            high, low = split_terms(d_q[...])
            line = (dot_nt(high, pads[...]) + dot_nt(low, pads[...])) * INV_ROOT
            high, low = split_terms(line)
            turned = dot_nt(high, turns[0]) + dot_nt(low, turns[0])
            dq_out[here, :] = (line * cos[here, :width] + turned * sin[here, :width]).astype(BF16)

    return call(
        kernel,
        "attend_back",
        [*pieces, *outs_w, mix, prob, query, *kv_pieces, pad, turn, cosine, sine],
        [
            kept((rows, d_model)),
            shape((rows, half)),
            shape((rows, width)),
            *[shape((micros, span, width)) for _ in range(ctxs)],
        ],
        [
            pltpu.VMEM((keys, width), BF16),
            pltpu.VMEM((keys, pad.shape[1]), BF16),
            pltpu.VMEM((span, pad.shape[1]), F32),
        ],
        flops=10 * rows * width * keys,
    )


def project_back(terms, dq, queries, kvs, turn, cosine, sine, row_pieces):
    heads = len(row_pieces)
    micros, span, width = terms[0].shape
    rows = micros * span
    piece = span // heads
    half = queries[0].array.shape[0]
    count = len(terms)

    def kernel(*refs):
        parts = refs[:count]
        dq_in, q_own, q_other, kv_own, kv_other, turns, cos, sin = refs[count : count + 8]
        xs = refs[count + 8 : count + 8 + heads]
        d_line, d_gain = refs[count + 8 + heads : count + 10 + heads]
        outs = refs[count + 10 + heads : count + 10 + 2 * heads]
        unit = refs[-1]
        for m in range(micros):
            for k in range(heads):
                x = xs[k][m].astype(F32)
                scale = lax.rsqrt(jnp.mean(x * x, axis=-1, keepdims=True) + EPSILON)
                at = (m * heads + k) * piece
                unit[at : at + piece, :] = x * scale
        d_line[:, :width] = dq_in[...]
        lanes = lax.broadcasted_iota(jnp.int32, (span, width), 1)
        scaled = jnp.where(lanes < width // 2, INV_ROOT, 1.0)
        for m in range(micros):
            here = slice(m * span, (m + 1) * span)
            total = parts[0][m].astype(F32)
            for part in parts[1:]:
                total = total + part[m].astype(F32)
            total = total * scaled
            high, low = split_terms(total)
            turned = dot_nt(high, turns[1]) + dot_nt(low, turns[1])
            d_line[here, width:] = (
                total * cos[here, width:] + turned * sin[here, width:]
            ).astype(BF16)
        for t, (wq, wkv) in enumerate(((q_own, kv_own), (q_other, kv_other))):
            branch = dot_nt(d_line[:, :width], wq[...]) + dot_nt(d_line[:, width:], wkv[...])
            side = slice(t * half, (t + 1) * half)
            d_gain[:, side] = jnp.sum(branch * unit[:, side], axis=0, keepdims=True)
            branch = branch.astype(BF16)
            for m in range(micros):
                for k in range(heads):
                    at = (m * heads + k) * piece
                    outs[k][m, :, t * half : (t + 1) * half] = branch[at : at + piece]

    return call(
        kernel,
        "project_back",
        [*terms, dq, *queries, *kvs, turn, cosine, sine, *row_pieces],
        [
            kept((rows, 2 * width)),
            shape((1, 2 * half), F32),
            *[shape((micros, piece, 2 * half)) for _ in range(heads)],
        ],
        [pltpu.VMEM((rows, 2 * half), F32)],
        flops=8 * rows * half * width,
    )


def weight_grad(groups):
    half = groups[0][0][0].width
    total = sum(group[0][1].width for group in groups)
    args = [view for group in groups for pair in group for view in pair]

    def kernel(*refs):
        out = refs[-1]
        at = 0
        for g, group in enumerate(groups):
            n = group[0][1].width
            a, b, c, d = refs[4 * g : 4 * g + 4]
            out[:, at : at + n] = (dot_tn(a[...], b[...]) + dot_tn(c[...], d[...])).astype(BF16)
            at += n

    rows = groups[0][0][0].array.shape[0]
    return call(
        kernel, "weight_grad", args, [shape((half, total))], flops=4 * half * rows * total
    )[0]


def late_grad(nb, gf, d_gate, d_up, hidden, packed, packed_back):
    rows, d_model = nb.shape
    units = hidden.shape[1]
    half = d_model // 2
    count = units // UNIT_BLOCK
    hidden_at, _ = pack_places(half, units, LANES)

    def kernel(*refs):
        sides = refs[:4]
        lines = refs[4:10]
        out = refs[10]
        turned = refs[11:]
        j = pl.program_id(0)

        @pl.when(j == 0)
        def _():
            for side, flat in zip(sides, turned):
                flat[...] = side[...].T

        for part in range(3):

            @pl.when(j // count == part)
            def _(part=part):
                which = (0, 0, 1)[part]
                out[...] = (
                    dot(turned[which][...], lines[part][...])
                    + dot(turned[2 + which][...], lines[3 + part][...])
                ).astype(BF16)

    def side(block):
        return pl.BlockSpec((rows, half), lambda j: (0, block))

    def line(part, first):
        return pl.BlockSpec(
            (rows, UNIT_BLOCK),
            lambda j: (0, first // UNIT_BLOCK + jnp.clip(j - part * count, 0, count - 1)),
        )

    return pl.pallas_call(
        kernel,
        grid=(3 * count,),
        in_specs=[side(0), side(0), side(1), side(0)]
        + [line(part, 0) for part in range(3)]
        + [line(0, half), line(1, half + units), line(2, hidden_at)],
        out_specs=pl.BlockSpec((half, UNIT_BLOCK), lambda j: (0, j)),
        out_shape=kept((half, 3 * units)),
        scratch_shapes=[pltpu.VMEM((half, rows), BF16)] * 4,
        compiler_params=pltpu.CompilerParams(vmem_limit_bytes=VMEM_LIMIT),
        cost_estimate=pl.CostEstimate(
            flops=12 * half * rows * units, bytes_accessed=6 * half * units, transcendentals=0
        ),
        name="late_grad",
    )(nb, gf, packed, packed_back, d_gate, d_up, hidden, packed_back, packed_back, packed)


def relative_columns(value, section, ctxs):
    width = value.shape[-1] // (2 * ctxs)
    return jnp.concatenate(
        [
            lax.dynamic_slice_in_dim(
                value, (k * 2 + (section ^ t)) * width, width, axis=value.ndim - 1
            )
            for t in range(2)
            for k in range(ctxs)
        ],
        axis=-1,
    )


def stored_columns(value, section, ctxs):
    width = value.shape[-1] // (2 * ctxs)
    return jnp.concatenate(
        [
            lax.dynamic_slice_in_dim(
                value, ((section ^ t) * ctxs + k) * width, width, axis=value.ndim - 1
            )
            for k in range(ctxs)
            for t in range(2)
        ],
        axis=-1,
    )


def send_all(pieces, axis):
    return [pieces[0]] + [swap(piece, axis, k) for k, piece in enumerate(pieces[1:], 1)]


def send_rows(rows):
    return send_all([rows] * lax.axis_size("head"), "head")


def send_blocks(rows):
    return send_all([rows] * lax.axis_size("ctx"), "ctx")


class Fetch:
    def __init__(self, shard):
        self.shard = shard

    def send(self, gate):
        self.pieces = send_blocks(after(self.shard, gate))

    def settle(self, gate=None):
        own = place(after(self.pieces, gate), lax.axis_index("ctx"))
        self.pair = (own, swap(own, "section", 1))
        return self.pair

    def direct(self, gate=None, with_rows=None):
        shard = self.shard if gate is None else after(self.shard, gate)
        pieces = send_blocks(shard)
        if with_rows is not None:
            pieces = after(pieces, with_rows)
        own = place(pieces, lax.axis_index("ctx"))
        self.pair = (own, swap(own, "section", 1))
        return pieces[1:]

    def first(self, gate=None):
        shard = self.shard if gate is None else after(self.shard, gate)
        self.own = lax.all_gather(shard, "ctx", axis=0, tiled=True)
        return self.own

    def second(self, gate=None):
        own = self.own if gate is None else after(self.own, gate)
        self.pair = (own, swap(own, "section", 1))
        return self.pair[1]


class Settle:
    def __init__(self, source):
        self.source = source

    def first(self, whole):
        self.kept = lax.psum_scatter(whole, "ctx", scatter_dimension=0, tiled=True)
        return whole

    def direct(self, whole):
        ctxs = lax.axis_size("ctx")
        ctx = lax.axis_index("ctx")
        size = whole.shape[0] // ctxs
        parts = [
            lax.dynamic_slice_in_dim(whole, (ctx ^ k) * size, size, axis=0) for k in range(ctxs)
        ]
        total = None
        for term in send_all(parts, "ctx"):
            term = term.astype(F32)
            total = term if total is None else total + term
        self.kept = total.astype(BF16)
        return whole

    def second(self, gate=None):
        kept = self.kept if gate is None else after(self.kept, gate)
        self.kept = kept
        sent = swap_from(kept, self.source)
        self.halves = (kept, sent) if self.source == 1 else (sent, kept)
        return sent


class Chain:
    def __init__(self):
        self.tasks = {}
        self.due = {}

    def plan(self, start, end, task):
        self.tasks.setdefault(start, []).append((end, task))

    def enter(self, name, value):
        done = self.due.pop(name, [])
        return after(value, done) if done else value

    def leave(self, name, value):
        for end, task in self.tasks.pop(name, []):
            result = task(value)
            if end is not None:
                self.due.setdefault(end, []).append(result)


class Plan:
    pass


def pick(first, a, b):
    return jnp.where(first, a, b)


def turning(heads_turned, heads):
    turn = np.zeros((heads * HEAD_DIM, heads * HEAD_DIM), np.float32)
    for h in range(heads_turned):
        for i in range(HALF):
            turn[h * HEAD_DIM + HALF + i, h * HEAD_DIM + i] = -1.0
            turn[h * HEAD_DIM + i, h * HEAD_DIM + HALF + i] = 1.0
    return turn


def padding(heads):
    pad = np.zeros((heads * HEAD_DIM, heads * LANES), np.float32)
    for h in range(heads):
        for i in range(HEAD_DIM):
            pad[h * HEAD_DIM + i, h * LANES + i] = 1.0
    return pad


def local(
    layer_input,
    out_cotangent,
    block_order,
    gain_attn,
    w_query,
    w_key,
    w_value,
    w_out,
    gain_ffn,
    w_gate,
    w_up,
    w_down,
):
    section = lax.axis_index("section")
    head = lax.axis_index("head")
    ctx = lax.axis_index("ctx")
    heads = lax.axis_size("head")
    ctxs = lax.axis_size("ctx")
    first = section == 0
    micros_all = layer_input.shape[0] // 2
    micros = micros_all // GROUPS
    rows_dev = layer_input.shape[1]
    d_model = layer_input.shape[2]
    span = heads * rows_dev
    rows = micros * span
    block_rows = ctxs * span // block_order.shape[1]
    d_half = d_model // ctxs // 2
    width = w_query.shape[2]
    k_width = w_key.shape[2]
    units = w_gate.shape[2]
    group_size = width // k_width
    line_heads = width // HEAD_DIM
    chain = Chain()

    turn = jnp.asarray(
        np.stack([turning(line_heads, line_heads), turning(k_width // HEAD_DIM, line_heads)]), BF16
    )
    pad = jnp.asarray(padding(line_heads), BF16)

    def places_of(order, ctx_index):
        piece = jnp.arange(span, dtype=jnp.int32)
        stored = (ctx_index * heads + (head ^ (piece // rows_dev))) * rows_dev + piece % rows_dev
        block = stored // block_rows
        match = block[:, None] == jnp.arange(order.shape[1], dtype=jnp.int32)[None, :]
        base = jnp.sum(jnp.where(match[None], order[:, None, :], 0), axis=2)
        return base * block_rows + (stored % block_rows)[None]

    frequency = jnp.power(ROPE_BASE, jnp.arange(HALF, dtype=F32) * (-2.0 / HEAD_DIM))

    def group_of(index):
        group = Plan()
        at = section * micros_all + index * micros
        group.name = "ab"[index]
        order = lax.dynamic_slice_in_dim(block_order, at, micros, axis=0)
        places_q = places_of(order, ctx)
        places_k = jnp.concatenate([places_of(order, ctx ^ k) for k in range(ctxs)], axis=1)
        group.place_q = places_q[:, :, None]
        group.place_k = places_k[:, None, :]
        angles = places_q.reshape(rows, 1).astype(F32) * frequency
        cosine, sine = jnp.cos(angles), jnp.sin(angles)
        turned = 2 * (line_heads + k_width // HEAD_DIM)
        fixed = width - k_width
        group.cosine = jnp.concatenate(
            [cosine] * turned + [jnp.ones((rows, fixed), F32)], axis=1
        )
        group.sine = jnp.concatenate([sine] * turned + [jnp.zeros((rows, fixed), F32)], axis=1)

        def mine(value):
            part = lax.dynamic_slice_in_dim(value, at, micros, axis=0)
            return relative_columns(part, section, ctxs)

        group.x = mine(layer_input)
        group.cot = mine(out_cotangent)
        group.keep, group.d_in = {}, {}
        return group

    members = [group_of(index) for index in range(GROUPS)]
    tail = members[-1].name
    for group in members:
        group.x_pieces = send_rows(group.x)

    def exchange(shard, gate=None):
        def cut(which):
            return lax.dynamic_slice_in_dim(shard, which * d_half, d_half, axis=0)

        kept, given = cut(section), cut(1 - section)
        if gate is not None:
            given = after(given, gate)
        taken = swap(given, "section", 1)
        return pick(first, kept, taken), pick(first, taken, kept)

    gains = jnp.stack([gain_attn[0], gain_ffn[0]], axis=1)
    gains = jnp.pad(gains, ((0, 0), (0, LANES - 2)))
    early_shards = exchange(
        jnp.concatenate([w_query[0], w_key[0], w_value[0], gains], axis=1)
    )
    early0 = Fetch(early_shards[0])
    out_shards = exchange(w_out[0].T)
    late_shards = exchange(jnp.concatenate([w_gate[0], w_up[0], w_down[0].T], axis=1))
    late0, late1 = Fetch(late_shards[0]), Fetch(late_shards[1])
    out0 = Fetch(out_shards[0])
    both1 = Fetch(jnp.concatenate([out_shards[1], early_shards[1]], axis=1))
    prepared = [group.x_pieces for group in members], [
        (group.cosine, group.sine, group.place_q, group.place_k) for group in members
    ]
    landed = early0.direct(None, (prepared, late_shards, out_shards, both1.shard))
    late0.first(landed)
    out0.send(landed[:1])

    def views0(name):
        if name == "o":
            return [View(part, width, 0) for part in out0.pair]
        at = {"q": (width, 0), "kv": (width, 1), "g": (LANES, 2 * width // LANES)}[name]
        return [View(part, *at) for part in early0.pair]

    def views1(name):
        at = {
            "o": (width, 0),
            "q": (width, 1),
            "kv": (width, 2),
            "g": (LANES, 3 * width // LANES),
        }[name]
        return [View(part, *at) for part in both1.pair]

    token = [None]

    def enter(name, group, value):
        if token[0] is not None and GROUPS > 1:
            value = after(value, token[0])
        return chain.enter(name + group.name, value)

    def leave(name, group, value):
        token[0] = value
        chain.leave(name + group.name, value)

    def forward(label, group, layer_in, views, late_fetch):
        keep = Plan()
        keep.x = layer_in
        pieces = group.x_pieces if label == "0" else send_rows(layer_in)
        leave(label + "F0", group, layer_in)
        yield
        pieces = enter(label + "F1", group, pieces)
        keep.x_pieces = pieces
        keep.na, keep.query, kv, keep.gains = project(
            pieces, views("q"), views("kv"), views("g"), group.cosine, group.sine, turn
        )
        kv = kv.reshape(micros, span, width)
        pieces = send_blocks(kv)
        leave(label + "F1", group, kv)
        yield
        keep.kv = enter(label + "F2", group, pieces)
        keep.prob, keep.mix, *parts = attend(
            keep.query, keep.kv, group.place_q, group.place_k, pad, views("o"),
            heads, rows_dev, group_size,
        )
        terms = send_all(parts, "head")
        leave(label + "F2", group, parts[0])
        yield
        terms = enter(label + "F3", group, terms)
        keep.mid, own_nb = add_mid(layer_in, terms, keep.gains)
        pieces = send_rows(own_nb)
        leave(label + "F3", group, own_nb)
        yield
        pieces = enter(label + "F4", group, pieces)
        keep.late = late_fetch.pair
        keep.gate, keep.up, keep.hidden, keep.nb, packed, *parts = feed(
            pieces, keep.late, units, keep.na, keep.mix
        )
        keep.packed = swap(packed, "section", 1)
        group.parts = parts
        group.keep[label] = keep
        leave(label + "F4", group, parts[0])
        if label == "0":
            terms = send_all(parts, "head")
            yield
            terms = enter(label + "F5", group, terms)
            group.out = add_out(keep.mid, terms)

    def backward(label, group, pieces, grad, views):
        keep = group.keep[label]
        pieces = enter(label + "B1", group, pieces)
        keep.d_gate, keep.d_up, keep.gf, packed, *parts = feed_back(
            pieces, keep.late, keep.gate, keep.up
        )
        keep.packed_back = swap(packed, "section", 1)
        terms = send_all(parts, "head")
        leave(label + "B1", group, parts[0])
        yield
        terms = enter(label + "B2", group, terms)
        d_mid, own_ga, keep.gain_b = norm_back(terms, keep.mid, keep.gains, 1, grad)
        pieces = send_rows(own_ga)
        leave(label + "B2", group, own_ga)
        yield
        pieces = enter(label + "B3", group, pieces)
        keep.ga, ga_other, dq, *parts = attend_back(
            pieces, views("o"), keep.mix, keep.prob, keep.query, keep.kv, pad, turn,
            group.cosine, group.sine, group_size,
        )
        terms = send_all(parts, "ctx")
        keep.ga_other = swap(ga_other, "section", 1)
        leave(label + "B3", group, parts[0])
        yield
        terms = enter(label + "B4", group, terms)
        keep.d_line, keep.gain_a, *parts = project_back(
            terms, dq, views("q"), views("kv"), turn, group.cosine, group.sine, keep.x_pieces
        )
        terms = send_all(parts, "head")
        keep.d_line_other = swap(keep.d_line, "section", 1)
        leave(label + "B4", group, parts[0])
        yield
        terms = enter(label + "B5", group, terms)
        d_input, d_low, _ = norm_back(terms, keep.x, keep.gains, 0, d_mid)
        if label == "1":
            group.d_in[label] = d_low
            group.pieces = send_rows(d_low)
        else:
            group.d_in[label] = d_input
        leave(label + "B5", group, group.d_in[label])
        yield

    def drive(*stages):
        waiting = list(stages)
        while waiting:
            waiting = [stage for stage in waiting if next(stage, stage) is not stage]

    def gather_cot(group):
        def task(gate):
            group.cot_pieces = send_rows(after(group.cot, gate))
            return group.cot_pieces

        return task

    def on_last(start, end, task):
        chain.plan(start + tail, end + tail if end else None, task)

    on_last("0F1", "0F2", out0.settle)
    for group in members:
        chain.plan("0F1" + group.name, "0F2" + group.name, gather_cot(group))
    on_last("0F3", None, late0.second)
    on_last("0F3", None, lambda gate: both1.first(late0.pair[0]))
    on_last("1F0", None, both1.second)
    on_last("1F0", None, lambda gate: late1.first(both1.pair[0]))
    on_last("1F3", None, late1.second)
    drive(*(forward("0", group, group.x, views0, late0) for group in members))

    def scatter_out(group):
        def task(gate):
            parts = after(group.parts, gate)
            group.final = add_out(group.keep["1"].mid, send_all(parts, "head"))
            return group.final

        return task

    for group in members:
        chain.plan("1B3" + group.name, "1B4" + group.name, scatter_out(group))
    drive(*(forward("1", group, group.out, views1, late1) for group in members))

    _, mix_at = pack_places(d_model // 2, units, width)

    def rows_of(label, *names):
        def joined(name):
            parts = [getattr(group.keep[label], name) for group in members]
            return parts[0] if len(parts) == 1 else jnp.concatenate(parts, axis=0)

        return [joined(name) for name in names]

    def late_of(label, gate):
        names = ("nb", "gf", "d_gate", "d_up", "hidden", "packed", "packed_back")
        return late_grad(*after(rows_of(label, *names), gate))

    def out_group(ga, mix, ga_other, packed):
        return (
            (View(ga, d_model // 2, 0), View(mix)),
            (View(ga_other), View(packed, width, mix_at // width)),
        )

    def early_group(na, d_line, packed, d_line_other):
        return (
            (View(na, d_model // 2, 0), View(d_line)),
            (View(packed, d_model // 2, 0), View(d_line_other)),
        )

    out_names = ("ga", "mix", "ga_other", "packed")
    early_names = ("na", "d_line", "packed", "d_line_other")

    def out_of(label, gate):
        return weight_grad([out_group(*after(rows_of(label, *out_names), gate))])

    def early_of(label, gate):
        return weight_grad([early_group(*after(rows_of(label, *early_names), gate))])

    def both_of(label, gate):
        values = after(rows_of(label, *out_names, *early_names), gate)
        return weight_grad([out_group(*values[:4]), early_group(*values[4:])])

    late_1, both_1, late_0, out_0, early_0 = (Settle(s) for s in (0, 0, 1, 1, 1))
    on_last("1B2", "1B3", lambda gate: late_1.first(late_of("1", gate)))
    on_last("1B5", "0B1", late_1.second)
    on_last("1B5", "0B1", lambda gate: both_1.first(both_of("1", (gate, late_1.kept))))
    on_last("0B2", "0B3", both_1.second)
    on_last("0B2", "0B3", lambda gate: late_0.first(late_of("0", (gate, both_1.kept))))
    on_last("0B3", "0B4", lambda gate: out_0.direct(out_of("0", gate)))
    on_last("0B4", None, late_0.second)
    on_last("0B4", None, lambda gate: early_0.direct(early_of("0", (gate, late_0.kept))))
    gain_mine = []

    def sum_gains(gate):
        def gain_of(label, name):
            total = getattr(members[0].keep[label], name)
            for group in members[1:]:
                total = total + getattr(group.keep[label], name)
            return total[0]

        gain_rows = after(
            jnp.stack([gain_of(label, name) for label in "01" for name in ("gain_a", "gain_b")]),
            gate,
        ).reshape(4, 2, ctxs, d_half)
        at = lambda k: lax.dynamic_index_in_dim(gain_rows, ctx ^ k, 2, keepdims=False)
        gain_sum = at(0)
        for k in range(1, ctxs):
            gain_sum = gain_sum + swap(at(k), "ctx", k)
        gain_total = gain_sum
        for k in range(1, heads):
            gain_total = gain_total + swap(gain_sum, "head", k)
        own, other = gain_total[:, 0], gain_total[:, 1]
        low, high = pick(first, own, other), pick(first, other, own)
        gain_total = jnp.concatenate([low, high], axis=1)
        gain_total = gain_total + swap(gain_total, "section", 1)
        gain_mine.append(pick(first, gain_total[:2], gain_total[2:]))
        return gain_mine[0]

    def by_layer(lower, upper):
        lower = stored_columns(lower, section, ctxs)
        upper = stored_columns(upper, section, ctxs)
        kept_rows = pick(first, lower, upper)
        got_rows = swap(pick(first, upper, lower).astype(BF16), "section", 1).astype(lower.dtype)
        return jnp.concatenate(
            [pick(first, kept_rows, got_rows), pick(first, got_rows, kept_rows)], axis=0
        )[None]

    def all_rows(name):
        parts = [name(group) for group in members]
        return parts[0] if len(parts) == 1 else jnp.concatenate(parts, axis=0)

    layer_outs = []

    def out_rows(gate):
        lower, upper = after((all_rows(lambda g: g.out), all_rows(lambda g: g.final)), gate)
        layer_outs.append(by_layer(lower, upper))
        return layer_outs[0]

    on_last("0B2", "0B4", out_rows)
    on_last("0B5", None, sum_gains)
    drive(*(backward("1", group, group.cot_pieces, group.cot, views1) for group in members))
    drive(*(backward("0", group, group.pieces, group.d_in["1"], views0) for group in members))
    out_0.second()
    early_0.second()

    def shard_of(lower, upper):
        return jnp.concatenate([pick(first, a, b) for a, b in zip(lower, upper)], axis=0)

    out_grad = shard_of(out_0.halves, [part[:, :width] for part in both_1.halves]).astype(F32)
    early_grad = shard_of(early_0.halves, [part[:, width:] for part in both_1.halves]).astype(F32)
    late = shard_of(late_0.halves, late_1.halves).astype(F32)
    g_query = early_grad[:, :width]
    g_key = early_grad[:, width : width + k_width]
    g_value = early_grad[:, width + k_width :]
    g_out = out_grad.T
    g_gate = late[:, :units]
    g_up = late[:, units : 2 * units]
    g_down = late[:, 2 * units :].T

    in_grad = by_layer(
        all_rows(lambda g: g.d_in["0"]), all_rows(lambda g: g.d_in["1"]).astype(F32)
    )
    return (
        layer_outs[0],
        in_grad,
        gain_mine[0][0][None],
        g_query[None],
        g_key[None],
        g_value[None],
        g_out[None],
        gain_mine[0][1][None],
        g_gate[None],
        g_up[None],
        g_down[None],
    )


def solution(mesh):
    row_spec = P(None, ("ctx", "head"), None)
    vector = P("section", "ctx")
    tall = P("section", "ctx", "head")
    wide = P("section", "head", "ctx")
    kept_rows = P("section", None, ("ctx", "head"), None)
    return jax.shard_map(
        local,
        mesh=mesh,
        in_specs=(row_spec, row_spec, P(), vector, tall, tall, tall, wide, vector, tall, tall, wide),
        out_specs=(kept_rows, kept_rows, vector, tall, tall, tall, wide, vector, tall, tall, wide),
        check_vma=False,
    )
```

time: 1710 us -> 666 us (0.39)
  waiting for transfers between devices: 791 us -> 264 us
  blocking collectives: 454 us -> 0 us
  matrix products: 231 us -> 0 us
  starting transfers between devices: 13.1 us -> 150 us
  Pallas kernels: 0 us -> 102 us
  other arithmetic: 108 us -> 25.5 us
  local copies, waits for them, and re-layouts: 74.8 us -> 97.3 us
    reduce_scatter x23 -> x3, waiting for transfers between devices: 440 us -> 0.01 us  [first(): self.kept = lax.psum_scatter(whole, 'ctx', scatter_dimension=0, tiled=True)]
    all_gather x34 -> x0, blocking collectives: 433 us -> none  [the longest x10 152 us: spread_grads(): return lax.all_gather(row_block, 'head', axis=0, tiled=True)]
    ppermute x8 -> x102, waiting for transfers between devices: 7.28 us -> 264 us  [the longest x97 263 us: swap(): return lax.ppermute(value, axis, [(i, i ^ step) for i in range(count)])]
    dot_general x135 -> x0, matrix products: 231 us -> none  [the longest x5 17.9 us: backward(): jnp.einsum('sd,fd->sf', d_ffn, w_down, preferred_element_type=jnp.float32)]
    ppermute x8 -> x102, starting transfers between devices: 10.3 us -> 139 us  [the longest x97 132 us: swap(): return lax.ppermute(value, axis, [(i, i ^ step) for i in range(count)])]
    unnamed x51 -> x6, waiting for transfers between devices: 124 us -> 0.1 us
    all_gather x5 -> x3, waiting for transfers between devices: 112 us -> 0.04 us  [first(): self.own = lax.all_gather(shard, 'ctx', axis=0, tiled=True)]
    reshape x5 -> x0, waiting for transfers between devices: 108 us -> none  [backward(): d_v_lin = d_value.astype(jnp.bfloat16).reshape(span_rows, -1)]
  transfers between devices with their start and end apart: 50 -> 108, of which waited for: 44 -> 47; matrix products, arithmetic and copies ran while one was open for 12% -> 7% of each run, Pallas kernels for 0% -> 11%
where the time goes in v1:
time: 666 us; the launch traced here: 655 us
  waiting for transfers between devices  264 us (40%)
  starting transfers between devices  150 us (23%)
  Pallas kernels  102 us (15%)
  local copies, waits for them, and re-layouts  97.3 us (15%)
  other arithmetic  25.5 us (4%)
  between operations  16.3 us (2%)
    ppermute x97, waiting for transfers between devices, swap(): return lax.ppermute(value, axis, [(i, i ^ step) for i in range(count)])  263 us
    ppermute x97, starting transfers between devices, swap(): return lax.ppermute(value, axis, [(i, i ^ step) for i in range(count)])  132 us
    unnamed x323, local copies, waits for them, and re-layouts  73.5 us
    pallas_call x21, Pallas kernels, call(): pl.pallas_call(kernel, grid=(1,), in_specs=specs, out_specs=out_specs, ou...  48.2 us
    pallas_call x2, Pallas kernels, late_grad(): pl.pallas_call(kernel, grid=(3 * count,), in_specs=[side(0), side(0), sid...  19 us
    pallas_call x2, Pallas kernels, feed_back(): pl.pallas_call(kernel, grid=(count,), in_specs=[rows_spec] * heads + spec...  17.8 us
    select_n x14, other arithmetic, pick(): return jnp.where(first, a, b)  17.1 us
    pallas_call x2, Pallas kernels, feed(): pl.pallas_call(kernel, grid=(count,), in_specs=[rows_spec] * heads + spec...  17 us
  transfers between devices with their start and end apart: 108, of which 47 were waited for; matrix products, arithmetic and copies ran while one was open for 7% of the time, Pallas kernels for 11%

profile of v1, /device:TPU:0, one launch (start us, length us, event | category | flops | bytes accessed | tf_op | source)
XLA Modules:
  0.0 654.7 jit_solution(2487678653191999360)
XLA Ops:
  42.0 9.0 %collective-permute-done.5.refs_2_ = bf16[192,896]{1,0:T(8,128)(2,1)S(1)} collective-permute-done((bf16[192,896]{1,0:T(8,128)(2,1)S(1)}, bf16[192,896]{1,0:T(8,128)(2,1)S(1)}, u32[]{:S(2)}, u32[]{:S(2)}) %collective-permute-start.5) | collective-permute-done | bytes 344096 | tf_op jit(solution)/shard_map/ppermute | solution.py:25
  65.5 4.9 collective-permute-done.15.refs_3_
  75.2 7.4 %collective-permute-done.10.refs_2_.refs_10_ = bf16[2,128,384]{2,1,0:T(8,128)(2,1)S(1)} collective-permute-done((bf16[2,128,384]{2,1,0:T(8,128)(2,1)}, bf16[2,128,384]{2,1,0:T(8,128)(2,1)S(1)}, u32[]{:S(2)}, u32[]{:S(2)}) %collective-permute-start.10) | collective-permute-done | bytes 196640 | tf_op jit(solution)/shard_map/ppermute | solution.py:25
  87.7 12.4 %collective-permute-done.18.refs_2_ = bf16[2,32,1536]{2,1,0:T(8,128)(2,1)} collective-permute-done((bf16[2,32,1536]{2,1,0:T(8,128)(2,1)S(1)}, bf16[2,32,1536]{2,1,0:T(8,128)(2,1)}, u32[]{:S(2)}, u32[]{:S(2)}) %collective-permute-start.18) | collective-permute-done | bytes 196640 | tf_op jit(solution)/shard_map/ppermute | solution.py:25
  102.2 5.0 attend.2
  113.6 4.8 collective-permute-done.20.refs_3_
  118.5 9.9 %collective-permute-done.21.refs_4_ = bf16[2,32,1536]{2,1,0:T(8,128)(2,1)S(1)} collective-permute-done((bf16[2,32,1536]{2,1,0:T(8,128)(2,1)S(1)}, bf16[2,32,1536]{2,1,0:T(8,128)(2,1)S(1)}, u32[]{:S(2)}, u32[]{:S(2)}) %collective-permute-start.21) | collective-permute-done | bytes 196640 | tf_op jit(solution)/shard_map/ppermute | solution.py:25
  135.0 6.8 %collective-permute-done.23.refs_1_ = bf16[2,32,1536]{2,1,0:T(8,128)(2,1)S(1)} collective-permute-done((bf16[2,32,1536]{2,1,0:T(8,128)(2,1)S(1)}, bf16[2,32,1536]{2,1,0:T(8,128)(2,1)S(1)}, u32[]{:S(2)}, u32[]{:S(2)}) %collective-permute-start.23) | collective-permute-done | bytes 196640 | tf_op jit(solution)/shard_map/ppermute | solution.py:25
  141.7 7.9 %collective-permute-done.24.refs_2_ = bf16[2,32,1536]{2,1,0:T(8,128)(2,1)S(1)} collective-permute-done((bf16[2,32,1536]{2,1,0:T(8,128)(2,1)S(1)}, bf16[2,32,1536]{2,1,0:T(8,128)(2,1)S(1)}, u32[]{:S(2)}, u32[]{:S(2)}) %collective-permute-start.24) | collective-permute-done | bytes 196640 | tf_op jit(solution)/shard_map/ppermute | solution.py:25
  149.7 8.6 %feed.2 = (f32[256,1024]{1,0:T(8,128)}, f32[256,1024]{1,0:T(8,128)}, bf16[256,1024]{1,0:T(8,128)(2,1)}, bf16[256,1536]{1,0:T(8,128)(2,1)}, bf16[256,3072]{1,0:T(...) custom-call(bf16[2,32,1536]{2,1,0:T(8,128)(2,1)S(1)} %get-tuple-elem, ...), custom_call_target="tpu_custom_call" | custom-call | flops 2415919104 | bytes 9437184 | tf_op jit(solution)/shard_map/feed/pallas_call | solution.py:330
  164.6 4.9 collective-permute-done.27.refs_2_
  169.5 9.8 %collective-permute-done.28.refs_3_ = bf16[2,32,1536]{2,1,0:T(8,128)(2,1)S(1)} collective-permute-done((bf16[2,32,1536]{2,1,0:T(8,128)(2,1)S(1)}, bf16[2,32,1536]{2,1,0:T(8,128)(2,1)S(1)}, u32[]{:S(2)}, u32[]{:S(2)}) %collective-permute-start.28) | collective-permute-done | bytes 196640 | tf_op jit(solution)/shard_map/ppermute | solution.py:25
  185.1 6.6 %collective-permute-done.30.refs_1_.refs_13_ = bf16[2,32,1536]{2,1,0:T(8,128)(2,1)S(1)} collective-permute-done((bf16[2,32,1536]{2,1,0:T(8,128)(2,1)S(1)}, bf16[2,32,1536]{2,1,0:T(8,128)(2,1)S(1)}, u32[]{:S(2)}, u32[]{:S(2)}) %collective-permute-start.30) | collective-permute-done | bytes 196640 | tf_op jit(solution)/shard_map/ppermute | solution.py:25
  191.7 8.0 %collective-permute-done.31.refs_2_.refs_14_ = bf16[2,32,1536]{2,1,0:T(8,128)(2,1)S(1)} collective-permute-done((bf16[2,32,1536]{2,1,0:T(8,128)(2,1)S(1)}, bf16[2,32,1536]{2,1,0:T(8,128)(2,1)S(1)}, u32[]{:S(2)}, u32[]{:S(2)}) %collective-permute-start.31) | collective-permute-done | bytes 196640 | tf_op jit(solution)/shard_map/ppermute | solution.py:25
  212.8 8.4 %collective-permute-done.34.refs_2_.refs_10_ = bf16[2,128,384]{2,1,0:T(8,128)(2,1)S(1)} collective-permute-done((bf16[2,128,384]{2,1,0:T(8,128)(2,1)S(1)}, bf16[2,128,384]{2,1,0:T(8,128)(2,1)S(1)}, u32[]{:S(2)}, u32[]{:S(2)}) %collective-permute-start.34) | collective-permute-done | bytes 196640 | tf_op jit(solution)/shard_map/ppermute | solution.py:25
  223.6 4.0 collective-permute-done.36.refs_4_.refs_12_
  230.5 5.0 attend.3
  235.5 5.6 collective-permute-start.37
  247.3 10.3 %collective-permute-done.38.refs_4_ = bf16[2,32,1536]{2,1,0:T(8,128)(2,1)S(1)} collective-permute-done((bf16[2,32,1536]{2,1,0:T(8,128)(2,1)S(1)}, bf16[2,32,1536]{2,1,0:T(8,128)(2,1)S(1)}, u32[]{:S(2)}, u32[]{:S(2)}) %collective-permute-start.38) | collective-permute-done | bytes 196640 | tf_op jit(solution)/shard_map/ppermute | solution.py:25
  263.3 6.7 %collective-permute-done.40.refs_1_ = bf16[2,32,1536]{2,1,0:T(8,128)(2,1)S(1)} collective-permute-done((bf16[2,32,1536]{2,1,0:T(8,128)(2,1)S(1)}, bf16[2,32,1536]{2,1,0:T(8,128)(2,1)S(1)}, u32[]{:S(2)}, u32[]{:S(2)}) %collective-permute-start.40) | collective-permute-done | bytes 196640 | tf_op jit(solution)/shard_map/ppermute | solution.py:25
  270.0 8.0 %collective-permute-done.41.refs_2_ = bf16[2,32,1536]{2,1,0:T(8,128)(2,1)S(1)} collective-permute-done((bf16[2,32,1536]{2,1,0:T(8,128)(2,1)S(1)}, bf16[2,32,1536]{2,1,0:T(8,128)(2,1)S(1)}, u32[]{:S(2)}, u32[]{:S(2)}) %collective-permute-start.41) | collective-permute-done | bytes 196640 | tf_op jit(solution)/shard_map/ppermute | solution.py:25
  281.1 8.4 %feed.3 = (f32[256,1024]{1,0:T(8,128)}, f32[256,1024]{1,0:T(8,128)}, bf16[256,1024]{1,0:T(8,128)(2,1)}, bf16[256,1536]{1,0:T(8,128)(2,1)}, bf16[256,3072]{1,0:T(...) custom-call(bf16[2,32,1536]{2,1,0:T(8,128)(2,1)S(1)} %get-tuple-elem, ...), custom_call_target="tpu_custom_call" | custom-call | flops 2415919104 | bytes 9437184 | tf_op jit(solution)/shard_map/feed/pallas_call | solution.py:330
  294.7 8.9 %feed_back.2 = (bf16[256,1024]{1,0:T(8,128)(2,1)}, bf16[256,1024]{1,0:T(8,128)(2,1)}, bf16[256,1536]{1,0:T(8,128)(2,1)}, bf16[256,2816]{1,0:T(8,128)(2,1)}, bf16...) custom-call(bf16[2,32,1536]{2,1,0:T(8,128)(2,1)S(1)} %copy-done.39, ...), custom_call_target="tpu_custom_call" | custom-call | flops 2415919104 | bytes 9437184 | tf_op jit(solution)/shard_map/feed_back/pallas_call | solution.py:402
  310.6 6.2 collective-permute-done.44.refs_4_
  316.8 8.5 %collective-permute-done.45.refs_5_ = bf16[2,32,1536]{2,1,0:T(8,128)(2,1)S(1)} collective-permute-done((bf16[2,32,1536]{2,1,0:T(8,128)(2,1)S(1)}, bf16[2,32,1536]{2,1,0:T(8,128)(2,1)S(1)}, u32[]{:S(2)}, u32[]{:S(2)}) %collective-permute-start.45) | collective-permute-done | bytes 196640 | tf_op jit(solution)/shard_map/ppermute | solution.py:25
  330.4 8.6 %late_grad.2 = bf16[768,3072]{1,0:T(8,128)(2,1)} custom-call(bf16[256,1536]{1,0:T(8,128)(2,1)S(1)} %copy-done.81, bf16[256,1536]{1,0:T(8,128)(2,1)S(1)} %copy-done.83, bf16[256,3072]{1,0:T(8,128)(2,1)S(1)} %collective-permute-done.50.refs_2_.refs_9_.refs_3_.refs_6_, bf16[256,2816]{1,0:T(8,128)(2,1)S(1)} %collective-permute-done.51.refs_3_.refs_7_.refs_8_, ...), custom_call_target="tpu_custom_call" | custom-call | flops 2415919104 | bytes 4718592 | tf_op jit(solution)/shard_map/late_grad/pallas_call | solution.py:649
  340.2 9.9 %reduce-scatter.6.cloned.1.call-start = ((), (), s32[]{:S(2)}) async-start(), calls=%async_computation.7 | async-start | bytes 2211840 | tf_op jit(solution)/shard_map/reduce_scatter | solution.py:743
  356.2 4.4 collective-permute-done.47.refs_1_
  360.6 10.2 %collective-permute-done.48.refs_2_ = bf16[2,32,1536]{2,1,0:T(8,128)(2,1)S(1)} collective-permute-done((bf16[2,32,1536]{2,1,0:T(8,128)(2,1)}, bf16[2,32,1536]{2,1,0:T(8,128)(2,1)S(1)}, u32[]{:S(2)}, u32[]{:S(2)}) %collective-permute-start.48) | collective-permute-done | bytes 196640 | tf_op jit(solution)/shard_map/ppermute | solution.py:25
  378.5 7.1 %attend_back.2 = (bf16[256,1536]{1,0:T(8,128)(2,1)}, bf16[256,768]{1,0:T(8,128)(2,1)}, bf16[256,384]{1,0:T(8,128)(2,1)S(1)}, bf16[2,128,384]{2,1,0:T(8,128)(2,1)...) custom-call(bf16[2,32,1536]{2,1,0:T(8,128)(2,1)S(1)} %copy-done.125, ...), custom_call_target="tpu_custom_call" | custom-call | flops 503316480 | bytes 8912896 | tf_op jit(solution)/shard_map/attend_back/pallas_call | solution.py:88
  395.8 8.8 %collective-permute-done.53.refs_3_ = bf16[2,32,1536]{2,1,0:T(8,128)(2,1)S(1)} collective-permute-done((bf16[2,32,1536]{2,1,0:T(8,128)(2,1)S(1)}, bf16[2,32,1536]{2,1,0:T(8,128)(2,1)S(1)}, u32[]{:S(2)}, u32[]{:S(2)}) %collective-permute-start.53) | collective-permute-done | bytes 196640 | tf_op jit(solution)/shard_map/ppermute | solution.py:25
  414.0 6.6 %collective-permute-done.58.refs_4_ = bf16[2,32,1536]{2,1,0:T(8,128)(2,1)S(1)} collective-permute-done((bf16[2,32,1536]{2,1,0:T(8,128)(2,1)S(1)}, bf16[2,32,1536]{2,1,0:T(8,128)(2,1)S(1)}, u32[]{:S(2)}, u32[]{:S(2)}) %collective-permute-start.58) | collective-permute-done | bytes 196640 | tf_op jit(solution)/shard_map/ppermute | solution.py:25
  420.5 7.6 %collective-permute-done.59.refs_5_ = bf16[2,32,1536]{2,1,0:T(8,128)(2,1)S(1)} collective-permute-done((bf16[2,32,1536]{2,1,0:T(8,128)(2,1)S(1)}, bf16[2,32,1536]{2,1,0:T(8,128)(2,1)S(1)}, u32[]{:S(2)}, u32[]{:S(2)}) %collective-permute-start.59) | collective-permute-done | bytes 196640 | tf_op jit(solution)/shard_map/ppermute | solution.py:25
  437.0 4.1 collective-permute-start.61
  443.5 4.9 collective-permute-done.61.refs_1_
  448.4 10.0 %collective-permute-done.62.refs_2_ = bf16[2,32,1536]{2,1,0:T(8,128)(2,1)S(1)} collective-permute-done((bf16[2,32,1536]{2,1,0:T(8,128)(2,1)}, bf16[2,32,1536]{2,1,0:T(8,128)(2,1)S(1)}, u32[]{:S(2)}, u32[]{:S(2)}) %collective-permute-start.62) | collective-permute-done | bytes 196640 | tf_op jit(solution)/shard_map/ppermute | solution.py:25
  462.0 8.8 %feed_back.3 = (bf16[256,1024]{1,0:T(8,128)(2,1)}, bf16[256,1024]{1,0:T(8,128)(2,1)}, bf16[256,1536]{1,0:T(8,128)(2,1)}, bf16[256,2816]{1,0:T(8,128)(2,1)}, bf16...) custom-call(bf16[2,32,1536]{2,1,0:T(8,128)(2,1)} %get-tuple-element., ...), custom_call_target="tpu_custom_call" | custom-call | flops 2415919104 | bytes 9437184 | tf_op jit(solution)/shard_map/feed_back/pallas_call | solution.py:402
  476.1 6.8 %collective-permute-done.67.refs_4_ = bf16[2,32,1536]{2,1,0:T(8,128)(2,1)S(1)} collective-permute-done((bf16[2,32,1536]{2,1,0:T(8,128)(2,1)S(1)}, bf16[2,32,1536]{2,1,0:T(8,128)(2,1)S(1)}, u32[]{:S(2)}, u32[]{:S(2)}) %collective-permute-start.67) | collective-permute-done | bytes 196640 | tf_op jit(solution)/shard_map/ppermute | solution.py:25
  482.9 7.9 %collective-permute-done.68.refs_5_ = bf16[2,32,1536]{2,1,0:T(8,128)(2,1)S(1)} collective-permute-done((bf16[2,32,1536]{2,1,0:T(8,128)(2,1)S(1)}, bf16[2,32,1536]{2,1,0:T(8,128)(2,1)S(1)}, u32[]{:S(2)}, u32[]{:S(2)}) %collective-permute-start.68) | collective-permute-done | bytes 196640 | tf_op jit(solution)/shard_map/ppermute | solution.py:25
  499.5 10.4 %late_grad.3 = bf16[768,3072]{1,0:T(8,128)(2,1)} custom-call(bf16[256,1536]{1,0:T(8,128)(2,1)S(1)} %copy-done.79, bf16[256,1536]{1,0:T(8,128)(2,1)S(1)} %copy-done.82, bf16[256,3072]{1,0:T(8,128)(2,1)S(1)} %collective-permute-done.75.refs_2_.refs_9_.refs_3_, bf16[256,2816]{1,0:T(8,128)(2,1)} %collective-permute-done.76.refs_3_.refs_7_.refs_8_, ...), custom_call_target="tpu_custom_call" | custom-call | flops 2415919104 | bytes 4718592 | tf_op jit(solution)/shard_map/late_grad/pallas_call | solution.py:649
  510.0 4.1 collective-permute-start.71
  527.5 4.1 collective-permute-done.72.refs_2_
  537.6 7.8 %attend_back.3 = (bf16[256,1536]{1,0:T(8,128)(2,1)}, bf16[256,768]{1,0:T(8,128)(2,1)S(1)}, bf16[256,384]{1,0:T(8,128)(2,1)S(1)}, bf16[2,128,384]{2,1,0:T(8,128)(...) custom-call(bf16[2,32,1536]{2,1,0:T(8,128)(2,1)S(1)} %copy-done.119, ...), custom_call_target="tpu_custom_call" | custom-call | flops 503316480 | bytes 8912896 | tf_op jit(solution)/shard_map/attend_back/pallas_call | solution.py:88
  555.9 6.4 collective-permute-done.79.refs_3_
  567.7 4.2 collective-permute-start.81
  582.3 8.5 %collective-permute-done.82.refs_5_ = bf16[2,32,1536]{2,1,0:T(8,128)(2,1)S(1)} collective-permute-done((bf16[2,32,1536]{2,1,0:T(8,128)(2,1)}, bf16[2,32,1536]{2,1,0:T(8,128)(2,1)S(1)}, u32[]{:S(2)}, u32[]{:S(2)}) %collective-permute-start.82) | collective-permute-done | bytes 196640 | tf_op jit(solution)/shard_map/ppermute | solution.py:25
  624.1 4.0 collective-permute-done.95
  628.1 5.8 collective-permute-done.94
  (607 shorter events, 291.0 us)
Async XLA Ops:
  7.2 122.1 %all-gather.4.cloned.1.call-start = ((), (), s32[]{:S(2)}) async-start(), calls=%async_computation.3 | async-start | bytes 5898240 | tf_op jit(solution)/shard_map/all_gather | solution.py:729
  9.7 23.9 %collective-permute-start = (bf16[2,32,1536]{2,1,0:T(8,128)(2,1)S(1)}, bf16[2,32,1536]{2,1,0:T(8,128)(2,1)S(1)}, u32[]{:S(2)}, u32[]{:S(2)}) collective-permute-start(bf16[2,32,1536]{2,1,0:T(8,128)(2,1)S(1)} %concatenate.54.refs_0_.refs_12_), channel_id=1, source_target_pairs={{0,4},{4,0},{8,12},{12,8},{1,5},{5,1},{9,13},{13,9},{2,6},{6,2},{1... | collective-permute-start | bytes 589832 | tf_op jit(solution)/shard_map/ppermute | solution.py:25
  12.7 26.4 %collective-permute-start.1 = (bf16[2,32,1536]{2,1,0:T(8,128)(2,1)S(1)}, bf16[2,32,1536]{2,1,0:T(8,128)(2,1)S(1)}, u32[]{:S(2)}, u32[]{:S(2)}) collective-permute-start(bf16[2,32,1536]{2,1,0:T(8,128)(2,1)S(1)} %concatenate.54.refs_0_.refs_12_), channel_id=1, source_target_pairs={{0,8},{4,12},{8,0},{12,4},{1,9},{5,13},{9,1},{13,5},{2,10},{6,14},... | collective-permute-start | bytes 589832 | tf_op jit(solution)/shard_map/ppermute | solution.py:25
  33.5 17.5 %collective-permute-start.5 = (bf16[192,896]{1,0:T(8,128)(2,1)S(1)}, bf16[192,896]{1,0:T(8,128)(2,1)S(1)}, u32[]{:S(2)}, u32[]{:S(2)}) collective-permute-start(bf16[192,896]{1,0:T(8,128)(2,1)S(1)} %get-tuple-element.183.refs_0_), channel_id=1, source_target_pairs={{0,2},{1,3},{2,0},{3,1},{4,6},{5,7},{6,4},{7,5},{8,10},{9,11},{10,... | collective-permute-start | bytes 1032200 | tf_op jit(solution)/shard_map/ppermute | solution.py:25
  52.0 127.5 %all-gather.6.cloned.1.call-start = ((), (), s32[]{:S(2)}) async-start(), calls=%async_computation.4 | async-start | bytes 2457600 | tf_op jit(solution)/shard_map/all_gather | solution.py:729
  70.5 29.6 %collective-permute-start.16 = (bf16[768,384]{1,0:T(8,128)(2,1)S(1)}, bf16[768,384]{1,0:T(8,128)(2,1)S(1)}, u32[]{:S(2)}, u32[]{:S(2)}) collective-permute-start(bf16[768,384]{1,0:T(8,128)(2,1)S(1)} %place.3.refs_8_.refs_4_), channel_id=1, source_target_pairs={{0,16},{16,0},{1,17},{17,1},{2,18},{18,2},{3,19},{19,3},{4,20},{20... | collective-permute-start | bytes 1769480 | tf_op jit(solution)/shard_map/ppermute | solution.py:25
  83.3 16.8 %collective-permute-start.18 = (bf16[2,32,1536]{2,1,0:T(8,128)(2,1)S(1)}, bf16[2,32,1536]{2,1,0:T(8,128)(2,1)}, u32[]{:S(2)}, u32[]{:S(2)}) collective-permute-start(bf16[2,32,1536]{2,1,0:T(8,128)(2,1)S(1)} %concatenate.61.refs_0_.refs_2_), channel_id=1, source_target_pairs={{0,8},{4,12},{8,0},{12,4},{1,9},{5,13},{9,1},{13,5},{2,10},{6,14},... | collective-permute-start | bytes 589832 | tf_op jit(solution)/shard_map/ppermute | solution.py:25
  111.2 17.2 %collective-permute-start.21 = (bf16[2,32,1536]{2,1,0:T(8,128)(2,1)S(1)}, bf16[2,32,1536]{2,1,0:T(8,128)(2,1)S(1)}, u32[]{:S(2)}, u32[]{:S(2)}) collective-permute-start(bf16[2,32,1536]{2,1,0:T(8,128)(2,1)S(1)} %get-tuple-element.202), channel_id=1, source_target_pairs={{0,8},{4,12},{8,0},{12,4},{1,9},{5,13},{9,1},{13,5},{2,10},{6,14},... | collective-permute-start | bytes 589832 | tf_op jit(solution)/shard_map/ppermute | solution.py:25
  111.2 17.2 %collective-permute-start.22 = (bf16[2,32,1536]{2,1,0:T(8,128)(2,1)S(1)}, bf16[2,32,1536]{2,1,0:T(8,128)(2,1)S(1)}, u32[]{:S(2)}, u32[]{:S(2)}) collective-permute-start(bf16[2,32,1536]{2,1,0:T(8,128)(2,1)S(1)} %get-tuple-element.203), channel_id=1, source_target_pairs={{0,12},{4,8},{8,4},{12,0},{1,13},{5,9},{9,5},{13,1},{2,14},{6,10},... | collective-permute-start | bytes 589832 | tf_op jit(solution)/shard_map/ppermute | solution.py:25
  129.4 20.3 %collective-permute-start.26 = (bf16[768,3072]{1,0:T(8,128)(2,1)}, bf16[768,3072]{1,0:T(8,128)(2,1)}, u32[]{:S(2)}, u32[]{:S(2)}) collective-permute-start(bf16[768,3072]{1,0:T(8,128)(2,1)} %all-gather.4.cloned.1.call-done.refs_4_.refs_6_.refs_8_), channel_id=1, source_target_pairs={{0,16},{16,0},{1,17},{17,1},{2,18},{18,2},{3,19},{19,3},{4,20},{20... | collective-permute-start | bytes 14155784 | tf_op jit(solution)/shard_map/ppermute | solution.py:25
  129.4 128.5 %all-gather.8.cloned.1.call-start = ((), (), s32[]{:S(2)}) async-start(), calls=%async_computation.5 | async-start | bytes 5898240 | tf_op jit(solution)/shard_map/all_gather | solution.py:729
  132.5 17.1 %collective-permute-start.24 = (bf16[2,32,1536]{2,1,0:T(8,128)(2,1)S(1)}, bf16[2,32,1536]{2,1,0:T(8,128)(2,1)S(1)}, u32[]{:S(2)}, u32[]{:S(2)}) collective-permute-start(bf16[2,32,1536]{2,1,0:T(8,128)(2,1)S(1)} %get-tuple-element.205.refs_0_), channel_id=1, source_target_pairs={{0,8},{4,12},{8,0},{12,4},{1,9},{5,13},{9,1},{13,5},{2,10},{6,14},... | collective-permute-start | bytes 589832 | tf_op jit(solution)/shard_map/ppermute | solution.py:25
  133.3 16.4 %collective-permute-start.25 = (bf16[2,32,1536]{2,1,0:T(8,128)(2,1)S(1)}, bf16[2,32,1536]{2,1,0:T(8,128)(2,1)S(1)}, u32[]{:S(2)}, u32[]{:S(2)}) collective-permute-start(bf16[2,32,1536]{2,1,0:T(8,128)(2,1)S(1)} %get-tuple-element.205.refs_0_), channel_id=1, source_target_pairs={{0,12},{4,8},{8,4},{12,0},{1,13},{5,9},{9,5},{13,1},{2,14},{6,10},... | collective-permute-start | bytes 589832 | tf_op jit(solution)/shard_map/ppermute | solution.py:25
  162.2 17.2 %collective-permute-start.28 = (bf16[2,32,1536]{2,1,0:T(8,128)(2,1)S(1)}, bf16[2,32,1536]{2,1,0:T(8,128)(2,1)S(1)}, u32[]{:S(2)}, u32[]{:S(2)}) collective-permute-start(bf16[2,32,1536]{2,1,0:T(8,128)(2,1)S(1)} %get-tuple-element.212), channel_id=1, source_target_pairs={{0,8},{4,12},{8,0},{12,4},{1,9},{5,13},{9,1},{13,5},{2,10},{6,14},... | collective-permute-start | bytes 589832 | tf_op jit(solution)/shard_map/ppermute | solution.py:25
  162.9 16.4 %collective-permute-start.29 = (bf16[2,32,1536]{2,1,0:T(8,128)(2,1)S(1)}, bf16[2,32,1536]{2,1,0:T(8,128)(2,1)S(1)}, u32[]{:S(2)}, u32[]{:S(2)}) collective-permute-start(bf16[2,32,1536]{2,1,0:T(8,128)(2,1)S(1)} %get-tuple-element.213), channel_id=1, source_target_pairs={{0,12},{4,8},{8,4},{12,0},{1,13},{5,9},{9,5},{13,1},{2,14},{6,10},... | collective-permute-start | bytes 589832 | tf_op jit(solution)/shard_map/ppermute | solution.py:25
  179.5 249.8 %reduce-scatter.4.cloned.1.call-start = ((), (), s32[]{:S(2)}) async-start(), calls=%async_computation.6 | async-start | bytes 5898240 | tf_op jit(solution)/shard_map/reduce_scatter | solution.py:743
  179.6 20.2 %collective-permute-start.33 = (bf16[768,1280]{1,0:T(8,128)(2,1)}, bf16[768,1280]{1,0:T(8,128)(2,1)S(1)}, u32[]{:S(2)}, u32[]{:S(2)}) collective-permute-start(bf16[768,1280]{1,0:T(8,128)(2,1)} %all-gather.6.cloned.1.call-done.refs_4_.refs_6_.refs_8_.refs_5_.refs_7_), channel_id=1, source_target_pairs={{0,16},{16,0},{1,17},{17,1},{2,18},{18,2},{3,19},{19,3},{4,20},{20... | collective-permute-start | bytes 5898248 | tf_op jit(solution)/shard_map/ppermute | solution.py:25
  182.6 17.1 %collective-permute-start.31 = (bf16[2,32,1536]{2,1,0:T(8,128)(2,1)S(1)}, bf16[2,32,1536]{2,1,0:T(8,128)(2,1)S(1)}, u32[]{:S(2)}, u32[]{:S(2)}) collective-permute-start(bf16[2,32,1536]{2,1,0:T(8,128)(2,1)S(1)} %add_out.2.refs_0_.refs_12_), channel_id=1, source_target_pairs={{0,8},{4,12},{8,0},{12,4},{1,9},{5,13},{9,1},{13,5},{2,10},{6,14},... | collective-permute-start | bytes 589832 | tf_op jit(solution)/shard_map/ppermute | solution.py:25
  183.4 16.4 %collective-permute-start.32 = (bf16[2,32,1536]{2,1,0:T(8,128)(2,1)S(1)}, bf16[2,32,1536]{2,1,0:T(8,128)(2,1)S(1)}, u32[]{:S(2)}, u32[]{:S(2)}) collective-permute-start(bf16[2,32,1536]{2,1,0:T(8,128)(2,1)S(1)} %add_out.2.refs_0_.refs_12_), channel_id=1, source_target_pairs={{0,12},{4,8},{8,4},{12,0},{1,13},{5,9},{9,5},{13,1},{2,14},{6,10},... | collective-permute-start | bytes 589832 | tf_op jit(solution)/shard_map/ppermute | solution.py:25
  210.7 16.9 %collective-permute-start.36 = (bf16[2,128,384]{2,1,0:T(8,128)(2,1)S(1)}, bf16[2,128,384]{2,1,0:T(8,128)(2,1)S(1)}, u32[]{:S(2)}, u32[]{:S(2)}) collective-permute-start(bf16[2,128,384]{2,1,0:T(8,128)(2,1)S(1)} %bitcast.72), channel_id=1, source_target_pairs={{0,3},{1,2},{2,1},{3,0},{4,7},{5,6},{6,5},{7,4},{8,11},{9,10},{10,... | collective-permute-start | bytes 589832 | tf_op jit(solution)/shard_map/ppermute | solution.py:25
  241.1 16.5 %collective-permute-start.38 = (bf16[2,32,1536]{2,1,0:T(8,128)(2,1)S(1)}, bf16[2,32,1536]{2,1,0:T(8,128)(2,1)S(1)}, u32[]{:S(2)}, u32[]{:S(2)}) collective-permute-start(bf16[2,32,1536]{2,1,0:T(8,128)(2,1)S(1)} %get-tuple-element.221), channel_id=1, source_target_pairs={{0,8},{4,12},{8,0},{12,4},{1,9},{5,13},{9,1},{13,5},{2,10},{6,14},... | collective-permute-start | bytes 589832 | tf_op jit(solution)/shard_map/ppermute | solution.py:25
  257.9 20.0 %collective-permute-start.43 = (bf16[768,3072]{1,0:T(8,128)(2,1)}, bf16[768,3072]{1,0:T(8,128)(2,1)S(1)}, u32[]{:S(2)}, u32[]{:S(2)}) collective-permute-start(bf16[768,3072]{1,0:T(8,128)(2,1)} %all-gather.8.cloned.1.call-done.refs_4_.refs_6_.refs_8_), channel_id=1, source_target_pairs={{0,16},{16,0},{1,17},{17,1},{2,18},{18,2},{3,19},{19,3},{4,20},{20... | collective-permute-start | bytes 14155784 | tf_op jit(solution)/shard_map/ppermute | solution.py:25
  260.8 17.1 %collective-permute-start.41 = (bf16[2,32,1536]{2,1,0:T(8,128)(2,1)S(1)}, bf16[2,32,1536]{2,1,0:T(8,128)(2,1)S(1)}, u32[]{:S(2)}, u32[]{:S(2)}) collective-permute-start(bf16[2,32,1536]{2,1,0:T(8,128)(2,1)S(1)} %get-tuple-element.224.refs_0_), channel_id=1, source_target_pairs={{0,8},{4,12},{8,0},{12,4},{1,9},{5,13},{9,1},{13,5},{2,10},{6,14},... | collective-permute-start | bytes 589832 | tf_op jit(solution)/shard_map/ppermute | solution.py:25
  292.2 34.3 %collective-permute-start.50 = (bf16[256,3072]{1,0:T(8,128)(2,1)}, bf16[256,3072]{1,0:T(8,128)(2,1)S(1)}, u32[]{:S(2)}, u32[]{:S(2)}) collective-permute-start(bf16[256,3072]{1,0:T(8,128)(2,1)} %get-tuple-element.245), channel_id=1, source_target_pairs={{0,16},{16,0},{1,17},{17,1},{2,18},{18,2},{3,19},{19,3},{4,20},{20... | collective-permute-start | bytes 4718600 | tf_op jit(solution)/shard_map/ppermute | solution.py:25
  303.6 22.9 %collective-permute-start.51 = (bf16[256,2816]{1,0:T(8,128)(2,1)}, bf16[256,2816]{1,0:T(8,128)(2,1)S(1)}, u32[]{:S(2)}, u32[]{:S(2)}) collective-permute-start(bf16[256,2816]{1,0:T(8,128)(2,1)} %get-tuple-element.246), channel_id=1, source_target_pairs={{0,16},{16,0},{1,17},{17,1},{2,18},{18,2},{3,19},{19,3},{4,20},{20... | collective-permute-start | bytes 4325384 | tf_op jit(solution)/shard_map/ppermute | solution.py:25
  308.2 17.1 %collective-permute-start.45 = (bf16[2,32,1536]{2,1,0:T(8,128)(2,1)S(1)}, bf16[2,32,1536]{2,1,0:T(8,128)(2,1)S(1)}, u32[]{:S(2)}, u32[]{:S(2)}) collective-permute-start(bf16[2,32,1536]{2,1,0:T(8,128)(2,1)S(1)} %get-tuple-element.237), channel_id=1, source_target_pairs={{0,8},{4,12},{8,0},{12,4},{1,9},{5,13},{9,1},{13,5},{2,10},{6,14},... | collective-permute-start | bytes 589832 | tf_op jit(solution)/shard_map/ppermute | solution.py:25
  309.0 16.3 %collective-permute-start.46 = (bf16[2,32,1536]{2,1,0:T(8,128)(2,1)S(1)}, bf16[2,32,1536]{2,1,0:T(8,128)(2,1)S(1)}, u32[]{:S(2)}, u32[]{:S(2)}) collective-permute-start(bf16[2,32,1536]{2,1,0:T(8,128)(2,1)S(1)} %get-tuple-element.238), channel_id=1, source_target_pairs={{0,12},{4,8},{8,4},{12,0},{1,13},{5,9},{9,5},{13,1},{2,14},{6,10},... | collective-permute-start | bytes 589832 | tf_op jit(solution)/shard_map/ppermute | solution.py:25
  340.2 154.0 %reduce-scatter.6.cloned.1.call-start = ((), (), s32[]{:S(2)}) async-start(), calls=%async_computation.7 | async-start | bytes 2211840 | tf_op jit(solution)/shard_map/reduce_scatter | solution.py:743
  353.7 17.1 %collective-permute-start.48 = (bf16[2,32,1536]{2,1,0:T(8,128)(2,1)}, bf16[2,32,1536]{2,1,0:T(8,128)(2,1)S(1)}, u32[]{:S(2)}, u32[]{:S(2)}) collective-permute-start(bf16[2,32,1536]{2,1,0:T(8,128)(2,1)} %copy-done.124), channel_id=1, source_target_pairs={{0,8},{4,12},{8,0},{12,4},{1,9},{5,13},{9,1},{13,5},{2,10},{6,14},... | collective-permute-start | bytes 589832 | tf_op jit(solution)/shard_map/ppermute | solution.py:25
  404.6 24.7 %collective-permute-start.65 = (bf16[256,768]{1,0:T(8,128)(2,1)}, bf16[256,768]{1,0:T(8,128)(2,1)}, u32[]{:S(2)}, u32[]{:S(2)}) collective-permute-start(bf16[256,768]{1,0:T(8,128)(2,1)} %get-tuple-element.280), channel_id=1, source_target_pairs={{0,16},{16,0},{1,17},{17,1},{2,18},{18,2},{3,19},{19,3},{4,20},{20... | collective-permute-start | bytes 1179656 | tf_op jit(solution)/shard_map/ppermute | solution.py:25
  409.4 19.9 %collective-permute-start.66 = (bf16[256,768]{1,0:T(8,128)(2,1)}, bf16[256,768]{1,0:T(8,128)(2,1)}, u32[]{:S(2)}, u32[]{:S(2)}) collective-permute-start(bf16[256,768]{1,0:T(8,128)(2,1)} %get-tuple-element.287.refs_5_), channel_id=1, source_target_pairs={{0,16},{16,0},{1,17},{17,1},{2,18},{18,2},{3,19},{19,3},{4,20},{20... | collective-permute-start | bytes 1179656 | tf_op jit(solution)/shard_map/ppermute | solution.py:25
  411.0 17.1 %collective-permute-start.59 = (bf16[2,32,1536]{2,1,0:T(8,128)(2,1)S(1)}, bf16[2,32,1536]{2,1,0:T(8,128)(2,1)S(1)}, u32[]{:S(2)}, u32[]{:S(2)}) collective-permute-start(bf16[2,32,1536]{2,1,0:T(8,128)(2,1)S(1)} %get-tuple-element.275), channel_id=1, source_target_pairs={{0,8},{4,12},{8,0},{12,4},{1,9},{5,13},{9,1},{13,5},{2,10},{6,14},... | collective-permute-start | bytes 589832 | tf_op jit(solution)/shard_map/ppermute | solution.py:25
  435.6 179.8 %reduce-scatter.8.cloned.1.call-start = ((), (), s32[]{:S(2)}) async-start(), calls=%async_computation.8 | async-start | bytes 5898240 | tf_op jit(solution)/shard_map/reduce_scatter | solution.py:743
  435.6 22.8 %collective-permute-start.64 = (bf16[192,3072]{1,0:T(8,128)(2,1)}, bf16[192,3072]{1,0:T(8,128)(2,1)S(1)}, u32[]{:S(2)}, u32[]{:S(2)}) collective-permute-start(bf16[192,3072]{1,0:T(8,128)(2,1)} %reduce-scatter.4.cloned.1.call-done), channel_id=1, source_target_pairs={{0,16},{1,17},{2,18},{3,19},{4,20},{5,21},{6,22},{7,23},{8,24},{9,... | collective-permute-start | bytes 3538952 | tf_op jit(solution)/shard_map/ppermute | solution.py:29
  441.1 17.4 %collective-permute-start.62 = (bf16[2,32,1536]{2,1,0:T(8,128)(2,1)}, bf16[2,32,1536]{2,1,0:T(8,128)(2,1)S(1)}, u32[]{:S(2)}, u32[]{:S(2)}) collective-permute-start(bf16[2,32,1536]{2,1,0:T(8,128)(2,1)} %get-tuple-element.290.refs_0_.refs_2_), channel_id=1, source_target_pairs={{0,8},{4,12},{8,0},{12,4},{1,9},{5,13},{9,1},{13,5},{2,10},{6,14},... | collective-permute-start | bytes 589832 | tf_op jit(solution)/shard_map/ppermute | solution.py:25
  442.1 16.4 %collective-permute-start.63 = (bf16[2,32,1536]{2,1,0:T(8,128)(2,1)}, bf16[2,32,1536]{2,1,0:T(8,128)(2,1)S(1)}, u32[]{:S(2)}, u32[]{:S(2)}) collective-permute-start(bf16[2,32,1536]{2,1,0:T(8,128)(2,1)} %get-tuple-element.290.refs_0_.refs_2_), channel_id=1, source_target_pairs={{0,12},{4,8},{8,4},{12,0},{1,13},{5,9},{9,5},{13,1},{2,14},{6,10},... | collective-permute-start | bytes 589832 | tf_op jit(solution)/shard_map/ppermute | solution.py:25
  443.5 50.6 %collective-permute-start.75 = (bf16[256,3072]{1,0:T(8,128)(2,1)}, bf16[256,3072]{1,0:T(8,128)(2,1)S(1)}, u32[]{:S(2)}, u32[]{:S(2)}) collective-permute-start(bf16[256,3072]{1,0:T(8,128)(2,1)} %get-tuple-element.310), channel_id=1, source_target_pairs={{0,16},{16,0},{1,17},{17,1},{2,18},{18,2},{3,19},{19,3},{4,20},{20... | collective-permute-start | bytes 4718600 | tf_op jit(solution)/shard_map/ppermute | solution.py:25
  470.8 23.3 %collective-permute-start.76 = (bf16[256,2816]{1,0:T(8,128)(2,1)}, bf16[256,2816]{1,0:T(8,128)(2,1)}, u32[]{:S(2)}, u32[]{:S(2)}) collective-permute-start(bf16[256,2816]{1,0:T(8,128)(2,1)} %get-tuple-element.311), channel_id=1, source_target_pairs={{0,16},{16,0},{1,17},{17,1},{2,18},{18,2},{3,19},{19,3},{4,20},{20... | collective-permute-start | bytes 4325384 | tf_op jit(solution)/shard_map/ppermute | solution.py:25
  473.7 17.1 %collective-permute-start.68 = (bf16[2,32,1536]{2,1,0:T(8,128)(2,1)S(1)}, bf16[2,32,1536]{2,1,0:T(8,128)(2,1)S(1)}, u32[]{:S(2)}, u32[]{:S(2)}) collective-permute-start(bf16[2,32,1536]{2,1,0:T(8,128)(2,1)S(1)} %get-tuple-element.298), channel_id=1, source_target_pairs={{0,8},{4,12},{8,0},{12,4},{1,9},{5,13},{9,1},{13,5},{2,10},{6,14},... | collective-permute-start | bytes 589832 | tf_op jit(solution)/shard_map/ppermute | solution.py:25
  510.0 17.5 %collective-permute-start.71 = (bf16[2,32,1536]{2,1,0:T(8,128)(2,1)}, bf16[2,32,1536]{2,1,0:T(8,128)(2,1)}, u32[]{:S(2)}, u32[]{:S(2)}) collective-permute-start(bf16[2,32,1536]{2,1,0:T(8,128)(2,1)} %copy-done.118), channel_id=1, source_target_pairs={{0,4},{4,0},{8,12},{12,8},{1,5},{5,1},{9,13},{13,9},{2,6},{6,2},{1... | collective-permute-start | bytes 589832 | tf_op jit(solution)/shard_map/ppermute | solution.py:25
  514.1 17.5 %collective-permute-start.72 = (bf16[2,32,1536]{2,1,0:T(8,128)(2,1)}, bf16[2,32,1536]{2,1,0:T(8,128)(2,1)}, u32[]{:S(2)}, u32[]{:S(2)}) collective-permute-start(bf16[2,32,1536]{2,1,0:T(8,128)(2,1)} %copy-done.118), channel_id=1, source_target_pairs={{0,8},{4,12},{8,0},{12,4},{1,9},{5,13},{9,1},{13,5},{2,10},{6,14},... | collective-permute-start | bytes 589832 | tf_op jit(solution)/shard_map/ppermute | solution.py:25
  515.0 16.5 %collective-permute-start.73 = (bf16[2,32,1536]{2,1,0:T(8,128)(2,1)}, bf16[2,32,1536]{2,1,0:T(8,128)(2,1)}, u32[]{:S(2)}, u32[]{:S(2)}) collective-permute-start(bf16[2,32,1536]{2,1,0:T(8,128)(2,1)} %copy-done.118), channel_id=1, source_target_pairs={{0,12},{4,8},{8,4},{12,0},{1,13},{5,9},{9,5},{13,1},{2,14},{6,10},... | collective-permute-start | bytes 589832 | tf_op jit(solution)/shard_map/ppermute | solution.py:25
  526.5 18.9 %collective-permute-start.70 = (bf16[2,32,1536]{2,1,0:T(8,128)(2,1)}, bf16[2,32,1536]{2,1,0:T(8,128)(2,1)}, u32[]{:S(2)}, u32[]{:S(2)}) collective-permute-start(bf16[2,32,1536]{2,1,0:T(8,128)(2,1)} %broadcast_select_fusion.9), channel_id=1, source_target_pairs={{0,16},{16,0},{1,17},{17,1},{2,18},{18,2},{3,19},{19,3},{4,20},{20... | collective-permute-start | bytes 589832 | tf_op jit(solution)/shard_map/ppermute | solution.py:25
  578.0 17.6 %collective-permute-start.99 = (bf16[192,384]{1,0:T(8,128)(2,1)}, bf16[192,384]{1,0:T(8,128)(2,1)}, u32[]{:S(2)}, u32[]{:S(2)}) collective-permute-start(bf16[192,384]{1,0:T(8,128)(2,1)} %get-tuple-element.424), channel_id=1, source_target_pairs={{0,3},{1,2},{2,1},{3,0},{4,7},{5,6},{6,5},{7,4},{8,11},{9,10},{10,... | collective-permute-start | bytes 442376 | tf_op jit(solution)/shard_map/ppermute | solution.py:25
  580.0 16.3 %collective-permute-start.98 = (bf16[192,384]{1,0:T(8,128)(2,1)}, bf16[192,384]{1,0:T(8,128)(2,1)}, u32[]{:S(2)}, u32[]{:S(2)}) collective-permute-start(bf16[192,384]{1,0:T(8,128)(2,1)} %get-tuple-element.425), channel_id=1, source_target_pairs={{0,2},{1,3},{2,0},{3,1},{4,6},{5,7},{6,4},{7,5},{8,10},{9,11},{10,... | collective-permute-start | bytes 442376 | tf_op jit(solution)/shard_map/ppermute | solution.py:25
  581.3 16.3 %collective-permute-start.97 = (bf16[192,384]{1,0:T(8,128)(2,1)}, bf16[192,384]{1,0:T(8,128)(2,1)}, u32[]{:S(2)}, u32[]{:S(2)}) collective-permute-start(bf16[192,384]{1,0:T(8,128)(2,1)} %get-tuple-element.423), channel_id=1, source_target_pairs={{0,1},{1,0},{2,3},{3,2},{4,5},{5,4},{6,7},{7,6},{8,9},{9,8},{10,11... | collective-permute-start | bytes 442376 | tf_op jit(solution)/shard_map/ppermute | solution.py:25
  590.8 24.6 %collective-permute-start.92 = (bf16[256,768]{1,0:T(8,128)(2,1)S(1)}, bf16[256,768]{1,0:T(8,128)(2,1)}, u32[]{:S(2)}, u32[]{:S(2)}) collective-permute-start(bf16[256,768]{1,0:T(8,128)(2,1)S(1)} %copy-done.106), channel_id=1, source_target_pairs={{0,16},{16,0},{1,17},{17,1},{2,18},{18,2},{3,19},{19,3},{4,20},{20... | collective-permute-start | bytes 1179656 | tf_op jit(solution)/shard_map/ppermute | solution.py:25
  622.8 18.8 %collective-permute-start.101 = (bf16[192,3072]{1,0:T(8,128)(2,1)}, bf16[192,3072]{1,0:T(8,128)(2,1)}, u32[]{:S(2)}, u32[]{:S(2)}) collective-permute-start(bf16[192,3072]{1,0:T(8,128)(2,1)} %reduce-scatter.8.cloned.1.call-done), channel_id=1, source_target_pairs={{16,0},{17,1},{18,2},{19,3},{20,4},{21,5},{22,6},{23,7},{24,8},{25... | collective-permute-start | bytes 3538952 | tf_op jit(solution)/shard_map/ppermute | solution.py:29
  (218 other events, 2423.6 us)
Sparse Core Ops, SparseCore 0:
  52.0 69.0 all-gather.3
  129.5 33.7 all-gather.5
  179.6 65.0 all-gather.7
  340.3 62.7 reduce-scatter.3
  435.7 34.0 reduce-scatter.5
  510.1 62.6 reduce-scatter.7

commit v2 on v1

--- a/solution.py
+++ b/solution.py
@@ -17,7 +17,8 @@
 F32 = jnp.float32
 BF16 = jnp.bfloat16
 GROUPS = 1
-VMEM_LIMIT = 48 * 1024 * 1024
+VMEM_LARGE = 60 * 1024 * 1024
+VMEM_SMALL = 12 * 1024 * 1024
 
 
 def swap(value, axis, step):
@@ -65,7 +66,7 @@
         self.block = block
 
 
-def call(kernel, name, args, outs, scratch=(), flops=0):
+def call(kernel, name, args, outs, scratch=(), flops=0, limit=VMEM_LARGE):
     specs, arrays = [], []
     size = 0
     for arg in args:
@@ -92,7 +93,7 @@
         out_specs=out_specs,
         out_shape=outs,
         scratch_shapes=list(scratch),
-        compiler_params=pltpu.CompilerParams(vmem_limit_bytes=VMEM_LIMIT),
+        compiler_params=pltpu.CompilerParams(vmem_limit_bytes=limit),
         cost_estimate=pl.CostEstimate(flops=flops, bytes_accessed=size, transcendentals=0),
         name=name,
     )(*arrays)
@@ -245,7 +246,11 @@
         nb[...] = (total * scale * gain[1:2, :]).astype(BF16)
 
     return call(
-        kernel, "add_mid", [x, gains, *terms], [shape(x.shape, F32), shape(x.shape)]
+        kernel,
+        "add_mid",
+        [x, gains, *terms],
+        [shape(x.shape, F32), shape(x.shape)],
+        limit=VMEM_SMALL,
     )
 
 
@@ -256,7 +261,7 @@
             total = total + part[...].astype(F32)
         refs[-1][...] = total.astype(BF16)
 
-    return call(kernel, "add_out", [mid, *terms], [shape(mid.shape)])[0]
+    return call(kernel, "add_out", [mid, *terms], [shape(mid.shape)], limit=VMEM_SMALL)[0]
 
 
 def blocks_of(pair, units):
@@ -310,8 +315,8 @@
         low, high = nb[:, :half], nb[:, half:]
         gate = dot(low, gate_w[0][...]) + dot(high, gate_w[1][...])
         up = dot(low, up_w[0][...]) + dot(high, up_w[1][...])
-        gate_out[...] = gate
-        up_out[...] = up
+        gate_out[...] = gate.astype(BF16)
+        up_out[...] = up.astype(BF16)
         hidden = (gate * jax.nn.sigmoid(gate) * up).astype(BF16)
         hidden_out[...] = hidden
         at = pl.multiple_of(hidden_at + j * UNIT_BLOCK, UNIT_BLOCK)
@@ -337,15 +342,15 @@
         + [pl.BlockSpec((rows, mix_at + width), lambda j: (0, 0))]
         + [rows_spec] * heads,
         out_shape=[
-            kept((rows, units), F32),
-            kept((rows, units), F32),
+            kept((rows, units)),
+            kept((rows, units)),
             kept((rows, units)),
             kept((rows, d_model)),
             kept((rows, mix_at + width)),
             *[shape((micros, piece, d_model)) for _ in range(heads)],
         ],
         scratch_shapes=[pltpu.VMEM((rows, d_model), F32)],
-        compiler_params=pltpu.CompilerParams(vmem_limit_bytes=VMEM_LIMIT),
+        compiler_params=pltpu.CompilerParams(vmem_limit_bytes=VMEM_LARGE),
         cost_estimate=pl.CostEstimate(
             flops=6 * rows * d_model * units, bytes_accessed=6 * d_model * units, transcendentals=0
         ),
@@ -378,7 +383,7 @@
             packed[:, :half] = gf[:, half:]
 
         d_hidden = dot(gf[:, :half], down_w[0][...]) + dot(gf[:, half:], down_w[1][...])
-        gate_v, up_v = gate_in[...], up_in[...]
+        gate_v, up_v = gate_in[...].astype(F32), up_in[...].astype(F32)
         sigma = jax.nn.sigmoid(gate_v)
         d_gate = (d_hidden * up_v * sigma * (1.0 + gate_v * (1.0 - sigma))).astype(BF16)
         d_up = (d_hidden * gate_v * sigma).astype(BF16)
@@ -414,7 +419,7 @@
             *[shape((micros, piece, d_model)) for _ in range(heads)],
         ],
         scratch_shapes=[pltpu.VMEM((rows, d_model), F32)],
-        compiler_params=pltpu.CompilerParams(vmem_limit_bytes=VMEM_LIMIT),
+        compiler_params=pltpu.CompilerParams(vmem_limit_bytes=VMEM_LARGE),
         cost_estimate=pl.CostEstimate(
             flops=6 * rows * d_model * units, bytes_accessed=6 * d_model * units, transcendentals=0
         ),
@@ -448,6 +453,7 @@
         "norm_back",
         [residual, gains, carried, *terms],
         [shape(residual.shape, F32), shape(residual.shape), shape((1, d_model), F32)],
+        limit=VMEM_SMALL,
     )
 
 
@@ -655,7 +661,7 @@
         out_specs=pl.BlockSpec((half, UNIT_BLOCK), lambda j: (0, j)),
         out_shape=kept((half, 3 * units)),
         scratch_shapes=[pltpu.VMEM((half, rows), BF16)] * 4,
-        compiler_params=pltpu.CompilerParams(vmem_limit_bytes=VMEM_LIMIT),
+        compiler_params=pltpu.CompilerParams(vmem_limit_bytes=VMEM_LARGE),
         cost_estimate=pl.CostEstimate(
             flops=12 * half * rows * units, bytes_accessed=6 * half * units, transcendentals=0
         ),
@@ -707,8 +713,8 @@
     def __init__(self, shard):
         self.shard = shard
 
-    def send(self, gate):
-        self.pieces = send_blocks(after(self.shard, gate))
+    def send(self, gate=None):
+        self.pieces = send_blocks(self.shard if gate is None else after(self.shard, gate))
 
     def settle(self, gate=None):
         own = place(after(self.pieces, gate), lax.axis_index("ctx"))
@@ -743,7 +749,9 @@
         self.kept = lax.psum_scatter(whole, "ctx", scatter_dimension=0, tiled=True)
         return whole
 
-    def direct(self, whole):
+    def direct(self, whole, gate=None):
+        if gate is not None:
+            whole = after(whole, gate)
         ctxs = lax.axis_size("ctx")
         ctx = lax.axis_index("ctx")
         size = whole.shape[0] // ctxs
@@ -868,14 +876,21 @@
         places_k = jnp.concatenate([places_of(order, ctx ^ k) for k in range(ctxs)], axis=1)
         group.place_q = places_q[:, :, None]
         group.place_k = places_k[:, None, :]
-        angles = places_q.reshape(rows, 1).astype(F32) * frequency
-        cosine, sine = jnp.cos(angles), jnp.sin(angles)
-        turned = 2 * (line_heads + k_width // HEAD_DIM)
-        fixed = width - k_width
-        group.cosine = jnp.concatenate(
-            [cosine] * turned + [jnp.ones((rows, fixed), F32)], axis=1
-        )
-        group.sine = jnp.concatenate([sine] * turned + [jnp.zeros((rows, fixed), F32)], axis=1)
+        group.places = places_q
+
+        def make_tables(places):
+            angles = places.reshape(rows, 1).astype(F32) * frequency
+            cosine, sine = jnp.cos(angles), jnp.sin(angles)
+            turned = 2 * (line_heads + k_width // HEAD_DIM)
+            fixed = width - k_width
+            group.cosine = jnp.concatenate(
+                [cosine] * turned + [jnp.ones((rows, fixed), F32)], axis=1
+            )
+            group.sine = jnp.concatenate(
+                [sine] * turned + [jnp.zeros((rows, fixed), F32)], axis=1
+            )
+
+        group.make_tables = make_tables
 
         def mine(value):
             part = lax.dynamic_slice_in_dim(value, at, micros, axis=0)
@@ -889,7 +904,8 @@
     members = [group_of(index) for index in range(GROUPS)]
     tail = members[-1].name
     for group in members:
-        group.x_pieces = send_rows(group.x)
+        group.firsts = send_rows(group.x)
+        group.cot_pieces = [group.cot] * heads
 
     def exchange(shard, gate=None):
         def cut(which):
@@ -907,17 +923,20 @@
         jnp.concatenate([w_query[0], w_key[0], w_value[0], gains], axis=1)
     )
     early0 = Fetch(early_shards[0])
-    out_shards = exchange(w_out[0].T)
-    late_shards = exchange(jnp.concatenate([w_gate[0], w_up[0], w_down[0].T], axis=1))
+    early0.send([group.firsts[1] for group in members])
+    tables = after([group.places for group in members], early0.pieces[1])
+    for group, places in zip(members, tables):
+        group.make_tables(places)
+    early0.settle([(group.cosine, group.sine, group.firsts) for group in members])
+    landed = early0.pair[:1]
+    w_late, w_o = after(((w_gate[0], w_up[0], w_down[0]), w_out[0]), landed)
+    out_shards = exchange(w_o.T)
+    late_shards = exchange(jnp.concatenate([w_late[0], w_late[1], w_late[2].T], axis=1))
     late0, late1 = Fetch(late_shards[0]), Fetch(late_shards[1])
     out0 = Fetch(out_shards[0])
     both1 = Fetch(jnp.concatenate([out_shards[1], early_shards[1]], axis=1))
-    prepared = [group.x_pieces for group in members], [
-        (group.cosine, group.sine, group.place_q, group.place_k) for group in members
-    ]
-    landed = early0.direct(None, (prepared, late_shards, out_shards, both1.shard))
     late0.first(landed)
-    out0.send(landed[:1])
+    out0.send(landed)
 
     def views0(name):
         if name == "o":
@@ -948,7 +967,7 @@
     def forward(label, group, layer_in, views, late_fetch):
         keep = Plan()
         keep.x = layer_in
-        pieces = group.x_pieces if label == "0" else send_rows(layer_in)
+        pieces = group.firsts if label == "0" else send_rows(layer_in)
         leave(label + "F0", group, layer_in)
         yield
         pieces = enter(label + "F1", group, pieces)
@@ -990,7 +1009,8 @@
 
     def backward(label, group, pieces, grad, views):
         keep = group.keep[label]
-        pieces = enter(label + "B1", group, pieces)
+        if label == "0":
+            pieces = enter(label + "B1", group, pieces)
         keep.d_gate, keep.d_up, keep.gf, packed, *parts = feed_back(
             pieces, keep.late, keep.gate, keep.up
         )
@@ -1035,19 +1055,23 @@
         while waiting:
             waiting = [stage for stage in waiting if next(stage, stage) is not stage]
 
-    def gather_cot(group):
+    def gather_cot(group, which):
         def task(gate):
-            group.cot_pieces = send_rows(after(group.cot, gate))
-            return group.cot_pieces
+            for k in which:
+                if k < heads:
+                    group.cot_pieces[k] = swap(after(group.cot, gate), "head", k)
+            return group.cot_pieces[1:]
 
         return task
+
+    for group in members:
+        chain.plan("0F1" + group.name, "0F2" + group.name, gather_cot(group, [2, 1]))
+        chain.plan("1F1" + group.name, "1F2" + group.name, gather_cot(group, range(3, heads)))
 
     def on_last(start, end, task):
         chain.plan(start + tail, end + tail if end else None, task)
 
     on_last("0F1", "0F2", out0.settle)
-    for group in members:
-        chain.plan("0F1" + group.name, "0F2" + group.name, gather_cot(group))
     on_last("0F3", None, late0.second)
     on_last("0F3", None, lambda gate: both1.first(late0.pair[0]))
     on_last("1F0", None, both1.second)
@@ -1055,17 +1079,28 @@
     on_last("1F3", None, late1.second)
     drive(*(forward("0", group, group.x, views0, late0) for group in members))
 
-    def scatter_out(group):
+    def scatter_out(group, which):
         def task(gate):
-            parts = after(group.parts, gate)
-            group.final = add_out(group.keep["1"].mid, send_all(parts, "head"))
+            group.terms += [
+                swap(after(group.parts[k], gate), "head", k) for k in which if k < heads
+            ]
+            return group.terms[1:]
+
+        return task
+
+    def finish_out(group):
+        def task(gate):
+            group.final = add_out(group.keep["1"].mid, group.terms)
             return group.final
 
         return task
 
+    drive(*(forward("1", group, group.out, views1, late1) for group in members))
     for group in members:
-        chain.plan("1B3" + group.name, "1B4" + group.name, scatter_out(group))
-    drive(*(forward("1", group, group.out, views1, late1) for group in members))
+        group.terms = [group.parts[0]]
+        chain.plan("1B3" + group.name, "1B4" + group.name, scatter_out(group, [2, 1]))
+        chain.plan("0B3" + group.name, "0B4" + group.name, scatter_out(group, range(3, heads)))
+        chain.plan("0B4" + group.name, "0B5" + group.name, finish_out(group))
 
     _, mix_at = pack_places(d_model // 2, units, width)
 
@@ -1112,8 +1147,15 @@
     on_last("0B2", "0B3", both_1.second)
     on_last("0B2", "0B3", lambda gate: late_0.first(late_of("0", (gate, both_1.kept))))
     on_last("0B3", "0B4", lambda gate: out_0.direct(out_of("0", gate)))
-    on_last("0B4", None, late_0.second)
-    on_last("0B4", None, lambda gate: early_0.direct(early_of("0", (gate, late_0.kept))))
+    on_last("0B4", "0B5", late_0.second)
+    last = []
+
+    def last_grad(gate):
+        last.append(early_of("0", gate))
+        return last[0]
+
+    on_last("0B4", "0B5", last_grad)
+    on_last("0B5", None, lambda gate: early_0.direct(last[0], gate))
     gain_mine = []
 
     def sum_gains(gate):
@@ -1123,22 +1165,15 @@
                 total = total + getattr(group.keep[label], name)
             return total[0]
 
-        gain_rows = after(
-            jnp.stack([gain_of(label, name) for label in "01" for name in ("gain_a", "gain_b")]),
-            gate,
-        ).reshape(4, 2, ctxs, d_half)
-        at = lambda k: lax.dynamic_index_in_dim(gain_rows, ctx ^ k, 2, keepdims=False)
-        gain_sum = at(0)
-        for k in range(1, ctxs):
-            gain_sum = gain_sum + swap(at(k), "ctx", k)
-        gain_total = gain_sum
-        for k in range(1, heads):
-            gain_total = gain_total + swap(gain_sum, "head", k)
-        own, other = gain_total[:, 0], gain_total[:, 1]
-        low, high = pick(first, own, other), pick(first, other, own)
-        gain_total = jnp.concatenate([low, high], axis=1)
-        gain_total = gain_total + swap(gain_total, "section", 1)
-        gain_mine.append(pick(first, gain_total[:2], gain_total[2:]))
+        gain_rows = jnp.stack(
+            [gain_of(label, name) for label in "01" for name in ("gain_a", "gain_b")]
+        )
+        gain_rows = stored_columns(gain_rows, section, ctxs)
+        total = lax.psum(gain_rows, ("section", "head", "ctx"))
+        two = lax.dynamic_slice_in_dim(total, section * 2, 2, axis=0)
+        gain_mine.append(
+            lax.dynamic_slice_in_dim(two, ctx * 2 * d_half, 2 * d_half, axis=1)
+        )
         return gain_mine[0]
 
     def by_layer(lower, upper):
@@ -1161,8 +1196,8 @@
         layer_outs.append(by_layer(lower, upper))
         return layer_outs[0]
 
-    on_last("0B2", "0B4", out_rows)
-    on_last("0B5", None, sum_gains)
+    on_last("0B5", None, out_rows)
+    on_last("0B4", None, sum_gains)
     drive(*(backward("1", group, group.cot_pieces, group.cot, views1) for group in members))
     drive(*(backward("0", group, group.pieces, group.d_in["1"], views0) for group in members))
     out_0.second()

time: 666 us -> 639 us (0.959)
  local copies, waits for them, and re-layouts: 97.3 us -> 40.6 us
  blocking collectives: 0 us -> 39.9 us
  Pallas kernels: 102 us -> 132 us
  starting transfers between devices: 150 us -> 133 us
  waiting for transfers between devices: 264 us -> 249 us
    unnamed x323 -> x194, local copies, waits for them, and re-layouts: 73.5 us -> 27.8 us
    psum x0 -> x1, blocking collectives: none -> 39.9 us  [sum_gains(): total = lax.psum(gain_rows, ('section', 'head', 'ctx'))]
    pallas_call x21, Pallas kernels: 48.2 us -> 69.8 us  [call(): pl.pallas_call(kernel, grid=(1,), in_specs=specs, out_specs=out_specs, ou...]
    ppermute x97 -> x90, waiting for transfers between devices: 263 us -> 248 us  [swap(): return lax.ppermute(value, axis, [(i, i ^ step) for i in range(count)])]
    reduce_scatter x3, starting transfers between devices: 9.94 us -> 0.29 us  [first(): self.kept = lax.psum_scatter(whole, 'ctx', scatter_dimension=0, tiled=True)]
    ppermute x97 -> x90, starting transfers between devices: 132 us -> 125 us  [swap(): return lax.ppermute(value, axis, [(i, i ^ step) for i in range(count)])]
    select_n x14 -> x12, other arithmetic: 17.1 us -> 12.1 us  [pick(): return jnp.where(first, a, b)]
  transfers between devices with their start and end apart: 108 -> 101, of which waited for: 47 -> 48; matrix products, arithmetic and copies ran while one was open for 7% -> 5% of each run, Pallas kernels for 11% -> 15%
where the time goes in v2:
time: 639 us; the launch traced here: 630 us
  waiting for transfers between devices  249 us (39%)
  starting transfers between devices  133 us (21%)
  Pallas kernels  132 us (21%)
  local copies, waits for them, and re-layouts  40.6 us (6%)
  blocking collectives  39.9 us (6%)
  other arithmetic  19.7 us (3%)
  between operations  15.9 us (2%)
    ppermute x90, waiting for transfers between devices, swap(): return lax.ppermute(value, axis, [(i, i ^ step) for i in range(count)])  248 us
    ppermute x90, starting transfers between devices, swap(): return lax.ppermute(value, axis, [(i, i ^ step) for i in range(count)])  125 us
    pallas_call x21, Pallas kernels, call(): pl.pallas_call(kernel, grid=(1,), in_specs=specs, out_specs=out_specs, ou...  69.8 us
    psum x1, blocking collectives, sum_gains(): total = lax.psum(gain_rows, ('section', 'head', 'ctx'))  39.9 us
    unnamed x194, local copies, waits for them, and re-layouts  27.8 us
    pallas_call x2, Pallas kernels, late_grad(): pl.pallas_call(kernel, grid=(3 * count,), in_specs=[side(0), side(0), sid...  23.4 us
    pallas_call x2, Pallas kernels, feed_back(): pl.pallas_call(kernel, grid=(count,), in_specs=[rows_spec] * heads + spec...  20.1 us
    pallas_call x2, Pallas kernels, feed(): pl.pallas_call(kernel, grid=(count,), in_specs=[rows_spec] * heads + spec...  18.4 us
  transfers between devices with their start and end apart: 101, of which 48 were waited for; matrix products, arithmetic and copies ran while one was open for 5% of the time, Pallas kernels for 15%

profile of v2, /device:TPU:0, one launch (start us, length us, event | category | flops | bytes accessed | tf_op | source)
XLA Modules:
  0.0 629.6 jit_solution(8693326481958131821)
XLA Ops:
  25.2 6.0 collective-permute-done.4.refs_1_
  34.7 4.7 collective-permute-done.5.refs_2_
  56.9 5.5 project.2
  71.3 7.1 %collective-permute-done.8.refs_2_.refs_10_ = bf16[2,128,384]{2,1,0:T(8,128)(2,1)S(1)} collective-permute-done((bf16[2,128,384]{2,1,0:T(8,128)(2,1)S(1)}, bf16[2,128,384]{2,1,0:T(8,128)(2,1)S(1)}, u32[]{:S(2)}, u32[]{:S(2)}) %collective-permute-start.8) | collective-permute-done | bytes 196640 | tf_op jit(solution)/shard_map/ppermute | solution.py:26
  83.4 6.8 %collective-permute-done.12.refs_2_ = bf16[2,32,1536]{2,1,0:T(8,128)(2,1)S(1)} collective-permute-done((bf16[2,32,1536]{2,1,0:T(8,128)(2,1)S(1)}, bf16[2,32,1536]{2,1,0:T(8,128)(2,1)S(1)}, u32[]{:S(2)}, u32[]{:S(2)}) %collective-permute-start.12) | collective-permute-done | bytes 196640 | tf_op jit(solution)/shard_map/ppermute | solution.py:26
  91.1 6.2 attend.2
  101.7 5.3 collective-permute-done.18.refs_3_
  107.0 7.9 %collective-permute-done.19.refs_4_ = bf16[2,32,1536]{2,1,0:T(8,128)(2,1)S(1)} collective-permute-done((bf16[2,32,1536]{2,1,0:T(8,128)(2,1)}, bf16[2,32,1536]{2,1,0:T(8,128)(2,1)S(1)}, u32[]{:S(2)}, u32[]{:S(2)}) %collective-permute-start.19) | collective-permute-done | bytes 196640 | tf_op jit(solution)/shard_map/ppermute | solution.py:26
  123.9 6.9 %collective-permute-done.21.refs_1_ = bf16[2,32,1536]{2,1,0:T(8,128)(2,1)S(1)} collective-permute-done((bf16[2,32,1536]{2,1,0:T(8,128)(2,1)S(1)}, bf16[2,32,1536]{2,1,0:T(8,128)(2,1)S(1)}, u32[]{:S(2)}, u32[]{:S(2)}) %collective-permute-start.21) | collective-permute-done | bytes 196640 | tf_op jit(solution)/shard_map/ppermute | solution.py:26
  130.8 7.8 %collective-permute-done.22.refs_2_ = bf16[2,32,1536]{2,1,0:T(8,128)(2,1)S(1)} collective-permute-done((bf16[2,32,1536]{2,1,0:T(8,128)(2,1)S(1)}, bf16[2,32,1536]{2,1,0:T(8,128)(2,1)S(1)}, u32[]{:S(2)}, u32[]{:S(2)}) %collective-permute-start.22) | collective-permute-done | bytes 196640 | tf_op jit(solution)/shard_map/ppermute | solution.py:26
  139.4 9.4 %feed.2 = (bf16[256,1024]{1,0:T(8,128)(2,1)}, bf16[256,1024]{1,0:T(8,128)(2,1)}, bf16[256,1024]{1,0:T(8,128)(2,1)}, bf16[256,1536]{1,0:T(8,128)(2,1)}, bf16[256,...) custom-call(bf16[2,32,1536]{2,1,0:T(8,128)(2,1)} %copy-done.14, ...), custom_call_target="tpu_custom_call" | custom-call | flops 2415919104 | bytes 9437184 | tf_op jit(solution)/shard_map/feed/pallas_call | solution.py:335
  154.9 5.1 collective-permute-done.26.refs_2_
  160.1 9.8 %collective-permute-done.27.refs_3_ = bf16[2,32,1536]{2,1,0:T(8,128)(2,1)S(1)} collective-permute-done((bf16[2,32,1536]{2,1,0:T(8,128)(2,1)}, bf16[2,32,1536]{2,1,0:T(8,128)(2,1)S(1)}, u32[]{:S(2)}, u32[]{:S(2)}) %collective-permute-start.27) | collective-permute-done | bytes 196640 | tf_op jit(solution)/shard_map/ppermute | solution.py:26
  176.5 6.8 %collective-permute-done.29.refs_1_.refs_13_ = bf16[2,32,1536]{2,1,0:T(8,128)(2,1)S(1)} collective-permute-done((bf16[2,32,1536]{2,1,0:T(8,128)(2,1)S(1)}, bf16[2,32,1536]{2,1,0:T(8,128)(2,1)S(1)}, u32[]{:S(2)}, u32[]{:S(2)}) %collective-permute-start.29) | collective-permute-done | bytes 196640 | tf_op jit(solution)/shard_map/ppermute | solution.py:26
  183.3 7.9 %collective-permute-done.30.refs_2_.refs_14_ = bf16[2,32,1536]{2,1,0:T(8,128)(2,1)S(1)} collective-permute-done((bf16[2,32,1536]{2,1,0:T(8,128)(2,1)S(1)}, bf16[2,32,1536]{2,1,0:T(8,128)(2,1)S(1)}, u32[]{:S(2)}, u32[]{:S(2)}) %collective-permute-start.30) | collective-permute-done | bytes 196640 | tf_op jit(solution)/shard_map/ppermute | solution.py:26
  193.3 5.2 project.3
  204.5 4.6 collective-permute-done.33.refs_2_.refs_10_
  216.6 6.3 attend.3
  222.9 6.7 %collective-permute-start.37 = (bf16[2,32,1536]{2,1,0:T(8,128)(2,1)}, bf16[2,32,1536]{2,1,0:T(8,128)(2,1)S(1)}, u32[]{:S(2)}, u32[]{:S(2)}) collective-permute-start(bf16[2,32,1536]{2,1,0:T(8,128)(2,1)} %get-tuple-element.245), channel_id=1, source_target_pairs={{0,4},{4,0},{8,12},{12,8},{1,5},{5,1},{9,13},{13,9},{2,6},{6,2},{1... | collective-permute-start | bytes 589832 | tf_op jit(solution)/shard_map/ppermute | solution.py:26
  235.5 10.3 %collective-permute-done.38.refs_4_ = bf16[2,32,1536]{2,1,0:T(8,128)(2,1)S(1)} collective-permute-done((bf16[2,32,1536]{2,1,0:T(8,128)(2,1)}, bf16[2,32,1536]{2,1,0:T(8,128)(2,1)S(1)}, u32[]{:S(2)}, u32[]{:S(2)}) %collective-permute-start.38) | collective-permute-done | bytes 196640 | tf_op jit(solution)/shard_map/ppermute | solution.py:26
  252.3 6.8 %collective-permute-done.40.refs_1_ = bf16[2,32,1536]{2,1,0:T(8,128)(2,1)S(1)} collective-permute-done((bf16[2,32,1536]{2,1,0:T(8,128)(2,1)S(1)}, bf16[2,32,1536]{2,1,0:T(8,128)(2,1)S(1)}, u32[]{:S(2)}, u32[]{:S(2)}) %collective-permute-start.40) | collective-permute-done | bytes 196640 | tf_op jit(solution)/shard_map/ppermute | solution.py:26
  259.1 7.8 %collective-permute-done.41.refs_2_ = bf16[2,32,1536]{2,1,0:T(8,128)(2,1)S(1)} collective-permute-done((bf16[2,32,1536]{2,1,0:T(8,128)(2,1)S(1)}, bf16[2,32,1536]{2,1,0:T(8,128)(2,1)S(1)}, u32[]{:S(2)}, u32[]{:S(2)}) %collective-permute-start.41) | collective-permute-done | bytes 196640 | tf_op jit(solution)/shard_map/ppermute | solution.py:26
  267.6 9.1 %feed.3 = (bf16[256,1024]{1,0:T(8,128)(2,1)}, bf16[256,1024]{1,0:T(8,128)(2,1)}, bf16[256,1024]{1,0:T(8,128)(2,1)}, bf16[256,1536]{1,0:T(8,128)(2,1)}, bf16[256,...) custom-call(bf16[2,32,1536]{2,1,0:T(8,128)(2,1)} %copy-done.15, ...), custom_call_target="tpu_custom_call" | custom-call | flops 2415919104 | bytes 9437184 | tf_op jit(solution)/shard_map/feed/pallas_call | solution.py:335
  276.8 10.1 %feed_back.2 = (bf16[256,1024]{1,0:T(8,128)(2,1)}, bf16[256,1024]{1,0:T(8,128)(2,1)}, bf16[256,1536]{1,0:T(8,128)(2,1)}, bf16[256,2816]{1,0:T(8,128)(2,1)}, bf16...) custom-call(bf16[2,32,1536]{2,1,0:T(8,128)(2,1)} %copy-done.8, ...), custom_call_target="tpu_custom_call" | custom-call | flops 2415919104 | bytes 9437184 | tf_op jit(solution)/shard_map/feed_back/pallas_call | solution.py:407
  293.7 6.7 %collective-permute-done.44.refs_4_ = bf16[2,32,1536]{2,1,0:T(8,128)(2,1)S(1)} collective-permute-done((bf16[2,32,1536]{2,1,0:T(8,128)(2,1)}, bf16[2,32,1536]{2,1,0:T(8,128)(2,1)S(1)}, u32[]{:S(2)}, u32[]{:S(2)}) %collective-permute-start.44) | collective-permute-done | bytes 196640 | tf_op jit(solution)/shard_map/ppermute | solution.py:26
  300.4 8.1 %collective-permute-done.45.refs_5_ = bf16[2,32,1536]{2,1,0:T(8,128)(2,1)S(1)} collective-permute-done((bf16[2,32,1536]{2,1,0:T(8,128)(2,1)}, bf16[2,32,1536]{2,1,0:T(8,128)(2,1)S(1)}, u32[]{:S(2)}, u32[]{:S(2)}) %collective-permute-start.45) | collective-permute-done | bytes 196640 | tf_op jit(solution)/shard_map/ppermute | solution.py:26
  312.1 11.6 %late_grad.2 = bf16[768,3072]{1,0:T(8,128)(2,1)} custom-call(bf16[256,1536]{1,0:T(8,128)(2,1)} %get-tuple-element.270.refs_0_, bf16[256,1536]{1,0:T(8,128)(2,1)} %get-tuple-element.271.refs_1_, bf16[256,3072]{1,0:T(8,128)(2,1)} %copy-done.29, bf16[256,2816]{1,0:T(8,128)(2,1)} %copy-done.30, bf16[256,1024]{1,0:T(8,128)(2,1)} %get-tuple-element.274.refs_4_, ...), custom_call_target="tpu_custom_call" | custom-call | flops 2415919104 | bytes 4718592 | tf_op jit(solution)/shard_map/late_grad/pallas_call | solution.py:655
  330.4 4.4 collective-permute-done.47.refs_1_
  334.8 10.2 %collective-permute-done.48.refs_2_ = bf16[2,32,1536]{2,1,0:T(8,128)(2,1)S(1)} collective-permute-done((bf16[2,32,1536]{2,1,0:T(8,128)(2,1)S(1)}, bf16[2,32,1536]{2,1,0:T(8,128)(2,1)S(1)}, u32[]{:S(2)}, u32[]{:S(2)}) %collective-permute-start.48) | collective-permute-done | bytes 196640 | tf_op jit(solution)/shard_map/ppermute | solution.py:26
  345.8 8.9 %attend_back.2 = (bf16[256,1536]{1,0:T(8,128)(2,1)}, bf16[256,768]{1,0:T(8,128)(2,1)}, bf16[256,384]{1,0:T(8,128)(2,1)}, bf16[2,128,384]{2,1,0:T(8,128)(2,1)}, b...) custom-call(bf16[2,32,1536]{2,1,0:T(8,128)(2,1)} %copy-done.25, ...), custom_call_target="tpu_custom_call" | custom-call | flops 503316480 | bytes 8912896 | tf_op jit(solution)/shard_map/attend_back/pallas_call | solution.py:89
  371.1 5.2 project_back.2
  380.9 6.8 %collective-permute-done.57.refs_4_ = bf16[2,32,1536]{2,1,0:T(8,128)(2,1)S(1)} collective-permute-done((bf16[2,32,1536]{2,1,0:T(8,128)(2,1)}, bf16[2,32,1536]{2,1,0:T(8,128)(2,1)S(1)}, u32[]{:S(2)}, u32[]{:S(2)}) %collective-permute-start.57) | collective-permute-done | bytes 196640 | tf_op jit(solution)/shard_map/ppermute | solution.py:26
  387.7 7.6 %collective-permute-done.58.refs_5_ = bf16[2,32,1536]{2,1,0:T(8,128)(2,1)S(1)} collective-permute-done((bf16[2,32,1536]{2,1,0:T(8,128)(2,1)}, bf16[2,32,1536]{2,1,0:T(8,128)(2,1)S(1)}, u32[]{:S(2)}, u32[]{:S(2)}) %collective-permute-start.58) | collective-permute-done | bytes 196640 | tf_op jit(solution)/shard_map/ppermute | solution.py:26
  398.3 4.2 weight_grad.3
  405.4 4.1 collective-permute-start.60
  412.0 4.7 collective-permute-done.60.refs_1_
  416.6 10.0 %collective-permute-done.61.refs_2_ = bf16[2,32,1536]{2,1,0:T(8,128)(2,1)S(1)} collective-permute-done((bf16[2,32,1536]{2,1,0:T(8,128)(2,1)S(1)}, bf16[2,32,1536]{2,1,0:T(8,128)(2,1)S(1)}, u32[]{:S(2)}, u32[]{:S(2)}) %collective-permute-start.61) | collective-permute-done | bytes 196640 | tf_op jit(solution)/shard_map/ppermute | solution.py:26
  427.9 10.0 %feed_back.3 = (bf16[256,1024]{1,0:T(8,128)(2,1)}, bf16[256,1024]{1,0:T(8,128)(2,1)}, bf16[256,1536]{1,0:T(8,128)(2,1)}, bf16[256,2816]{1,0:T(8,128)(2,1)}, bf16...) custom-call(bf16[2,32,1536]{2,1,0:T(8,128)(2,1)} %copy-done.10, ...), custom_call_target="tpu_custom_call" | custom-call | flops 2415919104 | bytes 9437184 | tf_op jit(solution)/shard_map/feed_back/pallas_call | solution.py:407
  443.2 7.0 %collective-permute-done.66.refs_4_ = bf16[2,32,1536]{2,1,0:T(8,128)(2,1)S(1)} collective-permute-done((bf16[2,32,1536]{2,1,0:T(8,128)(2,1)}, bf16[2,32,1536]{2,1,0:T(8,128)(2,1)S(1)}, u32[]{:S(2)}, u32[]{:S(2)}) %collective-permute-start.66) | collective-permute-done | bytes 196640 | tf_op jit(solution)/shard_map/ppermute | solution.py:26
  450.2 7.9 %collective-permute-done.67.refs_5_ = bf16[2,32,1536]{2,1,0:T(8,128)(2,1)S(1)} collective-permute-done((bf16[2,32,1536]{2,1,0:T(8,128)(2,1)}, bf16[2,32,1536]{2,1,0:T(8,128)(2,1)S(1)}, u32[]{:S(2)}, u32[]{:S(2)}) %collective-permute-start.67) | collective-permute-done | bytes 196640 | tf_op jit(solution)/shard_map/ppermute | solution.py:26
  459.4 11.7 %late_grad.3 = bf16[768,3072]{1,0:T(8,128)(2,1)} custom-call(bf16[256,1536]{1,0:T(8,128)(2,1)} %get-tuple-element.332.refs_0_, bf16[256,1536]{1,0:T(8,128)(2,1)} %get-tuple-element.333.refs_1_, bf16[256,3072]{1,0:T(8,128)(2,1)} %collective-permute-done.73.refs_2_.refs_9_.refs_3_, bf16[256,2816]{1,0:T(8,128)(2,1)} %collective-permute-done.74.refs_3_.refs_7_.refs_8_, ...), custom_call_target="tpu_custom_call" | custom-call | flops 2415919104 | bytes 4718592 | tf_op jit(solution)/shard_map/late_grad/pallas_call | solution.py:655
  480.0 4.8 collective-permute-done.69.refs_1_
  484.8 9.9 %collective-permute-done.70.refs_2_ = bf16[2,32,1536]{2,1,0:T(8,128)(2,1)S(1)} collective-permute-done((bf16[2,32,1536]{2,1,0:T(8,128)(2,1)S(1)}, bf16[2,32,1536]{2,1,0:T(8,128)(2,1)S(1)}, u32[]{:S(2)}, u32[]{:S(2)}) %collective-permute-start.70) | collective-permute-done | bytes 196640 | tf_op jit(solution)/shard_map/ppermute | solution.py:26
  495.5 8.7 %attend_back.3 = (bf16[256,1536]{1,0:T(8,128)(2,1)}, bf16[256,768]{1,0:T(8,128)(2,1)}, bf16[256,384]{1,0:T(8,128)(2,1)}, bf16[2,128,384]{2,1,0:T(8,128)(2,1)}, b...) custom-call(bf16[2,32,1536]{2,1,0:T(8,128)(2,1)} %copy-done.16, ...), custom_call_target="tpu_custom_call" | custom-call | flops 503316480 | bytes 8912896 | tf_op jit(solution)/shard_map/attend_back/pallas_call | solution.py:89
  516.6 4.8 collective-permute-done.78.refs_3_
  521.3 5.3 project_back.3
  540.2 39.9 %psum.7 = f32[4,1536]{1,0:T(4,128)S(1)} all-reduce(f32[4,1536]{1,0:T(4,128)S(1)} %concatenate.68), channel_id=1, replica_groups=mesh['section'=2,'head'=4,'ctx'=4] {'section','head','ctx'}, use_global_device_ids=true, to_apply=%region_7.8 | all-reduce | flops 6144 | bytes 49152 | tf_op jit(solution)/shard_map/psum | solution.py:1172
  608.7 5.1 collective-permute-done.88
  (456 shorter events, 235.9 us)
Async XLA Ops:
  7.2 109.5 %all-gather.4.cloned.1.call-start = ((), (), s32[]{:S(2)}) async-start(), calls=%async_computation.3 | async-start | bytes 5898240 | tf_op jit(solution)/shard_map/all_gather | solution.py:735
  11.7 22.9 %collective-permute-start.1 = (bf16[2,32,1536]{2,1,0:T(8,128)(2,1)S(1)}, bf16[2,32,1536]{2,1,0:T(8,128)(2,1)}, u32[]{:S(2)}, u32[]{:S(2)}) collective-permute-start(bf16[2,32,1536]{2,1,0:T(8,128)(2,1)S(1)} %concatenate.54.refs_0_.refs_12_), channel_id=1, source_target_pairs={{0,8},{4,12},{8,0},{12,4},{1,9},{5,13},{9,1},{13,5},{2,10},{6,14},... | collective-permute-start | bytes 589832 | tf_op jit(solution)/shard_map/ppermute | solution.py:26
  14.3 20.3 %collective-permute-start.2 = (bf16[2,32,1536]{2,1,0:T(8,128)(2,1)S(1)}, bf16[2,32,1536]{2,1,0:T(8,128)(2,1)}, u32[]{:S(2)}, u32[]{:S(2)}) collective-permute-start(bf16[2,32,1536]{2,1,0:T(8,128)(2,1)S(1)} %concatenate.54.refs_0_.refs_12_), channel_id=1, source_target_pairs={{0,12},{4,8},{8,4},{12,0},{1,13},{5,9},{9,5},{13,1},{2,14},{6,10},... | collective-permute-start | bytes 589832 | tf_op jit(solution)/shard_map/ppermute | solution.py:26
  23.3 16.0 %collective-permute-start.5 = (bf16[192,896]{1,0:T(8,128)(2,1)S(1)}, bf16[192,896]{1,0:T(8,128)(2,1)}, u32[]{:S(2)}, u32[]{:S(2)}) collective-permute-start(bf16[192,896]{1,0:T(8,128)(2,1)S(1)} %get-tuple-element.199.refs_0_), channel_id=1, source_target_pairs={{0,2},{1,3},{2,0},{3,1},{4,6},{5,7},{6,4},{7,5},{8,10},{9,11},{10,... | collective-permute-start | bytes 1032200 | tf_op jit(solution)/shard_map/ppermute | solution.py:26
  48.2 122.8 %all-gather.6.cloned.1.call-start = ((), (), s32[]{:S(2)}) async-start(), calls=%async_computation.4 | async-start | bytes 2457600 | tf_op jit(solution)/shard_map/all_gather | solution.py:735
  67.3 22.9 %collective-permute-start.17 = (bf16[768,384]{1,0:T(8,128)(2,1)}, bf16[768,384]{1,0:T(8,128)(2,1)S(1)}, u32[]{:S(2)}, u32[]{:S(2)}) collective-permute-start(bf16[768,384]{1,0:T(8,128)(2,1)} %place.3.refs_8_.refs_4_), channel_id=1, source_target_pairs={{0,16},{16,0},{1,17},{17,1},{2,18},{18,2},{3,19},{19,3},{4,20},{20... | collective-permute-start | bytes 1769480 | tf_op jit(solution)/shard_map/ppermute | solution.py:26
  97.5 17.4 %collective-permute-start.19 = (bf16[2,32,1536]{2,1,0:T(8,128)(2,1)}, bf16[2,32,1536]{2,1,0:T(8,128)(2,1)S(1)}, u32[]{:S(2)}, u32[]{:S(2)}) collective-permute-start(bf16[2,32,1536]{2,1,0:T(8,128)(2,1)} %get-tuple-element.219), channel_id=1, source_target_pairs={{0,8},{4,12},{8,0},{12,4},{1,9},{5,13},{9,1},{13,5},{2,10},{6,14},... | collective-permute-start | bytes 589832 | tf_op jit(solution)/shard_map/ppermute | solution.py:26
  116.7 21.9 %collective-permute-start.25 = (bf16[768,3072]{1,0:T(8,128)(2,1)}, bf16[768,3072]{1,0:T(8,128)(2,1)}, u32[]{:S(2)}, u32[]{:S(2)}) collective-permute-start(bf16[768,3072]{1,0:T(8,128)(2,1)} %all-gather.4.cloned.1.call-done.refs_4_.refs_6_.refs_8_), channel_id=1, source_target_pairs={{0,16},{16,0},{1,17},{17,1},{2,18},{18,2},{3,19},{19,3},{4,20},{20... | collective-permute-start | bytes 14155784 | tf_op jit(solution)/shard_map/ppermute | solution.py:26
  117.6 129.4 %all-gather.8.cloned.1.call-start = ((), (), s32[]{:S(2)}) async-start(), calls=%async_computation.5 | async-start | bytes 5898240 | tf_op jit(solution)/shard_map/all_gather | solution.py:735
  121.5 17.1 %collective-permute-start.22 = (bf16[2,32,1536]{2,1,0:T(8,128)(2,1)S(1)}, bf16[2,32,1536]{2,1,0:T(8,128)(2,1)S(1)}, u32[]{:S(2)}, u32[]{:S(2)}) collective-permute-start(bf16[2,32,1536]{2,1,0:T(8,128)(2,1)S(1)} %get-tuple-element.222.refs_0_), channel_id=1, source_target_pairs={{0,8},{4,12},{8,0},{12,4},{1,9},{5,13},{9,1},{13,5},{2,10},{6,14},... | collective-permute-start | bytes 589832 | tf_op jit(solution)/shard_map/ppermute | solution.py:26
  122.5 16.1 %collective-permute-start.23 = (bf16[2,32,1536]{2,1,0:T(8,128)(2,1)S(1)}, bf16[2,32,1536]{2,1,0:T(8,128)(2,1)S(1)}, u32[]{:S(2)}, u32[]{:S(2)}) collective-permute-start(bf16[2,32,1536]{2,1,0:T(8,128)(2,1)S(1)} %get-tuple-element.222.refs_0_), channel_id=1, source_target_pairs={{0,12},{4,8},{8,4},{12,0},{1,13},{5,9},{9,5},{13,1},{2,14},{6,10},... | collective-permute-start | bytes 589832 | tf_op jit(solution)/shard_map/ppermute | solution.py:26
  152.5 17.4 %collective-permute-start.27 = (bf16[2,32,1536]{2,1,0:T(8,128)(2,1)}, bf16[2,32,1536]{2,1,0:T(8,128)(2,1)S(1)}, u32[]{:S(2)}, u32[]{:S(2)}) collective-permute-start(bf16[2,32,1536]{2,1,0:T(8,128)(2,1)} %get-tuple-element.232), channel_id=1, source_target_pairs={{0,8},{4,12},{8,0},{12,4},{1,9},{5,13},{9,1},{13,5},{2,10},{6,14},... | collective-permute-start | bytes 589832 | tf_op jit(solution)/shard_map/ppermute | solution.py:26
  153.5 16.3 %collective-permute-start.28 = (bf16[2,32,1536]{2,1,0:T(8,128)(2,1)}, bf16[2,32,1536]{2,1,0:T(8,128)(2,1)S(1)}, u32[]{:S(2)}, u32[]{:S(2)}) collective-permute-start(bf16[2,32,1536]{2,1,0:T(8,128)(2,1)} %get-tuple-element.233), channel_id=1, source_target_pairs={{0,12},{4,8},{8,4},{12,0},{1,13},{5,9},{9,5},{13,1},{2,14},{6,10},... | collective-permute-start | bytes 589832 | tf_op jit(solution)/shard_map/ppermute | solution.py:26
  171.0 226.4 %reduce-scatter.4.cloned.1.call-start = ((), (), s32[]{:S(2)}) async-start(), calls=%async_computation.6 | async-start | bytes 5898240 | tf_op jit(solution)/shard_map/reduce_scatter | solution.py:749
  171.0 20.2 %collective-permute-start.32 = (bf16[768,1280]{1,0:T(8,128)(2,1)}, bf16[768,1280]{1,0:T(8,128)(2,1)S(1)}, u32[]{:S(2)}, u32[]{:S(2)}) collective-permute-start(bf16[768,1280]{1,0:T(8,128)(2,1)} %all-gather.6.cloned.1.call-done.refs_4_.refs_6_.refs_8_.refs_5_.refs_7_), channel_id=1, source_target_pairs={{0,16},{16,0},{1,17},{17,1},{2,18},{18,2},{3,19},{19,3},{4,20},{20... | collective-permute-start | bytes 5898248 | tf_op jit(solution)/shard_map/ppermute | solution.py:26
  174.1 17.1 %collective-permute-start.30 = (bf16[2,32,1536]{2,1,0:T(8,128)(2,1)S(1)}, bf16[2,32,1536]{2,1,0:T(8,128)(2,1)S(1)}, u32[]{:S(2)}, u32[]{:S(2)}) collective-permute-start(bf16[2,32,1536]{2,1,0:T(8,128)(2,1)S(1)} %add_out.2.refs_0_.refs_12_), channel_id=1, source_target_pairs={{0,8},{4,12},{8,0},{12,4},{1,9},{5,13},{9,1},{13,5},{2,10},{6,14},... | collective-permute-start | bytes 589832 | tf_op jit(solution)/shard_map/ppermute | solution.py:26
  175.1 16.1 %collective-permute-start.31 = (bf16[2,32,1536]{2,1,0:T(8,128)(2,1)S(1)}, bf16[2,32,1536]{2,1,0:T(8,128)(2,1)S(1)}, u32[]{:S(2)}, u32[]{:S(2)}) collective-permute-start(bf16[2,32,1536]{2,1,0:T(8,128)(2,1)S(1)} %add_out.2.refs_0_.refs_12_), channel_id=1, source_target_pairs={{0,12},{4,8},{8,4},{12,0},{1,13},{5,9},{9,5},{13,1},{2,14},{6,10},... | collective-permute-start | bytes 589832 | tf_op jit(solution)/shard_map/ppermute | solution.py:26
  229.6 16.1 %collective-permute-start.38 = (bf16[2,32,1536]{2,1,0:T(8,128)(2,1)}, bf16[2,32,1536]{2,1,0:T(8,128)(2,1)S(1)}, u32[]{:S(2)}, u32[]{:S(2)}) collective-permute-start(bf16[2,32,1536]{2,1,0:T(8,128)(2,1)} %get-tuple-element.246), channel_id=1, source_target_pairs={{0,8},{4,12},{8,0},{12,4},{1,9},{5,13},{9,1},{13,5},{2,10},{6,14},... | collective-permute-start | bytes 589832 | tf_op jit(solution)/shard_map/ppermute | solution.py:26
  247.0 19.9 %collective-permute-start.43 = (bf16[768,3072]{1,0:T(8,128)(2,1)}, bf16[768,3072]{1,0:T(8,128)(2,1)}, u32[]{:S(2)}, u32[]{:S(2)}) collective-permute-start(bf16[768,3072]{1,0:T(8,128)(2,1)} %all-gather.8.cloned.1.call-done.refs_4_.refs_6_.refs_8_), channel_id=1, source_target_pairs={{0,16},{16,0},{1,17},{17,1},{2,18},{18,2},{3,19},{19,3},{4,20},{20... | collective-permute-start | bytes 14155784 | tf_op jit(solution)/shard_map/ppermute | solution.py:26
  249.8 17.1 %collective-permute-start.41 = (bf16[2,32,1536]{2,1,0:T(8,128)(2,1)S(1)}, bf16[2,32,1536]{2,1,0:T(8,128)(2,1)S(1)}, u32[]{:S(2)}, u32[]{:S(2)}) collective-permute-start(bf16[2,32,1536]{2,1,0:T(8,128)(2,1)S(1)} %get-tuple-element.249.refs_0_), channel_id=1, source_target_pairs={{0,8},{4,12},{8,0},{12,4},{1,9},{5,13},{9,1},{13,5},{2,10},{6,14},... | collective-permute-start | bytes 589832 | tf_op jit(solution)/shard_map/ppermute | solution.py:26
  250.9 16.0 %collective-permute-start.42 = (bf16[2,32,1536]{2,1,0:T(8,128)(2,1)S(1)}, bf16[2,32,1536]{2,1,0:T(8,128)(2,1)S(1)}, u32[]{:S(2)}, u32[]{:S(2)}) collective-permute-start(bf16[2,32,1536]{2,1,0:T(8,128)(2,1)S(1)} %get-tuple-element.249.refs_0_), channel_id=1, source_target_pairs={{0,12},{4,8},{8,4},{12,0},{1,13},{5,9},{9,5},{13,1},{2,14},{6,10},... | collective-permute-start | bytes 589832 | tf_op jit(solution)/shard_map/ppermute | solution.py:26
  276.7 33.2 %collective-permute-start.50 = (bf16[256,3072]{1,0:T(8,128)(2,1)}, bf16[256,3072]{1,0:T(8,128)(2,1)S(1)}, u32[]{:S(2)}, u32[]{:S(2)}) collective-permute-start(bf16[256,3072]{1,0:T(8,128)(2,1)} %get-tuple-element.268), channel_id=1, source_target_pairs={{0,16},{16,0},{1,17},{17,1},{2,18},{18,2},{3,19},{19,3},{4,20},{20... | collective-permute-start | bytes 4718600 | tf_op jit(solution)/shard_map/ppermute | solution.py:26
  286.9 22.9 %collective-permute-start.51 = (bf16[256,2816]{1,0:T(8,128)(2,1)}, bf16[256,2816]{1,0:T(8,128)(2,1)S(1)}, u32[]{:S(2)}, u32[]{:S(2)}) collective-permute-start(bf16[256,2816]{1,0:T(8,128)(2,1)} %get-tuple-element.269), channel_id=1, source_target_pairs={{0,16},{16,0},{1,17},{17,1},{2,18},{18,2},{3,19},{19,3},{4,20},{20... | collective-permute-start | bytes 4325384 | tf_op jit(solution)/shard_map/ppermute | solution.py:26
  291.2 17.3 %collective-permute-start.45 = (bf16[2,32,1536]{2,1,0:T(8,128)(2,1)}, bf16[2,32,1536]{2,1,0:T(8,128)(2,1)S(1)}, u32[]{:S(2)}, u32[]{:S(2)}) collective-permute-start(bf16[2,32,1536]{2,1,0:T(8,128)(2,1)} %get-tuple-element.260), channel_id=1, source_target_pairs={{0,8},{4,12},{8,0},{12,4},{1,9},{5,13},{9,1},{13,5},{2,10},{6,14},... | collective-permute-start | bytes 589832 | tf_op jit(solution)/shard_map/ppermute | solution.py:26
  292.2 16.3 %collective-permute-start.46 = (bf16[2,32,1536]{2,1,0:T(8,128)(2,1)}, bf16[2,32,1536]{2,1,0:T(8,128)(2,1)S(1)}, u32[]{:S(2)}, u32[]{:S(2)}) collective-permute-start(bf16[2,32,1536]{2,1,0:T(8,128)(2,1)} %get-tuple-element.261), channel_id=1, source_target_pairs={{0,12},{4,8},{8,4},{12,0},{1,13},{5,9},{9,5},{13,1},{2,14},{6,10},... | collective-permute-start | bytes 589832 | tf_op jit(solution)/shard_map/ppermute | solution.py:26
  323.8 135.6 %reduce-scatter.6.cloned.1.call-start = ((), (), s32[]{:S(2)}) async-start(), calls=%async_computation.7 | async-start | bytes 2211840 | tf_op jit(solution)/shard_map/reduce_scatter | solution.py:749
  327.9 17.1 %collective-permute-start.48 = (bf16[2,32,1536]{2,1,0:T(8,128)(2,1)S(1)}, bf16[2,32,1536]{2,1,0:T(8,128)(2,1)S(1)}, u32[]{:S(2)}, u32[]{:S(2)}) collective-permute-start(bf16[2,32,1536]{2,1,0:T(8,128)(2,1)S(1)} %get-tuple-element.277.refs_0_), channel_id=1, source_target_pairs={{0,8},{4,12},{8,0},{12,4},{1,9},{5,13},{9,1},{13,5},{2,10},{6,14},... | collective-permute-start | bytes 589832 | tf_op jit(solution)/shard_map/ppermute | solution.py:26
  329.0 16.0 %collective-permute-start.49 = (bf16[2,32,1536]{2,1,0:T(8,128)(2,1)S(1)}, bf16[2,32,1536]{2,1,0:T(8,128)(2,1)S(1)}, u32[]{:S(2)}, u32[]{:S(2)}) collective-permute-start(bf16[2,32,1536]{2,1,0:T(8,128)(2,1)S(1)} %get-tuple-element.277.refs_0_), channel_id=1, source_target_pairs={{0,12},{4,8},{8,4},{12,0},{1,13},{5,9},{9,5},{13,1},{2,14},{6,10},... | collective-permute-start | bytes 589832 | tf_op jit(solution)/shard_map/ppermute | solution.py:26
  366.3 31.1 %collective-permute-start.64 = (bf16[256,768]{1,0:T(8,128)(2,1)}, bf16[256,768]{1,0:T(8,128)(2,1)S(1)}, u32[]{:S(2)}, u32[]{:S(2)}) collective-permute-start(bf16[256,768]{1,0:T(8,128)(2,1)} %get-tuple-element.303), channel_id=1, source_target_pairs={{0,16},{16,0},{1,17},{17,1},{2,18},{18,2},{3,19},{19,3},{4,20},{20... | collective-permute-start | bytes 1179656 | tf_op jit(solution)/shard_map/ppermute | solution.py:26
  376.3 21.1 %collective-permute-start.65 = (bf16[256,768]{1,0:T(8,128)(2,1)}, bf16[256,768]{1,0:T(8,128)(2,1)S(1)}, u32[]{:S(2)}, u32[]{:S(2)}) collective-permute-start(bf16[256,768]{1,0:T(8,128)(2,1)} %get-tuple-element.310.refs_5_), channel_id=1, source_target_pairs={{0,16},{16,0},{1,17},{17,1},{2,18},{18,2},{3,19},{19,3},{4,20},{20... | collective-permute-start | bytes 1179656 | tf_op jit(solution)/shard_map/ppermute | solution.py:26
  378.0 17.3 %collective-permute-start.58 = (bf16[2,32,1536]{2,1,0:T(8,128)(2,1)}, bf16[2,32,1536]{2,1,0:T(8,128)(2,1)S(1)}, u32[]{:S(2)}, u32[]{:S(2)}) collective-permute-start(bf16[2,32,1536]{2,1,0:T(8,128)(2,1)} %get-tuple-element.298), channel_id=1, source_target_pairs={{0,8},{4,12},{8,0},{12,4},{1,9},{5,13},{9,1},{13,5},{2,10},{6,14},... | collective-permute-start | bytes 589832 | tf_op jit(solution)/shard_map/ppermute | solution.py:26
  379.4 15.9 %collective-permute-start.59 = (bf16[2,32,1536]{2,1,0:T(8,128)(2,1)}, bf16[2,32,1536]{2,1,0:T(8,128)(2,1)S(1)}, u32[]{:S(2)}, u32[]{:S(2)}) collective-permute-start(bf16[2,32,1536]{2,1,0:T(8,128)(2,1)} %get-tuple-element.299), channel_id=1, source_target_pairs={{0,12},{4,8},{8,4},{12,0},{1,13},{5,9},{9,5},{13,1},{2,14},{6,10},... | collective-permute-start | bytes 589832 | tf_op jit(solution)/shard_map/ppermute | solution.py:26
  402.6 178.1 %reduce-scatter.8.cloned.1.call-start = ((), (), s32[]{:S(2)}) async-start(), calls=%async_computation.8 | async-start | bytes 5898240 | tf_op jit(solution)/shard_map/reduce_scatter | solution.py:749
  403.9 22.8 %collective-permute-start.63 = (bf16[192,3072]{1,0:T(8,128)(2,1)S(1)}, bf16[192,3072]{1,0:T(8,128)(2,1)S(1)}, u32[]{:S(2)}, u32[]{:S(2)}) collective-permute-start(bf16[192,3072]{1,0:T(8,128)(2,1)S(1)} %copy-done.39), channel_id=1, source_target_pairs={{0,16},{1,17},{2,18},{3,19},{4,20},{5,21},{6,22},{7,23},{8,24},{9,... | collective-permute-start | bytes 3538952 | tf_op jit(solution)/shard_map/ppermute | solution.py:30
  409.5 17.2 %collective-permute-start.61 = (bf16[2,32,1536]{2,1,0:T(8,128)(2,1)S(1)}, bf16[2,32,1536]{2,1,0:T(8,128)(2,1)S(1)}, u32[]{:S(2)}, u32[]{:S(2)}) collective-permute-start(bf16[2,32,1536]{2,1,0:T(8,128)(2,1)S(1)} %get-tuple-element.313.refs_0_.refs_2_), channel_id=1, source_target_pairs={{0,8},{4,12},{8,0},{12,4},{1,9},{5,13},{9,1},{13,5},{2,10},{6,14},... | collective-permute-start | bytes 589832 | tf_op jit(solution)/shard_map/ppermute | solution.py:26
  410.6 16.1 %collective-permute-start.62 = (bf16[2,32,1536]{2,1,0:T(8,128)(2,1)S(1)}, bf16[2,32,1536]{2,1,0:T(8,128)(2,1)S(1)}, u32[]{:S(2)}, u32[]{:S(2)}) collective-permute-start(bf16[2,32,1536]{2,1,0:T(8,128)(2,1)S(1)} %get-tuple-element.313.refs_0_.refs_2_), channel_id=1, source_target_pairs={{0,12},{4,8},{8,4},{12,0},{1,13},{5,9},{9,5},{13,1},{2,14},{6,10},... | collective-permute-start | bytes 589832 | tf_op jit(solution)/shard_map/ppermute | solution.py:26
  412.0 47.4 %collective-permute-start.73 = (bf16[256,3072]{1,0:T(8,128)(2,1)}, bf16[256,3072]{1,0:T(8,128)(2,1)}, u32[]{:S(2)}, u32[]{:S(2)}) collective-permute-start(bf16[256,3072]{1,0:T(8,128)(2,1)} %get-tuple-element.330), channel_id=1, source_target_pairs={{0,16},{16,0},{1,17},{17,1},{2,18},{18,2},{3,19},{19,3},{4,20},{20... | collective-permute-start | bytes 4718600 | tf_op jit(solution)/shard_map/ppermute | solution.py:26
  437.9 21.5 %collective-permute-start.74 = (bf16[256,2816]{1,0:T(8,128)(2,1)}, bf16[256,2816]{1,0:T(8,128)(2,1)}, u32[]{:S(2)}, u32[]{:S(2)}) collective-permute-start(bf16[256,2816]{1,0:T(8,128)(2,1)} %get-tuple-element.331), channel_id=1, source_target_pairs={{0,16},{16,0},{1,17},{17,1},{2,18},{18,2},{3,19},{19,3},{4,20},{20... | collective-permute-start | bytes 4325384 | tf_op jit(solution)/shard_map/ppermute | solution.py:26
  440.7 17.3 %collective-permute-start.67 = (bf16[2,32,1536]{2,1,0:T(8,128)(2,1)}, bf16[2,32,1536]{2,1,0:T(8,128)(2,1)S(1)}, u32[]{:S(2)}, u32[]{:S(2)}) collective-permute-start(bf16[2,32,1536]{2,1,0:T(8,128)(2,1)} %get-tuple-element.321), channel_id=1, source_target_pairs={{0,8},{4,12},{8,0},{12,4},{1,9},{5,13},{9,1},{13,5},{2,10},{6,14},... | collective-permute-start | bytes 589832 | tf_op jit(solution)/shard_map/ppermute | solution.py:26
  441.8 16.2 %collective-permute-start.68 = (bf16[2,32,1536]{2,1,0:T(8,128)(2,1)}, bf16[2,32,1536]{2,1,0:T(8,128)(2,1)S(1)}, u32[]{:S(2)}, u32[]{:S(2)}) collective-permute-start(bf16[2,32,1536]{2,1,0:T(8,128)(2,1)} %get-tuple-element.322), channel_id=1, source_target_pairs={{0,12},{4,8},{8,4},{12,0},{1,13},{5,9},{9,5},{13,1},{2,14},{6,10},... | collective-permute-start | bytes 589832 | tf_op jit(solution)/shard_map/ppermute | solution.py:26
  472.2 22.5 %collective-permute-start.72 = (bf16[192,1152]{1,0:T(8,128)(2,1)S(1)}, bf16[192,1152]{1,0:T(8,128)(2,1)S(1)}, u32[]{:S(2)}, u32[]{:S(2)}) collective-permute-start(bf16[192,1152]{1,0:T(8,128)(2,1)S(1)} %copy-done.59), channel_id=1, source_target_pairs={{0,16},{1,17},{2,18},{3,19},{4,20},{5,21},{6,22},{7,23},{8,24},{9,... | collective-permute-start | bytes 1327112 | tf_op jit(solution)/shard_map/ppermute | solution.py:30
  477.5 17.2 %collective-permute-start.70 = (bf16[2,32,1536]{2,1,0:T(8,128)(2,1)S(1)}, bf16[2,32,1536]{2,1,0:T(8,128)(2,1)S(1)}, u32[]{:S(2)}, u32[]{:S(2)}) collective-permute-start(bf16[2,32,1536]{2,1,0:T(8,128)(2,1)S(1)} %get-tuple-element.339.refs_0_), channel_id=1, source_target_pairs={{0,8},{4,12},{8,0},{12,4},{1,9},{5,13},{9,1},{13,5},{2,10},{6,14},... | collective-permute-start | bytes 589832 | tf_op jit(solution)/shard_map/ppermute | solution.py:26
  478.6 16.1 %collective-permute-start.71 = (bf16[2,32,1536]{2,1,0:T(8,128)(2,1)S(1)}, bf16[2,32,1536]{2,1,0:T(8,128)(2,1)S(1)}, u32[]{:S(2)}, u32[]{:S(2)}) collective-permute-start(bf16[2,32,1536]{2,1,0:T(8,128)(2,1)S(1)} %get-tuple-element.339.refs_0_), channel_id=1, source_target_pairs={{0,12},{4,8},{8,4},{12,0},{1,13},{5,9},{9,5},{13,1},{2,14},{6,10},... | collective-permute-start | bytes 589832 | tf_op jit(solution)/shard_map/ppermute | solution.py:26
  526.7 63.2 %collective-permute-start.80 = (bf16[2,32,1536]{2,1,0:T(8,128)(2,1)}, bf16[2,32,1536]{2,1,0:T(8,128)(2,1)S(1)}, u32[]{:S(2)}, u32[]{:S(2)}) collective-permute-start(bf16[2,32,1536]{2,1,0:T(8,128)(2,1)} %get-tuple-element.362), channel_id=1, source_target_pairs={{0,4},{4,0},{8,12},{12,8},{1,5},{5,1},{9,13},{13,9},{2,6},{6,2},{1... | collective-permute-start | bytes 589832 | tf_op jit(solution)/shard_map/ppermute | solution.py:26
  528.5 61.4 %collective-permute-start.81 = (bf16[2,32,1536]{2,1,0:T(8,128)(2,1)}, bf16[2,32,1536]{2,1,0:T(8,128)(2,1)S(1)}, u32[]{:S(2)}, u32[]{:S(2)}) collective-permute-start(bf16[2,32,1536]{2,1,0:T(8,128)(2,1)} %get-tuple-element.363), channel_id=1, source_target_pairs={{0,8},{4,12},{8,0},{12,4},{1,9},{5,13},{9,1},{13,5},{2,10},{6,14},... | collective-permute-start | bytes 589832 | tf_op jit(solution)/shard_map/ppermute | solution.py:26
  536.6 53.2 %collective-permute-start.82 = (bf16[2,32,1536]{2,1,0:T(8,128)(2,1)}, bf16[2,32,1536]{2,1,0:T(8,128)(2,1)S(1)}, u32[]{:S(2)}, u32[]{:S(2)}) collective-permute-start(bf16[2,32,1536]{2,1,0:T(8,128)(2,1)} %get-tuple-element.364), channel_id=1, source_target_pairs={{0,12},{4,8},{8,4},{12,0},{1,13},{5,9},{9,5},{13,1},{2,14},{6,10},... | collective-permute-start | bytes 589832 | tf_op jit(solution)/shard_map/ppermute | solution.py:26
  538.3 45.8 %collective-permute-start.84 = (bf16[256,768]{1,0:T(8,128)(2,1)}, bf16[256,768]{1,0:T(8,128)(2,1)}, u32[]{:S(2)}, u32[]{:S(2)}) collective-permute-start(bf16[256,768]{1,0:T(8,128)(2,1)} %get-tuple-element.368.refs_1_), channel_id=1, source_target_pairs={{0,16},{16,0},{1,17},{17,1},{2,18},{18,2},{3,19},{19,3},{4,20},{20... | collective-permute-start | bytes 1179656 | tf_op jit(solution)/shard_map/ppermute | solution.py:26
  538.5 42.3 %collective-permute-start.94 = (bf16[192,384]{1,0:T(8,128)(2,1)S(1)}, bf16[192,384]{1,0:T(8,128)(2,1)S(1)}, u32[]{:S(2)}, u32[]{:S(2)}) collective-permute-start(bf16[192,384]{1,0:T(8,128)(2,1)S(1)} %get-tuple-element.432), channel_id=1, source_target_pairs={{16,0},{17,1},{18,2},{19,3},{20,4},{21,5},{22,6},{23,7},{24,8},{25... | collective-permute-start | bytes 442376 | tf_op jit(solution)/shard_map/ppermute | solution.py:30
  (146 other events, 1588.6 us)
Sparse Core Ops, SparseCore 0:
  48.3 68.4 all-gather.3
  119.2 34.3 all-gather.5
  171.1 63.7 all-gather.7
  323.9 61.3 reduce-scatter.3
  402.7 33.2 reduce-scatter.5
  471.3 61.0 reduce-scatter.7

commit v3 on v2

--- a/solution.py
+++ b/solution.py
@@ -13,7 +13,7 @@
 ROPE_BASE = 100000.0
 MASKED = -1e30
 LANES = 128
-UNIT_BLOCK = 256
+UNIT_BLOCK = 512
 F32 = jnp.float32
 BF16 = jnp.bfloat16
 GROUPS = 1
@@ -279,7 +279,7 @@
 
 
 def pack_places(half, units, width):
-    hidden_at = 2 * half
+    hidden_at = -(-2 * half // UNIT_BLOCK) * UNIT_BLOCK
     mix_at = -(-(hidden_at + units) // width) * width
     return hidden_at, mix_at
 
@@ -364,6 +364,7 @@
     rows, units = gate.shape
     half = d_model // 2
     count = units // UNIT_BLOCK
+    back_at = -(-half // UNIT_BLOCK) * UNIT_BLOCK
 
     def kernel(*refs):
         xs = refs[:heads]
@@ -389,9 +390,9 @@
         d_up = (d_hidden * gate_v * sigma).astype(BF16)
         d_gate_out[...] = d_gate
         d_up_out[...] = d_up
-        at = pl.multiple_of(half + j * UNIT_BLOCK, UNIT_BLOCK)
+        at = pl.multiple_of(back_at + j * UNIT_BLOCK, UNIT_BLOCK)
         packed[:, pl.ds(at, UNIT_BLOCK)] = d_gate
-        at = pl.multiple_of(half + units + j * UNIT_BLOCK, UNIT_BLOCK)
+        at = pl.multiple_of(back_at + units + j * UNIT_BLOCK, UNIT_BLOCK)
         packed[:, pl.ds(at, UNIT_BLOCK)] = d_up
         total[:, :half] += dot_nt(d_gate, gate_w[0][...]) + dot_nt(d_up, up_w[0][...])
         total[:, half:] += dot_nt(d_gate, gate_w[1][...]) + dot_nt(d_up, up_w[1][...])
@@ -409,13 +410,13 @@
         grid=(count,),
         in_specs=[rows_spec] * heads + specs + [block, block],
         out_specs=[block, block, whole]
-        + [pl.BlockSpec((rows, half + 2 * units), lambda j: (0, 0))]
+        + [pl.BlockSpec((rows, back_at + 2 * units), lambda j: (0, 0))]
         + [rows_spec] * heads,
         out_shape=[
             kept((rows, units)),
             kept((rows, units)),
             kept((rows, d_model)),
-            kept((rows, half + 2 * units)),
+            kept((rows, back_at + 2 * units)),
             *[shape((micros, piece, d_model)) for _ in range(heads)],
         ],
         scratch_shapes=[pltpu.VMEM((rows, d_model), F32)],
@@ -620,28 +621,27 @@
     half = d_model // 2
     count = units // UNIT_BLOCK
     hidden_at, _ = pack_places(half, units, LANES)
+    back_at = -(-half // UNIT_BLOCK) * UNIT_BLOCK
 
     def kernel(*refs):
         sides = refs[:4]
         lines = refs[4:10]
         out = refs[10]
-        turned = refs[11:]
+        turned, line = refs[11:13], refs[13]
         j = pl.program_id(0)
 
         @pl.when(j == 0)
         def _():
-            for side, flat in zip(sides, turned):
-                flat[...] = side[...].T
+            for k, side in enumerate(sides):
+                turned[k % 2][:, k // 2 * rows : (k // 2 + 1) * rows] = side[...].T
 
         for part in range(3):
 
             @pl.when(j // count == part)
             def _(part=part):
-                which = (0, 0, 1)[part]
-                out[...] = (
-                    dot(turned[which][...], lines[part][...])
-                    + dot(turned[2 + which][...], lines[3 + part][...])
-                ).astype(BF16)
+                line[:rows, :] = lines[part][...]
+                line[rows:, :] = lines[3 + part][...]
+                out[...] = dot(turned[(0, 0, 1)[part]][...], line[...]).astype(BF16)
 
     def side(block):
         return pl.BlockSpec((rows, half), lambda j: (0, block))
@@ -657,16 +657,89 @@
         grid=(3 * count,),
         in_specs=[side(0), side(0), side(1), side(0)]
         + [line(part, 0) for part in range(3)]
-        + [line(0, half), line(1, half + units), line(2, hidden_at)],
+        + [line(0, back_at), line(1, back_at + units), line(2, hidden_at)],
         out_specs=pl.BlockSpec((half, UNIT_BLOCK), lambda j: (0, j)),
         out_shape=kept((half, 3 * units)),
-        scratch_shapes=[pltpu.VMEM((half, rows), BF16)] * 4,
+        scratch_shapes=[pltpu.VMEM((half, 2 * rows), BF16)] * 2
+        + [pltpu.VMEM((2 * rows, UNIT_BLOCK), BF16)],
         compiler_params=pltpu.CompilerParams(vmem_limit_bytes=VMEM_LARGE),
         cost_estimate=pl.CostEstimate(
             flops=12 * half * rows * units, bytes_accessed=6 * half * units, transcendentals=0
         ),
         name="late_grad",
     )(nb, gf, packed, packed_back, d_gate, d_up, hidden, packed_back, packed_back, packed)
+
+
+def finish_late(lower, upper, units):
+    size, _ = lower[0].shape
+    count = units // UNIT_BLOCK
+
+    def kernel(*refs):
+        parts, outs = refs[:12], refs[12:]
+        first = lax.axis_index("section") == 0
+        for which in range(3):
+            a0, a1, b0, b1 = (parts[4 * which + k][...].astype(F32) for k in range(4))
+            top, low = jnp.where(first, a0, b0), jnp.where(first, a1, b1)
+            if which < 2:
+                outs[which][:size, :] = top
+                outs[which][size:, :] = low
+            else:
+                outs[2][:, :size] = top.T
+                outs[2][:, size:] = low.T
+
+    specs, arrays = [], []
+    for which in range(3):
+        for array in (*lower, *upper):
+            specs.append(
+                pl.BlockSpec((size, UNIT_BLOCK), lambda j, which=which: (0, which * count + j))
+            )
+            arrays.append(array)
+    flat = pl.BlockSpec((2 * size, UNIT_BLOCK), lambda j: (0, j))
+    return pl.pallas_call(
+        kernel,
+        grid=(count,),
+        in_specs=specs,
+        out_specs=[flat, flat, pl.BlockSpec((UNIT_BLOCK, 2 * size), lambda j: (j, 0))],
+        out_shape=[
+            kept((2 * size, units), F32),
+            kept((2 * size, units), F32),
+            kept((units, 2 * size), F32),
+        ],
+        compiler_params=pltpu.CompilerParams(vmem_limit_bytes=VMEM_LARGE),
+        cost_estimate=pl.CostEstimate(
+            flops=0, bytes_accessed=48 * size * units, transcendentals=0
+        ),
+        name="finish_late",
+    )(*arrays)
+
+
+def finish_early(lower, lower_out, upper, k_width):
+    size, lines = lower[0].shape
+    width = lower_out[0].shape[1]
+
+    def kernel(*refs):
+        e0, e1, o0, o1, b0, b1, query, key, value, out = refs
+        first = lax.axis_index("section") == 0
+        for t, (e, o, b) in enumerate(((e0, o0, b0), (e1, o1, b1))):
+            rows = slice(t * size, (t + 1) * size)
+            both = b[...].astype(F32)
+            line = jnp.where(first, e[...].astype(F32), both[:, width:])
+            query[rows, :] = line[:, :width]
+            key[:, rows] = line[:, width : width + k_width].T
+            value[:, rows] = line[:, width + k_width :].T
+            out[:, rows] = jnp.where(first, o[...].astype(F32), both[:, :width]).T
+
+    return call(
+        kernel,
+        "finish_early",
+        [*lower, *lower_out, *upper],
+        [
+            kept((2 * size, width), F32),
+            kept((k_width, 2 * size), F32),
+            kept((k_width, 2 * size), F32),
+            kept((width, 2 * size), F32),
+        ],
+    )
 
 
 def relative_columns(value, section, ctxs):
@@ -1100,7 +1173,7 @@
         group.terms = [group.parts[0]]
         chain.plan("1B3" + group.name, "1B4" + group.name, scatter_out(group, [2, 1]))
         chain.plan("0B3" + group.name, "0B4" + group.name, scatter_out(group, range(3, heads)))
-        chain.plan("0B4" + group.name, "0B5" + group.name, finish_out(group))
+        chain.plan("0B5" + group.name, None, finish_out(group))
 
     _, mix_at = pack_places(d_model // 2, units, width)
 
@@ -1146,15 +1219,29 @@
     on_last("1B5", "0B1", lambda gate: both_1.first(both_of("1", (gate, late_1.kept))))
     on_last("0B2", "0B3", both_1.second)
     on_last("0B2", "0B3", lambda gate: late_0.first(late_of("0", (gate, both_1.kept))))
-    on_last("0B3", "0B4", lambda gate: out_0.direct(out_of("0", gate)))
-    on_last("0B4", "0B5", late_0.second)
+    early_out = []
+
+    def out_first(gate):
+        early_out.append(out_of("0", gate))
+        return early_out[0]
+
+    on_last("0B3", "0B4", out_first)
+    on_last("0B5", None, lambda gate: out_0.direct(early_out[0], gate))
+    late_done = []
+
+    def finish(gate):
+        late_done.append(finish_late(late_0.halves, late_1.halves, units))
+        return late_done[0]
+
+    on_last("0B5", None, late_0.second)
+    on_last("0B5", None, finish)
     last = []
 
     def last_grad(gate):
         last.append(early_of("0", gate))
         return last[0]
 
-    on_last("0B4", "0B5", last_grad)
+    on_last("0B5", None, last_grad)
     on_last("0B5", None, lambda gate: early_0.direct(last[0], gate))
     gain_mine = []
 
@@ -1168,12 +1255,25 @@
         gain_rows = jnp.stack(
             [gain_of(label, name) for label in "01" for name in ("gain_a", "gain_b")]
         )
-        gain_rows = stored_columns(gain_rows, section, ctxs)
-        total = lax.psum(gain_rows, ("section", "head", "ctx"))
-        two = lax.dynamic_slice_in_dim(total, section * 2, 2, axis=0)
-        gain_mine.append(
-            lax.dynamic_slice_in_dim(two, ctx * 2 * d_half, 2 * d_half, axis=1)
-        )
+        gain_rows = after(gain_rows, gate)
+        half = d_model // 2
+        got = swap(pick(first, gain_rows[2:], gain_rows[:2]), "section", 1)
+        got = jnp.concatenate([got[:, half:], got[:, :half]], axis=1)
+        blocks = (pick(first, gain_rows[:2], gain_rows[2:]) + got).reshape(4, ctxs, d_half)
+
+        def sum_over(values):
+            total = values[0]
+            for value in values[1:]:
+                total = total + value
+            return total
+
+        mine = [
+            lax.dynamic_index_in_dim(blocks, ctx ^ k, 1, keepdims=False) for k in range(ctxs)
+        ]
+        part = sum_over(send_all(mine, "ctx"))
+        part = sum_over(send_all([part] * heads, "head")).reshape(2, 2, d_half)
+        part = pick(first, part, part[:, ::-1])
+        gain_mine.append(part.reshape(2, 2 * d_half))
         return gain_mine[0]
 
     def by_layer(lower, upper):
@@ -1197,26 +1297,17 @@
         return layer_outs[0]
 
     on_last("0B5", None, out_rows)
-    on_last("0B4", None, sum_gains)
+    on_last("0B5", None, lambda gate: sum_gains((gate, early_0.kept)))
     drive(*(backward("1", group, group.cot_pieces, group.cot, views1) for group in members))
     drive(*(backward("0", group, group.pieces, group.d_in["1"], views0) for group in members))
     out_0.second()
     early_0.second()
 
-    def shard_of(lower, upper):
-        return jnp.concatenate([pick(first, a, b) for a, b in zip(lower, upper)], axis=0)
-
-    out_grad = shard_of(out_0.halves, [part[:, :width] for part in both_1.halves]).astype(F32)
-    early_grad = shard_of(early_0.halves, [part[:, width:] for part in both_1.halves]).astype(F32)
-    late = shard_of(late_0.halves, late_1.halves).astype(F32)
-    g_query = early_grad[:, :width]
-    g_key = early_grad[:, width : width + k_width]
-    g_value = early_grad[:, width + k_width :]
-    g_out = out_grad.T
-    g_gate = late[:, :units]
-    g_up = late[:, units : 2 * units]
-    g_down = late[:, 2 * units :].T
-
+    g_query, g_key, g_value, g_out = finish_early(
+        early_0.halves, out_0.halves, both_1.halves, k_width
+    )
+    g_key, g_value = g_key.T, g_value.T
+    g_gate, g_up, g_down = late_done[0]
     in_grad = by_layer(
         all_rows(lambda g: g.d_in["0"]), all_rows(lambda g: g.d_in["1"]).astype(F32)
     )

time: 639 us -> 622 us (0.973)
  blocking collectives: 39.9 us -> 0 us
  waiting for transfers between devices: 249 us -> 272 us
  starting transfers between devices: 133 us -> 140 us
    psum x1 -> x0, blocking collectives: 39.9 us -> none  [sum_gains(): total = lax.psum(gain_rows, ('section', 'head', 'ctx'))]
    ppermute x90 -> x97, waiting for transfers between devices: 248 us -> 271 us  [swap(): return lax.ppermute(value, axis, [(i, i ^ step) for i in range(count)])]
    select_n x12 -> x8, other arithmetic: 12.1 us -> 4 us  [pick(): return jnp.where(first, a, b)]
    ppermute x90 -> x97, starting transfers between devices: 125 us -> 132 us  [swap(): return lax.ppermute(value, axis, [(i, i ^ step) for i in range(count)])]
    pallas_call x2, Pallas kernels: 23.4 us -> 16.9 us  [late_grad(): pl.pallas_call(kernel, grid=(3 * count,), in_specs=[side(0), side(0), sid...]
    pallas_call x21 -> x22, Pallas kernels: 69.8 us -> 72.6 us  [call(): pl.pallas_call(kernel, grid=(1,), in_specs=specs, out_specs=out_specs, ou...]
    unnamed x194 -> x199, local copies, waits for them, and re-layouts: 27.8 us -> 27.8 us
  transfers between devices with their start and end apart: 101 -> 108, of which waited for: 48 -> 51; matrix products, arithmetic and copies ran while one was open for 5% -> 4% of each run, Pallas kernels for 15% -> 15%
where the time goes in v3:
time: 622 us; the launch traced here: 612 us
  waiting for transfers between devices  272 us (44%)
  starting transfers between devices  140 us (23%)
  Pallas kernels  130 us (21%)
  local copies, waits for them, and re-layouts  39 us (6%)
  other arithmetic  15.9 us (3%)
  between operations  15.8 us (3%)
    ppermute x97, waiting for transfers between devices, swap(): return lax.ppermute(value, axis, [(i, i ^ step) for i in range(count)])  271 us
    ppermute x97, starting transfers between devices, swap(): return lax.ppermute(value, axis, [(i, i ^ step) for i in range(count)])  132 us
    pallas_call x22, Pallas kernels, call(): pl.pallas_call(kernel, grid=(1,), in_specs=specs, out_specs=out_specs, ou...  72.6 us
    unnamed x199, local copies, waits for them, and re-layouts  27.8 us
    pallas_call x2, Pallas kernels, feed_back(): pl.pallas_call(kernel, grid=(count,), in_specs=[rows_spec] * heads + spec...  18.5 us
    pallas_call x2, Pallas kernels, feed(): pl.pallas_call(kernel, grid=(count,), in_specs=[rows_spec] * heads + spec...  17.3 us
    pallas_call x2, Pallas kernels, late_grad(): pl.pallas_call(kernel, grid=(3 * count,), in_specs=[side(0), side(0), sid...  16.9 us
  transfers between devices with their start and end apart: 108, of which 51 were waited for; matrix products, arithmetic and copies ran while one was open for 4% of the time, Pallas kernels for 15%

profile of v3, /device:TPU:0, one launch (start us, length us, event | category | flops | bytes accessed | tf_op | source)
XLA Modules:
  0.0 611.9 jit_solution(16242510475610803588)
XLA Ops:
  25.7 5.5 collective-permute-done.4.refs_1_
  34.7 5.7 collective-permute-done.5.refs_2_
  58.6 5.4 project.2
  71.7 7.1 %collective-permute-done.8.refs_2_.refs_10_ = bf16[2,128,384]{2,1,0:T(8,128)(2,1)S(1)} collective-permute-done((bf16[2,128,384]{2,1,0:T(8,128)(2,1)S(1)}, bf16[2,128,384]{2,1,0:T(8,128)(2,1)S(1)}, u32[]{:S(2)}, u32[]{:S(2)}) %collective-permute-start.8) | collective-permute-done | bytes 196640 | tf_op jit(solution)/shard_map/ppermute | solution.py:26
  83.8 6.8 %collective-permute-done.12.refs_2_ = bf16[2,32,1536]{2,1,0:T(8,128)(2,1)S(1)} collective-permute-done((bf16[2,32,1536]{2,1,0:T(8,128)(2,1)S(1)}, bf16[2,32,1536]{2,1,0:T(8,128)(2,1)S(1)}, u32[]{:S(2)}, u32[]{:S(2)}) %collective-permute-start.12) | collective-permute-done | bytes 196640 | tf_op jit(solution)/shard_map/ppermute | solution.py:26
  91.5 6.2 %attend.2 = (bf16[4,256,512]{2,1,0:T(8,128)(2,1)}, bf16[256,384]{1,0:T(8,128)(2,1)}, bf16[2,32,1536]{2,1,0:T(8,128)(2,1)}, bf16[2,32,1536]{2,1,0:T(8,128)(2,1)},...) custom-call(bf16[256,384]{1,0:T(8,128)(2,1)} %get-tuple-element.209.refs_0_.refs_8_, ...), custom_call_target="tpu_custom_call" | custom-call | flops 503316480 | bytes 4592640 | tf_op jit(solution)/shard_map/attend/pallas_call | solution.py:89
  102.1 5.4 collective-permute-done.18.refs_3_
  107.5 7.8 %collective-permute-done.19.refs_4_ = bf16[2,32,1536]{2,1,0:T(8,128)(2,1)S(1)} collective-permute-done((bf16[2,32,1536]{2,1,0:T(8,128)(2,1)}, bf16[2,32,1536]{2,1,0:T(8,128)(2,1)S(1)}, u32[]{:S(2)}, u32[]{:S(2)}) %collective-permute-start.19) | collective-permute-done | bytes 196640 | tf_op jit(solution)/shard_map/ppermute | solution.py:26
  123.9 6.9 %collective-permute-done.21.refs_1_ = bf16[2,32,1536]{2,1,0:T(8,128)(2,1)S(1)} collective-permute-done((bf16[2,32,1536]{2,1,0:T(8,128)(2,1)S(1)}, bf16[2,32,1536]{2,1,0:T(8,128)(2,1)S(1)}, u32[]{:S(2)}, u32[]{:S(2)}) %collective-permute-start.21) | collective-permute-done | bytes 196640 | tf_op jit(solution)/shard_map/ppermute | solution.py:26
  130.7 7.8 %collective-permute-done.22.refs_2_ = bf16[2,32,1536]{2,1,0:T(8,128)(2,1)S(1)} collective-permute-done((bf16[2,32,1536]{2,1,0:T(8,128)(2,1)S(1)}, bf16[2,32,1536]{2,1,0:T(8,128)(2,1)S(1)}, u32[]{:S(2)}, u32[]{:S(2)}) %collective-permute-start.22) | collective-permute-done | bytes 196640 | tf_op jit(solution)/shard_map/ppermute | solution.py:26
  139.3 8.8 %feed.2 = (bf16[256,1024]{1,0:T(8,128)(2,1)}, bf16[256,1024]{1,0:T(8,128)(2,1)}, bf16[256,1024]{1,0:T(8,128)(2,1)}, bf16[256,1536]{1,0:T(8,128)(2,1)}, bf16[256,...) custom-call(bf16[2,32,1536]{2,1,0:T(8,128)(2,1)} %copy-done.14, ...), custom_call_target="tpu_custom_call" | custom-call | flops 2415919104 | bytes 9437184 | tf_op jit(solution)/shard_map/feed/pallas_call | solution.py:335
  154.3 5.4 collective-permute-done.26.refs_2_
  159.6 9.6 %collective-permute-done.27.refs_3_ = bf16[2,32,1536]{2,1,0:T(8,128)(2,1)S(1)} collective-permute-done((bf16[2,32,1536]{2,1,0:T(8,128)(2,1)}, bf16[2,32,1536]{2,1,0:T(8,128)(2,1)S(1)}, u32[]{:S(2)}, u32[]{:S(2)}) %collective-permute-start.27) | collective-permute-done | bytes 196640 | tf_op jit(solution)/shard_map/ppermute | solution.py:26
  176.3 6.8 %collective-permute-done.29.refs_1_.refs_13_ = bf16[2,32,1536]{2,1,0:T(8,128)(2,1)S(1)} collective-permute-done((bf16[2,32,1536]{2,1,0:T(8,128)(2,1)S(1)}, bf16[2,32,1536]{2,1,0:T(8,128)(2,1)S(1)}, u32[]{:S(2)}, u32[]{:S(2)}) %collective-permute-start.29) | collective-permute-done | bytes 196640 | tf_op jit(solution)/shard_map/ppermute | solution.py:26
  183.1 7.9 %collective-permute-done.30.refs_2_.refs_14_ = bf16[2,32,1536]{2,1,0:T(8,128)(2,1)S(1)} collective-permute-done((bf16[2,32,1536]{2,1,0:T(8,128)(2,1)S(1)}, bf16[2,32,1536]{2,1,0:T(8,128)(2,1)S(1)}, u32[]{:S(2)}, u32[]{:S(2)}) %collective-permute-start.30) | collective-permute-done | bytes 196640 | tf_op jit(solution)/shard_map/ppermute | solution.py:26
  193.1 5.2 project.3
  204.2 4.9 collective-permute-done.33.refs_2_.refs_10_
  217.0 6.2 %attend.3 = (bf16[4,256,512]{2,1,0:T(8,128)(2,1)}, bf16[256,384]{1,0:T(8,128)(2,1)}, bf16[2,32,1536]{2,1,0:T(8,128)(2,1)}, bf16[2,32,1536]{2,1,0:T(8,128)(2,1)},...) custom-call(bf16[256,384]{1,0:T(8,128)(2,1)} %get-tuple-element.242.refs_0_.refs_8_, ...), custom_call_target="tpu_custom_call" | custom-call | flops 503316480 | bytes 4592640 | tf_op jit(solution)/shard_map/attend/pallas_call | solution.py:89
  223.2 6.6 %collective-permute-start.37 = (bf16[2,32,1536]{2,1,0:T(8,128)(2,1)}, bf16[2,32,1536]{2,1,0:T(8,128)(2,1)S(1)}, u32[]{:S(2)}, u32[]{:S(2)}) collective-permute-start(bf16[2,32,1536]{2,1,0:T(8,128)(2,1)} %get-tuple-element.250), channel_id=1, source_target_pairs={{0,4},{4,0},{8,12},{12,8},{1,5},{5,1},{9,13},{13,9},{2,6},{6,2},{1... | collective-permute-start | bytes 589832 | tf_op jit(solution)/shard_map/ppermute | solution.py:26
  236.2 10.3 %collective-permute-done.38.refs_4_ = bf16[2,32,1536]{2,1,0:T(8,128)(2,1)S(1)} collective-permute-done((bf16[2,32,1536]{2,1,0:T(8,128)(2,1)}, bf16[2,32,1536]{2,1,0:T(8,128)(2,1)S(1)}, u32[]{:S(2)}, u32[]{:S(2)}) %collective-permute-start.38) | collective-permute-done | bytes 196640 | tf_op jit(solution)/shard_map/ppermute | solution.py:26
  252.9 6.8 %collective-permute-done.40.refs_1_ = bf16[2,32,1536]{2,1,0:T(8,128)(2,1)S(1)} collective-permute-done((bf16[2,32,1536]{2,1,0:T(8,128)(2,1)S(1)}, bf16[2,32,1536]{2,1,0:T(8,128)(2,1)S(1)}, u32[]{:S(2)}, u32[]{:S(2)}) %collective-permute-start.40) | collective-permute-done | bytes 196640 | tf_op jit(solution)/shard_map/ppermute | solution.py:26
  259.7 7.9 %collective-permute-done.41.refs_2_ = bf16[2,32,1536]{2,1,0:T(8,128)(2,1)S(1)} collective-permute-done((bf16[2,32,1536]{2,1,0:T(8,128)(2,1)S(1)}, bf16[2,32,1536]{2,1,0:T(8,128)(2,1)S(1)}, u32[]{:S(2)}, u32[]{:S(2)}) %collective-permute-start.41) | collective-permute-done | bytes 196640 | tf_op jit(solution)/shard_map/ppermute | solution.py:26
  268.3 8.5 %feed.3 = (bf16[256,1024]{1,0:T(8,128)(2,1)}, bf16[256,1024]{1,0:T(8,128)(2,1)}, bf16[256,1024]{1,0:T(8,128)(2,1)}, bf16[256,1536]{1,0:T(8,128)(2,1)}, bf16[256,...) custom-call(bf16[2,32,1536]{2,1,0:T(8,128)(2,1)} %copy-done.15, ...), custom_call_target="tpu_custom_call" | custom-call | flops 2415919104 | bytes 9437184 | tf_op jit(solution)/shard_map/feed/pallas_call | solution.py:335
  276.9 9.6 %feed_back.2 = (bf16[256,1024]{1,0:T(8,128)(2,1)}, bf16[256,1024]{1,0:T(8,128)(2,1)}, bf16[256,1536]{1,0:T(8,128)(2,1)}, bf16[256,3072]{1,0:T(8,128)(2,1)}, bf16...) custom-call(bf16[2,32,1536]{2,1,0:T(8,128)(2,1)} %copy-done.8, ...), custom_call_target="tpu_custom_call" | custom-call | flops 2415919104 | bytes 9437184 | tf_op jit(solution)/shard_map/feed_back/pallas_call | solution.py:408
  293.0 7.0 %collective-permute-done.44.refs_4_ = bf16[2,32,1536]{2,1,0:T(8,128)(2,1)S(1)} collective-permute-done((bf16[2,32,1536]{2,1,0:T(8,128)(2,1)}, bf16[2,32,1536]{2,1,0:T(8,128)(2,1)S(1)}, u32[]{:S(2)}, u32[]{:S(2)}) %collective-permute-start.44) | collective-permute-done | bytes 196640 | tf_op jit(solution)/shard_map/ppermute | solution.py:26
  300.0 7.9 %collective-permute-done.45.refs_5_ = bf16[2,32,1536]{2,1,0:T(8,128)(2,1)S(1)} collective-permute-done((bf16[2,32,1536]{2,1,0:T(8,128)(2,1)}, bf16[2,32,1536]{2,1,0:T(8,128)(2,1)S(1)}, u32[]{:S(2)}, u32[]{:S(2)}) %collective-permute-start.45) | collective-permute-done | bytes 196640 | tf_op jit(solution)/shard_map/ppermute | solution.py:26
  310.4 8.4 %late_grad.2 = bf16[768,3072]{1,0:T(8,128)(2,1)} custom-call(bf16[256,1536]{1,0:T(8,128)(2,1)} %get-tuple-element.275.refs_0_, bf16[256,1536]{1,0:T(8,128)(2,1)} %get-tuple-element.276.refs_1_, bf16[256,3072]{1,0:T(8,128)(2,1)} %copy-done.29, bf16[256,3072]{1,0:T(8,128)(2,1)} %collective-permute-done.51.refs_3_.refs_7_.refs_8_, ...), custom_call_target="tpu_custom_call" | custom-call | flops 2415919104 | bytes 4718592 | tf_op jit(solution)/shard_map/late_grad/pallas_call | solution.py:655
  325.6 4.8 collective-permute-done.47.refs_1_
  330.4 9.9 %collective-permute-done.48.refs_2_ = bf16[2,32,1536]{2,1,0:T(8,128)(2,1)S(1)} collective-permute-done((bf16[2,32,1536]{2,1,0:T(8,128)(2,1)S(1)}, bf16[2,32,1536]{2,1,0:T(8,128)(2,1)S(1)}, u32[]{:S(2)}, u32[]{:S(2)}) %collective-permute-start.48) | collective-permute-done | bytes 196640 | tf_op jit(solution)/shard_map/ppermute | solution.py:26
  341.1 9.0 %attend_back.2 = (bf16[256,1536]{1,0:T(8,128)(2,1)}, bf16[256,768]{1,0:T(8,128)(2,1)}, bf16[256,384]{1,0:T(8,128)(2,1)}, bf16[2,128,384]{2,1,0:T(8,128)(2,1)}, b...) custom-call(bf16[2,32,1536]{2,1,0:T(8,128)(2,1)} %copy-done.25, ...), custom_call_target="tpu_custom_call" | custom-call | flops 503316480 | bytes 8912896 | tf_op jit(solution)/shard_map/attend_back/pallas_call | solution.py:89
  357.4 4.5 collective-permute-done.52.refs_2_
  365.4 5.2 project_back.2
  375.2 6.6 %collective-permute-done.57.refs_4_ = bf16[2,32,1536]{2,1,0:T(8,128)(2,1)S(1)} collective-permute-done((bf16[2,32,1536]{2,1,0:T(8,128)(2,1)}, bf16[2,32,1536]{2,1,0:T(8,128)(2,1)S(1)}, u32[]{:S(2)}, u32[]{:S(2)}) %collective-permute-start.57) | collective-permute-done | bytes 196640 | tf_op jit(solution)/shard_map/ppermute | solution.py:26
  381.8 8.1 %collective-permute-done.58.refs_5_ = bf16[2,32,1536]{2,1,0:T(8,128)(2,1)S(1)} collective-permute-done((bf16[2,32,1536]{2,1,0:T(8,128)(2,1)}, bf16[2,32,1536]{2,1,0:T(8,128)(2,1)S(1)}, u32[]{:S(2)}, u32[]{:S(2)}) %collective-permute-start.58) | collective-permute-done | bytes 196640 | tf_op jit(solution)/shard_map/ppermute | solution.py:26
  406.2 4.6 collective-permute-done.60.refs_1_
  410.8 10.0 %collective-permute-done.61.refs_2_ = bf16[2,32,1536]{2,1,0:T(8,128)(2,1)S(1)} collective-permute-done((bf16[2,32,1536]{2,1,0:T(8,128)(2,1)S(1)}, bf16[2,32,1536]{2,1,0:T(8,128)(2,1)S(1)}, u32[]{:S(2)}, u32[]{:S(2)}) %collective-permute-start.61) | collective-permute-done | bytes 196640 | tf_op jit(solution)/shard_map/ppermute | solution.py:26
  422.0 8.9 %feed_back.3 = (bf16[256,1024]{1,0:T(8,128)(2,1)}, bf16[256,1024]{1,0:T(8,128)(2,1)}, bf16[256,1536]{1,0:T(8,128)(2,1)}, bf16[256,3072]{1,0:T(8,128)(2,1)}, bf16...) custom-call(bf16[2,32,1536]{2,1,0:T(8,128)(2,1)} %copy-done.10, ...), custom_call_target="tpu_custom_call" | custom-call | flops 2415919104 | bytes 9437184 | tf_op jit(solution)/shard_map/feed_back/pallas_call | solution.py:408
  437.0 6.8 %collective-permute-done.66.refs_4_ = bf16[2,32,1536]{2,1,0:T(8,128)(2,1)S(1)} collective-permute-done((bf16[2,32,1536]{2,1,0:T(8,128)(2,1)}, bf16[2,32,1536]{2,1,0:T(8,128)(2,1)S(1)}, u32[]{:S(2)}, u32[]{:S(2)}) %collective-permute-start.66) | collective-permute-done | bytes 196640 | tf_op jit(solution)/shard_map/ppermute | solution.py:26
  443.7 8.1 %collective-permute-done.67.refs_5_ = bf16[2,32,1536]{2,1,0:T(8,128)(2,1)S(1)} collective-permute-done((bf16[2,32,1536]{2,1,0:T(8,128)(2,1)}, bf16[2,32,1536]{2,1,0:T(8,128)(2,1)S(1)}, u32[]{:S(2)}, u32[]{:S(2)}) %collective-permute-start.67) | collective-permute-done | bytes 196640 | tf_op jit(solution)/shard_map/ppermute | solution.py:26
  453.2 8.5 %late_grad.3 = bf16[768,3072]{1,0:T(8,128)(2,1)} custom-call(bf16[256,1536]{1,0:T(8,128)(2,1)} %get-tuple-element.337.refs_0_, bf16[256,1536]{1,0:T(8,128)(2,1)} %get-tuple-element.338.refs_1_, bf16[256,3072]{1,0:T(8,128)(2,1)} %collective-permute-done.73.refs_2_.refs_9_.refs_3_, bf16[256,3072]{1,0:T(8,128)(2,1)} %collective-permute-done.74.refs_3_.refs_7_.refs_8_, ...), custom_call_target="tpu_custom_call" | custom-call | flops 2415919104 | bytes 4718592 | tf_op jit(solution)/shard_map/late_grad/pallas_call | solution.py:655
  470.8 4.7 collective-permute-done.69.refs_1_
  475.5 10.0 %collective-permute-done.70.refs_2_ = bf16[2,32,1536]{2,1,0:T(8,128)(2,1)S(1)} collective-permute-done((bf16[2,32,1536]{2,1,0:T(8,128)(2,1)S(1)}, bf16[2,32,1536]{2,1,0:T(8,128)(2,1)S(1)}, u32[]{:S(2)}, u32[]{:S(2)}) %collective-permute-start.70) | collective-permute-done | bytes 196640 | tf_op jit(solution)/shard_map/ppermute | solution.py:26
  486.4 8.8 %attend_back.3 = (bf16[256,1536]{1,0:T(8,128)(2,1)}, bf16[256,768]{1,0:T(8,128)(2,1)}, bf16[256,384]{1,0:T(8,128)(2,1)}, bf16[2,128,384]{2,1,0:T(8,128)(2,1)}, b...) custom-call(bf16[2,32,1536]{2,1,0:T(8,128)(2,1)} %copy-done.16, ...), custom_call_target="tpu_custom_call" | custom-call | flops 503316480 | bytes 8912896 | tf_op jit(solution)/shard_map/attend_back/pallas_call | solution.py:89
  511.3 5.3 project_back.3
  522.9 4.7 collective-permute-done.80.refs_4_
  527.6 8.9 %collective-permute-done.81.refs_5_ = bf16[2,32,1536]{2,1,0:T(8,128)(2,1)S(1)} collective-permute-done((bf16[2,32,1536]{2,1,0:T(8,128)(2,1)}, bf16[2,32,1536]{2,1,0:T(8,128)(2,1)S(1)}, u32[]{:S(2)}, u32[]{:S(2)}) %collective-permute-start.81) | collective-permute-done | bytes 196640 | tf_op jit(solution)/shard_map/ppermute | solution.py:26
  563.0 7.2 %collective-permute-done.88 = bf16[192,768]{1,0:T(8,128)(2,1)S(1)} collective-permute-done((bf16[192,768]{1,0:T(8,128)(2,1)S(1)}, bf16[192,768]{1,0:T(8,128)(2,1)S(1)}, u32[]{:S(2)}, u32[]{:S(2)}) %collective-permute-start.88) | collective-permute-done | bytes 294944 | tf_op jit(solution)/shard_map/ppermute | solution.py:26
  570.2 6.4 %collective-permute-done.87 = bf16[192,768]{1,0:T(8,128)(2,1)S(1)} collective-permute-done((bf16[192,768]{1,0:T(8,128)(2,1)S(1)}, bf16[192,768]{1,0:T(8,128)(2,1)S(1)}, u32[]{:S(2)}, u32[]{:S(2)}) %collective-permute-start.87) | collective-permute-done | bytes 294944 | tf_op jit(solution)/shard_map/ppermute | solution.py:26
  (476 shorter events, 253.0 us)
Async XLA Ops:
  7.2 110.0 %all-gather.4.cloned.1.call-start = ((), (), s32[]{:S(2)}) async-start(), calls=%async_computation.3 | async-start | bytes 5898240 | tf_op jit(solution)/shard_map/all_gather | solution.py:808
  11.7 22.9 %collective-permute-start.1 = (bf16[2,32,1536]{2,1,0:T(8,128)(2,1)S(1)}, bf16[2,32,1536]{2,1,0:T(8,128)(2,1)}, u32[]{:S(2)}, u32[]{:S(2)}) collective-permute-start(bf16[2,32,1536]{2,1,0:T(8,128)(2,1)S(1)} %concatenate.45.refs_0_.refs_12_), channel_id=1, source_target_pairs={{0,8},{4,12},{8,0},{12,4},{1,9},{5,13},{9,1},{13,5},{2,10},{6,14},... | collective-permute-start | bytes 589832 | tf_op jit(solution)/shard_map/ppermute | solution.py:26
  14.3 20.3 %collective-permute-start.2 = (bf16[2,32,1536]{2,1,0:T(8,128)(2,1)S(1)}, bf16[2,32,1536]{2,1,0:T(8,128)(2,1)}, u32[]{:S(2)}, u32[]{:S(2)}) collective-permute-start(bf16[2,32,1536]{2,1,0:T(8,128)(2,1)S(1)} %concatenate.45.refs_0_.refs_12_), channel_id=1, source_target_pairs={{0,12},{4,8},{8,4},{12,0},{1,13},{5,9},{9,5},{13,1},{2,14},{6,10},... | collective-permute-start | bytes 589832 | tf_op jit(solution)/shard_map/ppermute | solution.py:26
  23.9 16.4 %collective-permute-start.5 = (bf16[192,896]{1,0:T(8,128)(2,1)S(1)}, bf16[192,896]{1,0:T(8,128)(2,1)}, u32[]{:S(2)}, u32[]{:S(2)}) collective-permute-start(bf16[192,896]{1,0:T(8,128)(2,1)S(1)} %get-tuple-element.204.refs_0_), channel_id=1, source_target_pairs={{0,2},{1,3},{2,0},{3,1},{4,6},{5,7},{6,4},{7,5},{8,10},{9,11},{10,... | collective-permute-start | bytes 1032200 | tf_op jit(solution)/shard_map/ppermute | solution.py:26
  49.1 121.2 %all-gather.6.cloned.1.call-start = ((), (), s32[]{:S(2)}) async-start(), calls=%async_computation.4 | async-start | bytes 2457600 | tf_op jit(solution)/shard_map/all_gather | solution.py:808
  67.2 23.5 %collective-permute-start.17 = (bf16[768,384]{1,0:T(8,128)(2,1)}, bf16[768,384]{1,0:T(8,128)(2,1)S(1)}, u32[]{:S(2)}, u32[]{:S(2)}) collective-permute-start(bf16[768,384]{1,0:T(8,128)(2,1)} %place.3.refs_8_.refs_4_), channel_id=1, source_target_pairs={{0,16},{16,0},{1,17},{17,1},{2,18},{18,2},{3,19},{19,3},{4,20},{20... | collective-permute-start | bytes 1769480 | tf_op jit(solution)/shard_map/ppermute | solution.py:26
  97.9 17.4 %collective-permute-start.19 = (bf16[2,32,1536]{2,1,0:T(8,128)(2,1)}, bf16[2,32,1536]{2,1,0:T(8,128)(2,1)S(1)}, u32[]{:S(2)}, u32[]{:S(2)}) collective-permute-start(bf16[2,32,1536]{2,1,0:T(8,128)(2,1)} %get-tuple-element.224), channel_id=1, source_target_pairs={{0,8},{4,12},{8,0},{12,4},{1,9},{5,13},{9,1},{13,5},{2,10},{6,14},... | collective-permute-start | bytes 589832 | tf_op jit(solution)/shard_map/ppermute | solution.py:26
  117.2 21.3 %collective-permute-start.25 = (bf16[768,3072]{1,0:T(8,128)(2,1)}, bf16[768,3072]{1,0:T(8,128)(2,1)}, u32[]{:S(2)}, u32[]{:S(2)}) collective-permute-start(bf16[768,3072]{1,0:T(8,128)(2,1)} %all-gather.4.cloned.1.call-done.refs_4_.refs_6_.refs_8_), channel_id=1, source_target_pairs={{0,16},{16,0},{1,17},{17,1},{2,18},{18,2},{3,19},{19,3},{4,20},{20... | collective-permute-start | bytes 14155784 | tf_op jit(solution)/shard_map/ppermute | solution.py:26
  118.1 129.6 %all-gather.8.cloned.1.call-start = ((), (), s32[]{:S(2)}) async-start(), calls=%async_computation.5 | async-start | bytes 5898240 | tf_op jit(solution)/shard_map/all_gather | solution.py:808
  121.4 17.1 %collective-permute-start.22 = (bf16[2,32,1536]{2,1,0:T(8,128)(2,1)S(1)}, bf16[2,32,1536]{2,1,0:T(8,128)(2,1)S(1)}, u32[]{:S(2)}, u32[]{:S(2)}) collective-permute-start(bf16[2,32,1536]{2,1,0:T(8,128)(2,1)S(1)} %get-tuple-element.227.refs_0_), channel_id=1, source_target_pairs={{0,8},{4,12},{8,0},{12,4},{1,9},{5,13},{9,1},{13,5},{2,10},{6,14},... | collective-permute-start | bytes 589832 | tf_op jit(solution)/shard_map/ppermute | solution.py:26
  122.5 16.1 %collective-permute-start.23 = (bf16[2,32,1536]{2,1,0:T(8,128)(2,1)S(1)}, bf16[2,32,1536]{2,1,0:T(8,128)(2,1)S(1)}, u32[]{:S(2)}, u32[]{:S(2)}) collective-permute-start(bf16[2,32,1536]{2,1,0:T(8,128)(2,1)S(1)} %get-tuple-element.227.refs_0_), channel_id=1, source_target_pairs={{0,12},{4,8},{8,4},{12,0},{1,13},{5,9},{9,5},{13,1},{2,14},{6,10},... | collective-permute-start | bytes 589832 | tf_op jit(solution)/shard_map/ppermute | solution.py:26
  151.8 17.4 %collective-permute-start.27 = (bf16[2,32,1536]{2,1,0:T(8,128)(2,1)}, bf16[2,32,1536]{2,1,0:T(8,128)(2,1)S(1)}, u32[]{:S(2)}, u32[]{:S(2)}) collective-permute-start(bf16[2,32,1536]{2,1,0:T(8,128)(2,1)} %get-tuple-element.237), channel_id=1, source_target_pairs={{0,8},{4,12},{8,0},{12,4},{1,9},{5,13},{9,1},{13,5},{2,10},{6,14},... | collective-permute-start | bytes 589832 | tf_op jit(solution)/shard_map/ppermute | solution.py:26
  152.9 16.3 %collective-permute-start.28 = (bf16[2,32,1536]{2,1,0:T(8,128)(2,1)}, bf16[2,32,1536]{2,1,0:T(8,128)(2,1)S(1)}, u32[]{:S(2)}, u32[]{:S(2)}) collective-permute-start(bf16[2,32,1536]{2,1,0:T(8,128)(2,1)} %get-tuple-element.238), channel_id=1, source_target_pairs={{0,12},{4,8},{8,4},{12,0},{1,13},{5,9},{9,5},{13,1},{2,14},{6,10},... | collective-permute-start | bytes 589832 | tf_op jit(solution)/shard_map/ppermute | solution.py:26
  170.3 221.6 %reduce-scatter.4.cloned.1.call-start = ((), (), s32[]{:S(2)}) async-start(), calls=%async_computation.6 | async-start | bytes 5898240 | tf_op jit(solution)/shard_map/reduce_scatter | solution.py:822
  170.7 20.3 %collective-permute-start.32 = (bf16[768,1280]{1,0:T(8,128)(2,1)}, bf16[768,1280]{1,0:T(8,128)(2,1)S(1)}, u32[]{:S(2)}, u32[]{:S(2)}) collective-permute-start(bf16[768,1280]{1,0:T(8,128)(2,1)} %all-gather.6.cloned.1.call-done.refs_4_.refs_6_.refs_8_.refs_5_.refs_7_), channel_id=1, source_target_pairs={{0,16},{16,0},{1,17},{17,1},{2,18},{18,2},{3,19},{19,3},{4,20},{20... | collective-permute-start | bytes 5898248 | tf_op jit(solution)/shard_map/ppermute | solution.py:26
  173.9 17.1 %collective-permute-start.30 = (bf16[2,32,1536]{2,1,0:T(8,128)(2,1)S(1)}, bf16[2,32,1536]{2,1,0:T(8,128)(2,1)S(1)}, u32[]{:S(2)}, u32[]{:S(2)}) collective-permute-start(bf16[2,32,1536]{2,1,0:T(8,128)(2,1)S(1)} %add_out.2.refs_0_.refs_12_), channel_id=1, source_target_pairs={{0,8},{4,12},{8,0},{12,4},{1,9},{5,13},{9,1},{13,5},{2,10},{6,14},... | collective-permute-start | bytes 589832 | tf_op jit(solution)/shard_map/ppermute | solution.py:26
  174.9 16.1 %collective-permute-start.31 = (bf16[2,32,1536]{2,1,0:T(8,128)(2,1)S(1)}, bf16[2,32,1536]{2,1,0:T(8,128)(2,1)S(1)}, u32[]{:S(2)}, u32[]{:S(2)}) collective-permute-start(bf16[2,32,1536]{2,1,0:T(8,128)(2,1)S(1)} %add_out.2.refs_0_.refs_12_), channel_id=1, source_target_pairs={{0,12},{4,8},{8,4},{12,0},{1,13},{5,9},{9,5},{13,1},{2,14},{6,10},... | collective-permute-start | bytes 589832 | tf_op jit(solution)/shard_map/ppermute | solution.py:26
  229.8 16.6 %collective-permute-start.38 = (bf16[2,32,1536]{2,1,0:T(8,128)(2,1)}, bf16[2,32,1536]{2,1,0:T(8,128)(2,1)S(1)}, u32[]{:S(2)}, u32[]{:S(2)}) collective-permute-start(bf16[2,32,1536]{2,1,0:T(8,128)(2,1)} %get-tuple-element.251), channel_id=1, source_target_pairs={{0,8},{4,12},{8,0},{12,4},{1,9},{5,13},{9,1},{13,5},{2,10},{6,14},... | collective-permute-start | bytes 589832 | tf_op jit(solution)/shard_map/ppermute | solution.py:26
  247.7 19.9 %collective-permute-start.43 = (bf16[768,3072]{1,0:T(8,128)(2,1)}, bf16[768,3072]{1,0:T(8,128)(2,1)}, u32[]{:S(2)}, u32[]{:S(2)}) collective-permute-start(bf16[768,3072]{1,0:T(8,128)(2,1)} %all-gather.8.cloned.1.call-done.refs_4_.refs_6_.refs_8_), channel_id=1, source_target_pairs={{0,16},{16,0},{1,17},{17,1},{2,18},{18,2},{3,19},{19,3},{4,20},{20... | collective-permute-start | bytes 14155784 | tf_op jit(solution)/shard_map/ppermute | solution.py:26
  250.5 17.1 %collective-permute-start.41 = (bf16[2,32,1536]{2,1,0:T(8,128)(2,1)S(1)}, bf16[2,32,1536]{2,1,0:T(8,128)(2,1)S(1)}, u32[]{:S(2)}, u32[]{:S(2)}) collective-permute-start(bf16[2,32,1536]{2,1,0:T(8,128)(2,1)S(1)} %get-tuple-element.254.refs_0_), channel_id=1, source_target_pairs={{0,8},{4,12},{8,0},{12,4},{1,9},{5,13},{9,1},{13,5},{2,10},{6,14},... | collective-permute-start | bytes 589832 | tf_op jit(solution)/shard_map/ppermute | solution.py:26
  251.5 16.1 %collective-permute-start.42 = (bf16[2,32,1536]{2,1,0:T(8,128)(2,1)S(1)}, bf16[2,32,1536]{2,1,0:T(8,128)(2,1)S(1)}, u32[]{:S(2)}, u32[]{:S(2)}) collective-permute-start(bf16[2,32,1536]{2,1,0:T(8,128)(2,1)S(1)} %get-tuple-element.254.refs_0_), channel_id=1, source_target_pairs={{0,12},{4,8},{8,4},{12,0},{1,13},{5,9},{9,5},{13,1},{2,14},{6,10},... | collective-permute-start | bytes 589832 | tf_op jit(solution)/shard_map/ppermute | solution.py:26
  276.8 32.4 %collective-permute-start.50 = (bf16[256,3072]{1,0:T(8,128)(2,1)}, bf16[256,3072]{1,0:T(8,128)(2,1)S(1)}, u32[]{:S(2)}, u32[]{:S(2)}) collective-permute-start(bf16[256,3072]{1,0:T(8,128)(2,1)} %get-tuple-element.273), channel_id=1, source_target_pairs={{0,16},{16,0},{1,17},{17,1},{2,18},{18,2},{3,19},{19,3},{4,20},{20... | collective-permute-start | bytes 4718600 | tf_op jit(solution)/shard_map/ppermute | solution.py:26
  286.5 22.8 %collective-permute-start.51 = (bf16[256,3072]{1,0:T(8,128)(2,1)}, bf16[256,3072]{1,0:T(8,128)(2,1)}, u32[]{:S(2)}, u32[]{:S(2)}) collective-permute-start(bf16[256,3072]{1,0:T(8,128)(2,1)} %get-tuple-element.274), channel_id=1, source_target_pairs={{0,16},{16,0},{1,17},{17,1},{2,18},{18,2},{3,19},{19,3},{4,20},{20... | collective-permute-start | bytes 4718600 | tf_op jit(solution)/shard_map/ppermute | solution.py:26
  290.5 17.3 %collective-permute-start.45 = (bf16[2,32,1536]{2,1,0:T(8,128)(2,1)}, bf16[2,32,1536]{2,1,0:T(8,128)(2,1)S(1)}, u32[]{:S(2)}, u32[]{:S(2)}) collective-permute-start(bf16[2,32,1536]{2,1,0:T(8,128)(2,1)} %get-tuple-element.265), channel_id=1, source_target_pairs={{0,8},{4,12},{8,0},{12,4},{1,9},{5,13},{9,1},{13,5},{2,10},{6,14},... | collective-permute-start | bytes 589832 | tf_op jit(solution)/shard_map/ppermute | solution.py:26
  291.6 16.3 %collective-permute-start.46 = (bf16[2,32,1536]{2,1,0:T(8,128)(2,1)}, bf16[2,32,1536]{2,1,0:T(8,128)(2,1)S(1)}, u32[]{:S(2)}, u32[]{:S(2)}) collective-permute-start(bf16[2,32,1536]{2,1,0:T(8,128)(2,1)} %get-tuple-element.266), channel_id=1, source_target_pairs={{0,12},{4,8},{8,4},{12,0},{1,13},{5,9},{9,5},{13,1},{2,14},{6,10},... | collective-permute-start | bytes 589832 | tf_op jit(solution)/shard_map/ppermute | solution.py:26
  318.8 134.4 %reduce-scatter.6.cloned.1.call-start = ((), (), s32[]{:S(2)}) async-start(), calls=%async_computation.7 | async-start | bytes 2211840 | tf_op jit(solution)/shard_map/reduce_scatter | solution.py:822
  323.1 17.2 %collective-permute-start.48 = (bf16[2,32,1536]{2,1,0:T(8,128)(2,1)S(1)}, bf16[2,32,1536]{2,1,0:T(8,128)(2,1)S(1)}, u32[]{:S(2)}, u32[]{:S(2)}) collective-permute-start(bf16[2,32,1536]{2,1,0:T(8,128)(2,1)S(1)} %get-tuple-element.282.refs_0_), channel_id=1, source_target_pairs={{0,8},{4,12},{8,0},{12,4},{1,9},{5,13},{9,1},{13,5},{2,10},{6,14},... | collective-permute-start | bytes 589832 | tf_op jit(solution)/shard_map/ppermute | solution.py:26
  324.2 16.2 %collective-permute-start.49 = (bf16[2,32,1536]{2,1,0:T(8,128)(2,1)S(1)}, bf16[2,32,1536]{2,1,0:T(8,128)(2,1)S(1)}, u32[]{:S(2)}, u32[]{:S(2)}) collective-permute-start(bf16[2,32,1536]{2,1,0:T(8,128)(2,1)S(1)} %get-tuple-element.282.refs_0_), channel_id=1, source_target_pairs={{0,12},{4,8},{8,4},{12,0},{1,13},{5,9},{9,5},{13,1},{2,14},{6,10},... | collective-permute-start | bytes 589832 | tf_op jit(solution)/shard_map/ppermute | solution.py:26
  361.9 30.0 %collective-permute-start.64 = (bf16[256,768]{1,0:T(8,128)(2,1)}, bf16[256,768]{1,0:T(8,128)(2,1)S(1)}, u32[]{:S(2)}, u32[]{:S(2)}) collective-permute-start(bf16[256,768]{1,0:T(8,128)(2,1)} %get-tuple-element.308), channel_id=1, source_target_pairs={{0,16},{16,0},{1,17},{17,1},{2,18},{18,2},{3,19},{19,3},{4,20},{20... | collective-permute-start | bytes 1179656 | tf_op jit(solution)/shard_map/ppermute | solution.py:26
  370.6 21.3 %collective-permute-start.65 = (bf16[256,768]{1,0:T(8,128)(2,1)}, bf16[256,768]{1,0:T(8,128)(2,1)S(1)}, u32[]{:S(2)}, u32[]{:S(2)}) collective-permute-start(bf16[256,768]{1,0:T(8,128)(2,1)} %get-tuple-element.315.refs_5_), channel_id=1, source_target_pairs={{0,16},{16,0},{1,17},{17,1},{2,18},{18,2},{3,19},{19,3},{4,20},{20... | collective-permute-start | bytes 1179656 | tf_op jit(solution)/shard_map/ppermute | solution.py:26
  372.5 17.3 %collective-permute-start.58 = (bf16[2,32,1536]{2,1,0:T(8,128)(2,1)}, bf16[2,32,1536]{2,1,0:T(8,128)(2,1)S(1)}, u32[]{:S(2)}, u32[]{:S(2)}) collective-permute-start(bf16[2,32,1536]{2,1,0:T(8,128)(2,1)} %get-tuple-element.303), channel_id=1, source_target_pairs={{0,8},{4,12},{8,0},{12,4},{1,9},{5,13},{9,1},{13,5},{2,10},{6,14},... | collective-permute-start | bytes 589832 | tf_op jit(solution)/shard_map/ppermute | solution.py:26
  373.7 16.1 %collective-permute-start.59 = (bf16[2,32,1536]{2,1,0:T(8,128)(2,1)}, bf16[2,32,1536]{2,1,0:T(8,128)(2,1)S(1)}, u32[]{:S(2)}, u32[]{:S(2)}) collective-permute-start(bf16[2,32,1536]{2,1,0:T(8,128)(2,1)} %get-tuple-element.304), channel_id=1, source_target_pairs={{0,12},{4,8},{8,4},{12,0},{1,13},{5,9},{9,5},{13,1},{2,14},{6,10},... | collective-permute-start | bytes 589832 | tf_op jit(solution)/shard_map/ppermute | solution.py:26
  397.1 185.5 %reduce-scatter.8.cloned.1.call-start = ((), (), s32[]{:S(2)}) async-start(), calls=%async_computation.8 | async-start | bytes 5898240 | tf_op jit(solution)/shard_map/reduce_scatter | solution.py:822
  398.4 22.5 %collective-permute-start.63 = (bf16[192,3072]{1,0:T(8,128)(2,1)S(1)}, bf16[192,3072]{1,0:T(8,128)(2,1)S(1)}, u32[]{:S(2)}, u32[]{:S(2)}) collective-permute-start(bf16[192,3072]{1,0:T(8,128)(2,1)S(1)} %copy-done.30), channel_id=1, source_target_pairs={{0,16},{1,17},{2,18},{3,19},{4,20},{5,21},{6,22},{7,23},{8,24},{9,... | collective-permute-start | bytes 3538952 | tf_op jit(solution)/shard_map/ppermute | solution.py:30
  403.8 17.1 %collective-permute-start.61 = (bf16[2,32,1536]{2,1,0:T(8,128)(2,1)S(1)}, bf16[2,32,1536]{2,1,0:T(8,128)(2,1)S(1)}, u32[]{:S(2)}, u32[]{:S(2)}) collective-permute-start(bf16[2,32,1536]{2,1,0:T(8,128)(2,1)S(1)} %get-tuple-element.318.refs_0_.refs_2_), channel_id=1, source_target_pairs={{0,8},{4,12},{8,0},{12,4},{1,9},{5,13},{9,1},{13,5},{2,10},{6,14},... | collective-permute-start | bytes 589832 | tf_op jit(solution)/shard_map/ppermute | solution.py:26
  404.4 16.5 %collective-permute-start.62 = (bf16[2,32,1536]{2,1,0:T(8,128)(2,1)S(1)}, bf16[2,32,1536]{2,1,0:T(8,128)(2,1)S(1)}, u32[]{:S(2)}, u32[]{:S(2)}) collective-permute-start(bf16[2,32,1536]{2,1,0:T(8,128)(2,1)S(1)} %get-tuple-element.318.refs_0_.refs_2_), channel_id=1, source_target_pairs={{0,12},{4,8},{8,4},{12,0},{1,13},{5,9},{9,5},{13,1},{2,14},{6,10},... | collective-permute-start | bytes 589832 | tf_op jit(solution)/shard_map/ppermute | solution.py:26
  406.2 47.0 %collective-permute-start.73 = (bf16[256,3072]{1,0:T(8,128)(2,1)}, bf16[256,3072]{1,0:T(8,128)(2,1)}, u32[]{:S(2)}, u32[]{:S(2)}) collective-permute-start(bf16[256,3072]{1,0:T(8,128)(2,1)} %get-tuple-element.335), channel_id=1, source_target_pairs={{0,16},{16,0},{1,17},{17,1},{2,18},{18,2},{3,19},{19,3},{4,20},{20... | collective-permute-start | bytes 4718600 | tf_op jit(solution)/shard_map/ppermute | solution.py:26
  430.9 22.3 %collective-permute-start.74 = (bf16[256,3072]{1,0:T(8,128)(2,1)}, bf16[256,3072]{1,0:T(8,128)(2,1)}, u32[]{:S(2)}, u32[]{:S(2)}) collective-permute-start(bf16[256,3072]{1,0:T(8,128)(2,1)} %get-tuple-element.336), channel_id=1, source_target_pairs={{0,16},{16,0},{1,17},{17,1},{2,18},{18,2},{3,19},{19,3},{4,20},{20... | collective-permute-start | bytes 4718600 | tf_op jit(solution)/shard_map/ppermute | solution.py:26
  434.5 17.3 %collective-permute-start.67 = (bf16[2,32,1536]{2,1,0:T(8,128)(2,1)}, bf16[2,32,1536]{2,1,0:T(8,128)(2,1)S(1)}, u32[]{:S(2)}, u32[]{:S(2)}) collective-permute-start(bf16[2,32,1536]{2,1,0:T(8,128)(2,1)} %get-tuple-element.326), channel_id=1, source_target_pairs={{0,8},{4,12},{8,0},{12,4},{1,9},{5,13},{9,1},{13,5},{2,10},{6,14},... | collective-permute-start | bytes 589832 | tf_op jit(solution)/shard_map/ppermute | solution.py:26
  435.1 16.8 %collective-permute-start.68 = (bf16[2,32,1536]{2,1,0:T(8,128)(2,1)}, bf16[2,32,1536]{2,1,0:T(8,128)(2,1)S(1)}, u32[]{:S(2)}, u32[]{:S(2)}) collective-permute-start(bf16[2,32,1536]{2,1,0:T(8,128)(2,1)} %get-tuple-element.327), channel_id=1, source_target_pairs={{0,12},{4,8},{8,4},{12,0},{1,13},{5,9},{9,5},{13,1},{2,14},{6,10},... | collective-permute-start | bytes 589832 | tf_op jit(solution)/shard_map/ppermute | solution.py:26
  462.8 22.7 %collective-permute-start.72 = (bf16[192,1152]{1,0:T(8,128)(2,1)S(1)}, bf16[192,1152]{1,0:T(8,128)(2,1)S(1)}, u32[]{:S(2)}, u32[]{:S(2)}) collective-permute-start(bf16[192,1152]{1,0:T(8,128)(2,1)S(1)} %copy-done.52), channel_id=1, source_target_pairs={{0,16},{1,17},{2,18},{3,19},{4,20},{5,21},{6,22},{7,23},{8,24},{9,... | collective-permute-start | bytes 1327112 | tf_op jit(solution)/shard_map/ppermute | solution.py:30
  468.3 17.1 %collective-permute-start.70 = (bf16[2,32,1536]{2,1,0:T(8,128)(2,1)S(1)}, bf16[2,32,1536]{2,1,0:T(8,128)(2,1)S(1)}, u32[]{:S(2)}, u32[]{:S(2)}) collective-permute-start(bf16[2,32,1536]{2,1,0:T(8,128)(2,1)S(1)} %get-tuple-element.344.refs_0_), channel_id=1, source_target_pairs={{0,8},{4,12},{8,0},{12,4},{1,9},{5,13},{9,1},{13,5},{2,10},{6,14},... | collective-permute-start | bytes 589832 | tf_op jit(solution)/shard_map/ppermute | solution.py:26
  468.9 16.5 %collective-permute-start.71 = (bf16[2,32,1536]{2,1,0:T(8,128)(2,1)S(1)}, bf16[2,32,1536]{2,1,0:T(8,128)(2,1)S(1)}, u32[]{:S(2)}, u32[]{:S(2)}) collective-permute-start(bf16[2,32,1536]{2,1,0:T(8,128)(2,1)S(1)} %get-tuple-element.344.refs_0_), channel_id=1, source_target_pairs={{0,12},{4,8},{8,4},{12,0},{1,13},{5,9},{9,5},{13,1},{2,14},{6,10},... | collective-permute-start | bytes 589832 | tf_op jit(solution)/shard_map/ppermute | solution.py:26
  519.2 17.3 %collective-permute-start.81 = (bf16[2,32,1536]{2,1,0:T(8,128)(2,1)}, bf16[2,32,1536]{2,1,0:T(8,128)(2,1)S(1)}, u32[]{:S(2)}, u32[]{:S(2)}) collective-permute-start(bf16[2,32,1536]{2,1,0:T(8,128)(2,1)} %get-tuple-element.368), channel_id=1, source_target_pairs={{0,8},{4,12},{8,0},{12,4},{1,9},{5,13},{9,1},{13,5},{2,10},{6,14},... | collective-permute-start | bytes 589832 | tf_op jit(solution)/shard_map/ppermute | solution.py:26
  522.2 32.1 %collective-permute-start.85 = (bf16[256,768]{1,0:T(8,128)(2,1)}, bf16[256,768]{1,0:T(8,128)(2,1)S(1)}, u32[]{:S(2)}, u32[]{:S(2)}) collective-permute-start(bf16[256,768]{1,0:T(8,128)(2,1)} %get-tuple-element.379.refs_1_), channel_id=1, source_target_pairs={{0,16},{16,0},{1,17},{17,1},{2,18},{18,2},{3,19},{19,3},{4,20},{20... | collective-permute-start | bytes 1179656 | tf_op jit(solution)/shard_map/ppermute | solution.py:26
  539.9 38.0 %collective-permute-start.83 = (bf16[2,32,1536]{2,1,0:T(8,128)(2,1)}, bf16[2,32,1536]{2,1,0:T(8,128)(2,1)}, u32[]{:S(2)}, u32[]{:S(2)}) collective-permute-start(bf16[2,32,1536]{2,1,0:T(8,128)(2,1)} %broadcast_select_fusion.7), channel_id=1, source_target_pairs={{0,16},{16,0},{1,17},{17,1},{2,18},{18,2},{3,19},{19,3},{4,20},{20... | collective-permute-start | bytes 589832 | tf_op jit(solution)/shard_map/ppermute | solution.py:26
  553.0 41.9 %collective-permute-start.100 = (bf16[192,384]{1,0:T(8,128)(2,1)S(1)}, bf16[192,384]{1,0:T(8,128)(2,1)S(1)}, u32[]{:S(2)}, u32[]{:S(2)}) collective-permute-start(bf16[192,384]{1,0:T(8,128)(2,1)S(1)} %add_convert_fusion.1.refs_2_), channel_id=1, source_target_pairs={{16,0},{17,1},{18,2},{19,3},{20,4},{21,5},{22,6},{23,7},{24,8},{25... | collective-permute-start | bytes 442376 | tf_op jit(solution)/shard_map/ppermute | solution.py:30
  582.7 16.6 %collective-permute-start.101 = (bf16[192,3072]{1,0:T(8,128)(2,1)}, bf16[192,3072]{1,0:T(8,128)(2,1)S(1)}, u32[]{:S(2)}, u32[]{:S(2)}) collective-permute-start(bf16[192,3072]{1,0:T(8,128)(2,1)} %reduce-scatter.8.cloned.1.call-done.refs_0_.refs_4_.refs_8_), channel_id=1, source_target_pairs={{16,0},{17,1},{18,2},{19,3},{20,4},{21,5},{22,6},{23,7},{24,8},{25... | collective-permute-start | bytes 3538952 | tf_op jit(solution)/shard_map/ppermute | solution.py:30
  (156 other events, 1606.1 us)
Sparse Core Ops, SparseCore 0:
  49.2 67.9 all-gather.3
  119.6 34.2 all-gather.5
  170.5 64.3 all-gather.7
  319.0 60.1 reduce-scatter.3
  397.2 32.8 reduce-scatter.5
  461.9 61.0 reduce-scatter.7

commit v4 on v3

--- a/solution.py
+++ b/solution.py
@@ -713,26 +713,25 @@
     )(*arrays)
 
 
-def finish_early(lower, lower_out, upper, k_width):
+def finish_early(lower, upper, width, k_width):
     size, lines = lower[0].shape
-    width = lower_out[0].shape[1]
 
     def kernel(*refs):
-        e0, e1, o0, o1, b0, b1, query, key, value, out = refs
+        a0, a1, b0, b1, query, key, value, out = refs
         first = lax.axis_index("section") == 0
-        for t, (e, o, b) in enumerate(((e0, o0, b0), (e1, o1, b1))):
+        for t, (a, b) in enumerate(((a0, b0), (a1, b1))):
             rows = slice(t * size, (t + 1) * size)
-            both = b[...].astype(F32)
-            line = jnp.where(first, e[...].astype(F32), both[:, width:])
+            both = jnp.where(first, a[...].astype(F32), b[...].astype(F32))
+            line = both[:, width:]
             query[rows, :] = line[:, :width]
             key[:, rows] = line[:, width : width + k_width].T
             value[:, rows] = line[:, width + k_width :].T
-            out[:, rows] = jnp.where(first, o[...].astype(F32), both[:, :width]).T
+            out[:, rows] = both[:, :width].T
 
     return call(
         kernel,
         "finish_early",
-        [*lower, *lower_out, *upper],
+        [*lower, *upper],
         [
             kept((2 * size, width), F32),
             kept((k_width, 2 * size), F32),
@@ -1112,6 +1111,7 @@
         terms = send_all(parts, "head")
         keep.d_line_other = swap(keep.d_line, "section", 1)
         leave(label + "B4", group, parts[0])
+        leave(label + "B4z", group, terms[1])
         yield
         terms = enter(label + "B5", group, terms)
         d_input, d_low, _ = norm_back(terms, keep.x, keep.gains, 0, d_mid)
@@ -1213,36 +1213,29 @@
         values = after(rows_of(label, *out_names, *early_names), gate)
         return weight_grad([out_group(*values[:4]), early_group(*values[4:])])
 
-    late_1, both_1, late_0, out_0, early_0 = (Settle(s) for s in (0, 0, 1, 1, 1))
+    late_1, both_1, late_0, both_0 = (Settle(s) for s in (0, 0, 1, 1))
     on_last("1B2", "1B3", lambda gate: late_1.first(late_of("1", gate)))
     on_last("1B5", "0B1", late_1.second)
     on_last("1B5", "0B1", lambda gate: both_1.first(both_of("1", (gate, late_1.kept))))
     on_last("0B2", "0B3", both_1.second)
     on_last("0B2", "0B3", lambda gate: late_0.first(late_of("0", (gate, both_1.kept))))
-    early_out = []
-
-    def out_first(gate):
-        early_out.append(out_of("0", gate))
-        return early_out[0]
-
-    on_last("0B3", "0B4", out_first)
-    on_last("0B5", None, lambda gate: out_0.direct(early_out[0], gate))
+    on_last("0B5", None, late_0.second)
     late_done = []
 
     def finish(gate):
         late_done.append(finish_late(late_0.halves, late_1.halves, units))
         return late_done[0]
 
-    on_last("0B5", None, late_0.second)
     on_last("0B5", None, finish)
+    on_last("0B5", None, lambda gate: both_0.second(late_done[0]))
     last = []
 
     def last_grad(gate):
-        last.append(early_of("0", gate))
+        last.append(both_0.first(both_of("0", gate)))
         return last[0]
 
-    on_last("0B5", None, last_grad)
-    on_last("0B5", None, lambda gate: early_0.direct(last[0], gate))
+    on_last("0B4z", "0B5", last_grad)
+
     gain_mine = []
 
     def sum_gains(gate):
@@ -1297,14 +1290,12 @@
         return layer_outs[0]
 
     on_last("0B5", None, out_rows)
-    on_last("0B5", None, lambda gate: sum_gains((gate, early_0.kept)))
+    on_last("0B5", None, lambda gate: sum_gains((gate, last[0])))
     drive(*(backward("1", group, group.cot_pieces, group.cot, views1) for group in members))
     drive(*(backward("0", group, group.pieces, group.d_in["1"], views0) for group in members))
-    out_0.second()
-    early_0.second()
 
     g_query, g_key, g_value, g_out = finish_early(
-        early_0.halves, out_0.halves, both_1.halves, k_width
+        both_0.halves, both_1.halves, width, k_width
     )
     g_key, g_value = g_key.T, g_value.T
     g_gate, g_up, g_down = late_done[0]

time: 622 us -> 597 us (0.960)
  waiting for transfers between devices: 272 us -> 262 us
    ppermute x97 -> x91, waiting for transfers between devices: 271 us -> 250 us  [swap(): return lax.ppermute(value, axis, [(i, i ^ step) for i in range(count)])]
    reduce_scatter x3 -> x4, waiting for transfers between devices: 0.02 us -> 8.48 us  [first(): self.kept = lax.psum_scatter(whole, 'ctx', scatter_dimension=0, tiled=True)]
    ppermute x97 -> x91, starting transfers between devices: 132 us -> 128 us  [swap(): return lax.ppermute(value, axis, [(i, i ^ step) for i in range(count)])]
    unnamed x199 -> x193, local copies, waits for them, and re-layouts: 27.8 us -> 24.8 us
    pallas_call x22 -> x21, Pallas kernels: 72.6 us -> 71.1 us  [call(): pl.pallas_call(kernel, grid=(1,), in_specs=specs, out_specs=out_specs, ou...]
  transfers between devices with their start and end apart: 108 -> 102, of which waited for: 51 -> 55; matrix products, arithmetic and copies ran while one was open for 4% -> 3% of each run, Pallas kernels for 15% -> 16%
where the time goes in v4:
time: 597 us; the launch traced here: 587 us
  waiting for transfers between devices  262 us (44%)
  starting transfers between devices  134 us (22%)
  Pallas kernels  128 us (21%)
  local copies, waits for them, and re-layouts  34 us (6%)
  between operations  15.9 us (3%)
  other arithmetic  12.3 us (2%)
    ppermute x91, waiting for transfers between devices, swap(): return lax.ppermute(value, axis, [(i, i ^ step) for i in range(count)])  250 us
    ppermute x91, starting transfers between devices, swap(): return lax.ppermute(value, axis, [(i, i ^ step) for i in range(count)])  128 us
    pallas_call x21, Pallas kernels, call(): pl.pallas_call(kernel, grid=(1,), in_specs=specs, out_specs=out_specs, ou...  71.1 us
    unnamed x193, local copies, waits for them, and re-layouts  24.8 us
    pallas_call x2, Pallas kernels, feed_back(): pl.pallas_call(kernel, grid=(count,), in_specs=[rows_spec] * heads + spec...  18.6 us
    pallas_call x2, Pallas kernels, feed(): pl.pallas_call(kernel, grid=(count,), in_specs=[rows_spec] * heads + spec...  17.3 us
    pallas_call x2, Pallas kernels, late_grad(): pl.pallas_call(kernel, grid=(3 * count,), in_specs=[side(0), side(0), sid...  16.9 us
  transfers between devices with their start and end apart: 102, of which 55 were waited for; matrix products, arithmetic and copies ran while one was open for 3% of the time, Pallas kernels for 16%

profile of v4, /device:TPU:0, one launch (start us, length us, event | category | flops | bytes accessed | tf_op | source)
XLA Modules:
  0.0 586.6 jit_solution(2038153422473987121)
XLA Ops:
  25.7 5.5 collective-permute-done.4.refs_1_
  34.7 5.7 collective-permute-done.5.refs_2_
  58.6 5.4 project.2
  71.8 7.1 %collective-permute-done.8.refs_2_.refs_10_ = bf16[2,128,384]{2,1,0:T(8,128)(2,1)S(1)} collective-permute-done((bf16[2,128,384]{2,1,0:T(8,128)(2,1)S(1)}, bf16[2,128,384]{2,1,0:T(8,128)(2,1)S(1)}, u32[]{:S(2)}, u32[]{:S(2)}) %collective-permute-start.8) | collective-permute-done | bytes 196640 | tf_op jit(solution)/shard_map/ppermute | solution.py:26
  83.9 6.8 %collective-permute-done.12.refs_2_ = bf16[2,32,1536]{2,1,0:T(8,128)(2,1)S(1)} collective-permute-done((bf16[2,32,1536]{2,1,0:T(8,128)(2,1)S(1)}, bf16[2,32,1536]{2,1,0:T(8,128)(2,1)S(1)}, u32[]{:S(2)}, u32[]{:S(2)}) %collective-permute-start.12) | collective-permute-done | bytes 196640 | tf_op jit(solution)/shard_map/ppermute | solution.py:26
  91.6 6.2 %attend.2 = (bf16[4,256,512]{2,1,0:T(8,128)(2,1)}, bf16[256,384]{1,0:T(8,128)(2,1)}, bf16[2,32,1536]{2,1,0:T(8,128)(2,1)}, bf16[2,32,1536]{2,1,0:T(8,128)(2,1)},...) custom-call(bf16[256,384]{1,0:T(8,128)(2,1)} %get-tuple-element.212.refs_0_.refs_8_, ...), custom_call_target="tpu_custom_call" | custom-call | flops 503316480 | bytes 4592640 | tf_op jit(solution)/shard_map/attend/pallas_call | solution.py:89
  102.2 5.4 collective-permute-done.18.refs_3_
  107.5 7.9 %collective-permute-done.19.refs_4_ = bf16[2,32,1536]{2,1,0:T(8,128)(2,1)S(1)} collective-permute-done((bf16[2,32,1536]{2,1,0:T(8,128)(2,1)}, bf16[2,32,1536]{2,1,0:T(8,128)(2,1)S(1)}, u32[]{:S(2)}, u32[]{:S(2)}) %collective-permute-start.19) | collective-permute-done | bytes 196640 | tf_op jit(solution)/shard_map/ppermute | solution.py:26
  124.0 6.9 %collective-permute-done.21.refs_1_ = bf16[2,32,1536]{2,1,0:T(8,128)(2,1)S(1)} collective-permute-done((bf16[2,32,1536]{2,1,0:T(8,128)(2,1)S(1)}, bf16[2,32,1536]{2,1,0:T(8,128)(2,1)S(1)}, u32[]{:S(2)}, u32[]{:S(2)}) %collective-permute-start.21) | collective-permute-done | bytes 196640 | tf_op jit(solution)/shard_map/ppermute | solution.py:26
  130.8 7.8 %collective-permute-done.22.refs_2_ = bf16[2,32,1536]{2,1,0:T(8,128)(2,1)S(1)} collective-permute-done((bf16[2,32,1536]{2,1,0:T(8,128)(2,1)S(1)}, bf16[2,32,1536]{2,1,0:T(8,128)(2,1)S(1)}, u32[]{:S(2)}, u32[]{:S(2)}) %collective-permute-start.22) | collective-permute-done | bytes 196640 | tf_op jit(solution)/shard_map/ppermute | solution.py:26
  139.4 8.8 %feed.2 = (bf16[256,1024]{1,0:T(8,128)(2,1)}, bf16[256,1024]{1,0:T(8,128)(2,1)}, bf16[256,1024]{1,0:T(8,128)(2,1)}, bf16[256,1536]{1,0:T(8,128)(2,1)}, bf16[256,...) custom-call(bf16[2,32,1536]{2,1,0:T(8,128)(2,1)} %copy-done.14, ...), custom_call_target="tpu_custom_call" | custom-call | flops 2415919104 | bytes 9437184 | tf_op jit(solution)/shard_map/feed/pallas_call | solution.py:335
  154.4 5.4 collective-permute-done.26.refs_2_
  159.8 9.6 %collective-permute-done.27.refs_3_ = bf16[2,32,1536]{2,1,0:T(8,128)(2,1)S(1)} collective-permute-done((bf16[2,32,1536]{2,1,0:T(8,128)(2,1)}, bf16[2,32,1536]{2,1,0:T(8,128)(2,1)S(1)}, u32[]{:S(2)}, u32[]{:S(2)}) %collective-permute-start.27) | collective-permute-done | bytes 196640 | tf_op jit(solution)/shard_map/ppermute | solution.py:26
  176.5 6.8 %collective-permute-done.29.refs_1_.refs_13_ = bf16[2,32,1536]{2,1,0:T(8,128)(2,1)S(1)} collective-permute-done((bf16[2,32,1536]{2,1,0:T(8,128)(2,1)S(1)}, bf16[2,32,1536]{2,1,0:T(8,128)(2,1)S(1)}, u32[]{:S(2)}, u32[]{:S(2)}) %collective-permute-start.29) | collective-permute-done | bytes 196640 | tf_op jit(solution)/shard_map/ppermute | solution.py:26
  183.2 7.9 %collective-permute-done.30.refs_2_.refs_14_ = bf16[2,32,1536]{2,1,0:T(8,128)(2,1)S(1)} collective-permute-done((bf16[2,32,1536]{2,1,0:T(8,128)(2,1)S(1)}, bf16[2,32,1536]{2,1,0:T(8,128)(2,1)S(1)}, u32[]{:S(2)}, u32[]{:S(2)}) %collective-permute-start.30) | collective-permute-done | bytes 196640 | tf_op jit(solution)/shard_map/ppermute | solution.py:26
  193.2 5.2 project.3
  204.4 4.9 collective-permute-done.33.refs_2_.refs_10_
  212.1 4.4 collective-permute-done.35.refs_4_.refs_12_
  217.1 6.2 %attend.3 = (bf16[4,256,512]{2,1,0:T(8,128)(2,1)}, bf16[256,384]{1,0:T(8,128)(2,1)}, bf16[2,32,1536]{2,1,0:T(8,128)(2,1)}, bf16[2,32,1536]{2,1,0:T(8,128)(2,1)},...) custom-call(bf16[256,384]{1,0:T(8,128)(2,1)} %get-tuple-element.245.refs_0_.refs_8_, ...), custom_call_target="tpu_custom_call" | custom-call | flops 503316480 | bytes 4592640 | tf_op jit(solution)/shard_map/attend/pallas_call | solution.py:89
  223.4 6.6 %collective-permute-start.37 = (bf16[2,32,1536]{2,1,0:T(8,128)(2,1)}, bf16[2,32,1536]{2,1,0:T(8,128)(2,1)S(1)}, u32[]{:S(2)}, u32[]{:S(2)}) collective-permute-start(bf16[2,32,1536]{2,1,0:T(8,128)(2,1)} %get-tuple-element.253), channel_id=1, source_target_pairs={{0,4},{4,0},{8,12},{12,8},{1,5},{5,1},{9,13},{13,9},{2,6},{6,2},{1... | collective-permute-start | bytes 589832 | tf_op jit(solution)/shard_map/ppermute | solution.py:26
  236.3 10.3 %collective-permute-done.38.refs_4_ = bf16[2,32,1536]{2,1,0:T(8,128)(2,1)S(1)} collective-permute-done((bf16[2,32,1536]{2,1,0:T(8,128)(2,1)}, bf16[2,32,1536]{2,1,0:T(8,128)(2,1)S(1)}, u32[]{:S(2)}, u32[]{:S(2)}) %collective-permute-start.38) | collective-permute-done | bytes 196640 | tf_op jit(solution)/shard_map/ppermute | solution.py:26
  253.0 6.8 %collective-permute-done.40.refs_1_ = bf16[2,32,1536]{2,1,0:T(8,128)(2,1)S(1)} collective-permute-done((bf16[2,32,1536]{2,1,0:T(8,128)(2,1)S(1)}, bf16[2,32,1536]{2,1,0:T(8,128)(2,1)S(1)}, u32[]{:S(2)}, u32[]{:S(2)}) %collective-permute-start.40) | collective-permute-done | bytes 196640 | tf_op jit(solution)/shard_map/ppermute | solution.py:26
  259.8 7.9 %collective-permute-done.41.refs_2_ = bf16[2,32,1536]{2,1,0:T(8,128)(2,1)S(1)} collective-permute-done((bf16[2,32,1536]{2,1,0:T(8,128)(2,1)S(1)}, bf16[2,32,1536]{2,1,0:T(8,128)(2,1)S(1)}, u32[]{:S(2)}, u32[]{:S(2)}) %collective-permute-start.41) | collective-permute-done | bytes 196640 | tf_op jit(solution)/shard_map/ppermute | solution.py:26
  268.5 8.5 %feed.3 = (bf16[256,1024]{1,0:T(8,128)(2,1)}, bf16[256,1024]{1,0:T(8,128)(2,1)}, bf16[256,1024]{1,0:T(8,128)(2,1)}, bf16[256,1536]{1,0:T(8,128)(2,1)}, bf16[256,...) custom-call(bf16[2,32,1536]{2,1,0:T(8,128)(2,1)} %copy-done.15, ...), custom_call_target="tpu_custom_call" | custom-call | flops 2415919104 | bytes 9437184 | tf_op jit(solution)/shard_map/feed/pallas_call | solution.py:335
  277.1 9.7 %feed_back.2 = (bf16[256,1024]{1,0:T(8,128)(2,1)}, bf16[256,1024]{1,0:T(8,128)(2,1)}, bf16[256,1536]{1,0:T(8,128)(2,1)}, bf16[256,3072]{1,0:T(8,128)(2,1)}, bf16...) custom-call(bf16[2,32,1536]{2,1,0:T(8,128)(2,1)} %copy-done.8, ...), custom_call_target="tpu_custom_call" | custom-call | flops 2415919104 | bytes 9437184 | tf_op jit(solution)/shard_map/feed_back/pallas_call | solution.py:408
  293.3 7.0 %collective-permute-done.44.refs_4_ = bf16[2,32,1536]{2,1,0:T(8,128)(2,1)S(1)} collective-permute-done((bf16[2,32,1536]{2,1,0:T(8,128)(2,1)}, bf16[2,32,1536]{2,1,0:T(8,128)(2,1)S(1)}, u32[]{:S(2)}, u32[]{:S(2)}) %collective-permute-start.44) | collective-permute-done | bytes 196640 | tf_op jit(solution)/shard_map/ppermute | solution.py:26
  300.3 7.9 %collective-permute-done.45.refs_5_ = bf16[2,32,1536]{2,1,0:T(8,128)(2,1)S(1)} collective-permute-done((bf16[2,32,1536]{2,1,0:T(8,128)(2,1)}, bf16[2,32,1536]{2,1,0:T(8,128)(2,1)S(1)}, u32[]{:S(2)}, u32[]{:S(2)}) %collective-permute-start.45) | collective-permute-done | bytes 196640 | tf_op jit(solution)/shard_map/ppermute | solution.py:26
  310.7 8.4 %late_grad.2 = bf16[768,3072]{1,0:T(8,128)(2,1)} custom-call(bf16[256,1536]{1,0:T(8,128)(2,1)} %get-tuple-element.278.refs_0_, bf16[256,1536]{1,0:T(8,128)(2,1)} %get-tuple-element.279.refs_1_, bf16[256,3072]{1,0:T(8,128)(2,1)} %copy-done.29, bf16[256,3072]{1,0:T(8,128)(2,1)} %collective-permute-done.51.refs_3_.refs_7_.refs_8_, ...), custom_call_target="tpu_custom_call" | custom-call | flops 2415919104 | bytes 4718592 | tf_op jit(solution)/shard_map/late_grad/pallas_call | solution.py:655
  325.8 4.8 collective-permute-done.47.refs_1_
  330.7 9.9 %collective-permute-done.48.refs_2_ = bf16[2,32,1536]{2,1,0:T(8,128)(2,1)S(1)} collective-permute-done((bf16[2,32,1536]{2,1,0:T(8,128)(2,1)S(1)}, bf16[2,32,1536]{2,1,0:T(8,128)(2,1)S(1)}, u32[]{:S(2)}, u32[]{:S(2)}) %collective-permute-start.48) | collective-permute-done | bytes 196640 | tf_op jit(solution)/shard_map/ppermute | solution.py:26
  341.3 9.0 %attend_back.2 = (bf16[256,1536]{1,0:T(8,128)(2,1)}, bf16[256,768]{1,0:T(8,128)(2,1)}, bf16[256,384]{1,0:T(8,128)(2,1)}, bf16[2,128,384]{2,1,0:T(8,128)(2,1)}, b...) custom-call(bf16[2,32,1536]{2,1,0:T(8,128)(2,1)} %copy-done.25, ...), custom_call_target="tpu_custom_call" | custom-call | flops 503316480 | bytes 8912896 | tf_op jit(solution)/shard_map/attend_back/pallas_call | solution.py:89
  357.7 4.5 collective-permute-done.52.refs_2_
  365.7 5.2 project_back.2
  375.4 6.6 %collective-permute-done.57.refs_4_ = bf16[2,32,1536]{2,1,0:T(8,128)(2,1)S(1)} collective-permute-done((bf16[2,32,1536]{2,1,0:T(8,128)(2,1)}, bf16[2,32,1536]{2,1,0:T(8,128)(2,1)S(1)}, u32[]{:S(2)}, u32[]{:S(2)}) %collective-permute-start.57) | collective-permute-done | bytes 196640 | tf_op jit(solution)/shard_map/ppermute | solution.py:26
  382.0 8.1 %collective-permute-done.58.refs_5_ = bf16[2,32,1536]{2,1,0:T(8,128)(2,1)S(1)} collective-permute-done((bf16[2,32,1536]{2,1,0:T(8,128)(2,1)}, bf16[2,32,1536]{2,1,0:T(8,128)(2,1)S(1)}, u32[]{:S(2)}, u32[]{:S(2)}) %collective-permute-start.58) | collective-permute-done | bytes 196640 | tf_op jit(solution)/shard_map/ppermute | solution.py:26
  406.5 4.6 collective-permute-done.60.refs_1_
  411.1 10.0 %collective-permute-done.61.refs_2_ = bf16[2,32,1536]{2,1,0:T(8,128)(2,1)S(1)} collective-permute-done((bf16[2,32,1536]{2,1,0:T(8,128)(2,1)S(1)}, bf16[2,32,1536]{2,1,0:T(8,128)(2,1)S(1)}, u32[]{:S(2)}, u32[]{:S(2)}) %collective-permute-start.61) | collective-permute-done | bytes 196640 | tf_op jit(solution)/shard_map/ppermute | solution.py:26
  422.2 8.9 %feed_back.3 = (bf16[256,1024]{1,0:T(8,128)(2,1)}, bf16[256,1024]{1,0:T(8,128)(2,1)}, bf16[256,1536]{1,0:T(8,128)(2,1)}, bf16[256,3072]{1,0:T(8,128)(2,1)}, bf16...) custom-call(bf16[2,32,1536]{2,1,0:T(8,128)(2,1)} %copy-done.10, ...), custom_call_target="tpu_custom_call" | custom-call | flops 2415919104 | bytes 9437184 | tf_op jit(solution)/shard_map/feed_back/pallas_call | solution.py:408
  437.3 6.8 %collective-permute-done.66.refs_4_ = bf16[2,32,1536]{2,1,0:T(8,128)(2,1)S(1)} collective-permute-done((bf16[2,32,1536]{2,1,0:T(8,128)(2,1)}, bf16[2,32,1536]{2,1,0:T(8,128)(2,1)S(1)}, u32[]{:S(2)}, u32[]{:S(2)}) %collective-permute-start.66) | collective-permute-done | bytes 196640 | tf_op jit(solution)/shard_map/ppermute | solution.py:26
  444.0 8.1 %collective-permute-done.67.refs_5_ = bf16[2,32,1536]{2,1,0:T(8,128)(2,1)S(1)} collective-permute-done((bf16[2,32,1536]{2,1,0:T(8,128)(2,1)}, bf16[2,32,1536]{2,1,0:T(8,128)(2,1)S(1)}, u32[]{:S(2)}, u32[]{:S(2)}) %collective-permute-start.67) | collective-permute-done | bytes 196640 | tf_op jit(solution)/shard_map/ppermute | solution.py:26
  453.5 8.5 %late_grad.3 = bf16[768,3072]{1,0:T(8,128)(2,1)} custom-call(bf16[256,1536]{1,0:T(8,128)(2,1)} %get-tuple-element.340.refs_0_, bf16[256,1536]{1,0:T(8,128)(2,1)} %get-tuple-element.341.refs_1_, bf16[256,3072]{1,0:T(8,128)(2,1)} %collective-permute-done.73.refs_2_.refs_9_.refs_3_.refs_6_, bf16[256,3072]{1,0:T(8,128)(2,1)} %collective-permute-done.74.refs_3_.refs_7_.refs_8_, ...), custom_call_target="tpu_custom_call" | custom-call | flops 2415919104 | bytes 4718592 | tf_op jit(solution)/shard_map/late_grad/pallas_call | solution.py:655
  471.1 4.7 collective-permute-done.69.refs_1_
  475.8 10.0 %collective-permute-done.70.refs_2_ = bf16[2,32,1536]{2,1,0:T(8,128)(2,1)S(1)} collective-permute-done((bf16[2,32,1536]{2,1,0:T(8,128)(2,1)S(1)}, bf16[2,32,1536]{2,1,0:T(8,128)(2,1)S(1)}, u32[]{:S(2)}, u32[]{:S(2)}) %collective-permute-start.70) | collective-permute-done | bytes 196640 | tf_op jit(solution)/shard_map/ppermute | solution.py:26
  486.6 8.8 %attend_back.3 = (bf16[256,1536]{1,0:T(8,128)(2,1)}, bf16[256,768]{1,0:T(8,128)(2,1)}, bf16[256,384]{1,0:T(8,128)(2,1)}, bf16[2,128,384]{2,1,0:T(8,128)(2,1)}, b...) custom-call(bf16[2,32,1536]{2,1,0:T(8,128)(2,1)} %copy-done.16, ...), custom_call_target="tpu_custom_call" | custom-call | flops 503316480 | bytes 8912896 | tf_op jit(solution)/shard_map/attend_back/pallas_call | solution.py:89
  506.6 5.2 project_back.3
  512.4 4.7 collective-permute-start.79
  520.2 6.6 %collective-permute-done.79.refs_4_ = bf16[2,32,1536]{2,1,0:T(8,128)(2,1)S(1)} collective-permute-done((bf16[2,32,1536]{2,1,0:T(8,128)(2,1)}, bf16[2,32,1536]{2,1,0:T(8,128)(2,1)S(1)}, u32[]{:S(2)}, u32[]{:S(2)}) %collective-permute-start.79) | collective-permute-done | bytes 196640 | tf_op jit(solution)/shard_map/ppermute | solution.py:26
  563.2 8.4 %reduce-scatter.9.cloned.1.call-done.refs_0_ = bf16[192,1152]{1,0:T(8,128)(2,1)} async-done(((bf16[768,1152]{1,0:T(8,128)(2,1)}), bf16[192,1152]{1,0:T(8,128)(2,1)}) %reduce-scatter.9.cloned.1.call-update) | async-done | bytes 442384 | tf_op jit(solution)/shard_map/reduce_scatter | solution.py:821
  (454 shorter events, 230.6 us)
Async XLA Ops:
  7.2 110.1 %all-gather.4.cloned.1.call-start = ((), (), s32[]{:S(2)}) async-start(), calls=%async_computation.4 | async-start | bytes 5898240 | tf_op jit(solution)/shard_map/all_gather | solution.py:807
  11.7 22.9 %collective-permute-start.1 = (bf16[2,32,1536]{2,1,0:T(8,128)(2,1)S(1)}, bf16[2,32,1536]{2,1,0:T(8,128)(2,1)}, u32[]{:S(2)}, u32[]{:S(2)}) collective-permute-start(bf16[2,32,1536]{2,1,0:T(8,128)(2,1)S(1)} %concatenate.45.refs_0_.refs_12_), channel_id=1, source_target_pairs={{0,8},{4,12},{8,0},{12,4},{1,9},{5,13},{9,1},{13,5},{2,10},{6,14},... | collective-permute-start | bytes 589832 | tf_op jit(solution)/shard_map/ppermute | solution.py:26
  14.3 20.3 %collective-permute-start.2 = (bf16[2,32,1536]{2,1,0:T(8,128)(2,1)S(1)}, bf16[2,32,1536]{2,1,0:T(8,128)(2,1)}, u32[]{:S(2)}, u32[]{:S(2)}) collective-permute-start(bf16[2,32,1536]{2,1,0:T(8,128)(2,1)S(1)} %concatenate.45.refs_0_.refs_12_), channel_id=1, source_target_pairs={{0,12},{4,8},{8,4},{12,0},{1,13},{5,9},{9,5},{13,1},{2,14},{6,10},... | collective-permute-start | bytes 589832 | tf_op jit(solution)/shard_map/ppermute | solution.py:26
  23.9 16.5 %collective-permute-start.5 = (bf16[192,896]{1,0:T(8,128)(2,1)S(1)}, bf16[192,896]{1,0:T(8,128)(2,1)}, u32[]{:S(2)}, u32[]{:S(2)}) collective-permute-start(bf16[192,896]{1,0:T(8,128)(2,1)S(1)} %get-tuple-element.207.refs_0_), channel_id=1, source_target_pairs={{0,2},{1,3},{2,0},{3,1},{4,6},{5,7},{6,4},{7,5},{8,10},{9,11},{10,... | collective-permute-start | bytes 1032200 | tf_op jit(solution)/shard_map/ppermute | solution.py:26
  49.2 121.2 %all-gather.6.cloned.1.call-start = ((), (), s32[]{:S(2)}) async-start(), calls=%async_computation.5 | async-start | bytes 2457600 | tf_op jit(solution)/shard_map/all_gather | solution.py:807
  67.2 23.5 %collective-permute-start.17 = (bf16[768,384]{1,0:T(8,128)(2,1)}, bf16[768,384]{1,0:T(8,128)(2,1)S(1)}, u32[]{:S(2)}, u32[]{:S(2)}) collective-permute-start(bf16[768,384]{1,0:T(8,128)(2,1)} %place.3.refs_8_.refs_4_), channel_id=1, source_target_pairs={{0,16},{16,0},{1,17},{17,1},{2,18},{18,2},{3,19},{19,3},{4,20},{20... | collective-permute-start | bytes 1769480 | tf_op jit(solution)/shard_map/ppermute | solution.py:26
  98.0 17.4 %collective-permute-start.19 = (bf16[2,32,1536]{2,1,0:T(8,128)(2,1)}, bf16[2,32,1536]{2,1,0:T(8,128)(2,1)S(1)}, u32[]{:S(2)}, u32[]{:S(2)}) collective-permute-start(bf16[2,32,1536]{2,1,0:T(8,128)(2,1)} %get-tuple-element.227), channel_id=1, source_target_pairs={{0,8},{4,12},{8,0},{12,4},{1,9},{5,13},{9,1},{13,5},{2,10},{6,14},... | collective-permute-start | bytes 589832 | tf_op jit(solution)/shard_map/ppermute | solution.py:26
  117.3 21.3 %collective-permute-start.25 = (bf16[768,3072]{1,0:T(8,128)(2,1)}, bf16[768,3072]{1,0:T(8,128)(2,1)}, u32[]{:S(2)}, u32[]{:S(2)}) collective-permute-start(bf16[768,3072]{1,0:T(8,128)(2,1)} %all-gather.4.cloned.1.call-done.refs_4_.refs_6_.refs_8_), channel_id=1, source_target_pairs={{0,16},{16,0},{1,17},{17,1},{2,18},{18,2},{3,19},{19,3},{4,20},{20... | collective-permute-start | bytes 14155784 | tf_op jit(solution)/shard_map/ppermute | solution.py:26
  118.1 129.6 %all-gather.8.cloned.1.call-start = ((), (), s32[]{:S(2)}) async-start(), calls=%async_computation.6 | async-start | bytes 5898240 | tf_op jit(solution)/shard_map/all_gather | solution.py:807
  121.5 17.1 %collective-permute-start.22 = (bf16[2,32,1536]{2,1,0:T(8,128)(2,1)S(1)}, bf16[2,32,1536]{2,1,0:T(8,128)(2,1)S(1)}, u32[]{:S(2)}, u32[]{:S(2)}) collective-permute-start(bf16[2,32,1536]{2,1,0:T(8,128)(2,1)S(1)} %get-tuple-element.230.refs_0_), channel_id=1, source_target_pairs={{0,8},{4,12},{8,0},{12,4},{1,9},{5,13},{9,1},{13,5},{2,10},{6,14},... | collective-permute-start | bytes 589832 | tf_op jit(solution)/shard_map/ppermute | solution.py:26
  122.6 16.1 %collective-permute-start.23 = (bf16[2,32,1536]{2,1,0:T(8,128)(2,1)S(1)}, bf16[2,32,1536]{2,1,0:T(8,128)(2,1)S(1)}, u32[]{:S(2)}, u32[]{:S(2)}) collective-permute-start(bf16[2,32,1536]{2,1,0:T(8,128)(2,1)S(1)} %get-tuple-element.230.refs_0_), channel_id=1, source_target_pairs={{0,12},{4,8},{8,4},{12,0},{1,13},{5,9},{9,5},{13,1},{2,14},{6,10},... | collective-permute-start | bytes 589832 | tf_op jit(solution)/shard_map/ppermute | solution.py:26
  151.9 17.4 %collective-permute-start.27 = (bf16[2,32,1536]{2,1,0:T(8,128)(2,1)}, bf16[2,32,1536]{2,1,0:T(8,128)(2,1)S(1)}, u32[]{:S(2)}, u32[]{:S(2)}) collective-permute-start(bf16[2,32,1536]{2,1,0:T(8,128)(2,1)} %get-tuple-element.240), channel_id=1, source_target_pairs={{0,8},{4,12},{8,0},{12,4},{1,9},{5,13},{9,1},{13,5},{2,10},{6,14},... | collective-permute-start | bytes 589832 | tf_op jit(solution)/shard_map/ppermute | solution.py:26
  153.0 16.3 %collective-permute-start.28 = (bf16[2,32,1536]{2,1,0:T(8,128)(2,1)}, bf16[2,32,1536]{2,1,0:T(8,128)(2,1)S(1)}, u32[]{:S(2)}, u32[]{:S(2)}) collective-permute-start(bf16[2,32,1536]{2,1,0:T(8,128)(2,1)} %get-tuple-element.241), channel_id=1, source_target_pairs={{0,12},{4,8},{8,4},{12,0},{1,13},{5,9},{9,5},{13,1},{2,14},{6,10},... | collective-permute-start | bytes 589832 | tf_op jit(solution)/shard_map/ppermute | solution.py:26
  170.4 221.7 %reduce-scatter.5.cloned.1.call-start = ((), (), s32[]{:S(2)}) async-start(), calls=%async_computation.7 | async-start | bytes 5898240 | tf_op jit(solution)/shard_map/reduce_scatter | solution.py:821
  170.8 20.3 %collective-permute-start.32 = (bf16[768,1280]{1,0:T(8,128)(2,1)}, bf16[768,1280]{1,0:T(8,128)(2,1)S(1)}, u32[]{:S(2)}, u32[]{:S(2)}) collective-permute-start(bf16[768,1280]{1,0:T(8,128)(2,1)} %all-gather.6.cloned.1.call-done.refs_4_.refs_6_.refs_8_.refs_5_.refs_7_), channel_id=1, source_target_pairs={{0,16},{16,0},{1,17},{17,1},{2,18},{18,2},{3,19},{19,3},{4,20},{20... | collective-permute-start | bytes 5898248 | tf_op jit(solution)/shard_map/ppermute | solution.py:26
  174.0 17.1 %collective-permute-start.30 = (bf16[2,32,1536]{2,1,0:T(8,128)(2,1)S(1)}, bf16[2,32,1536]{2,1,0:T(8,128)(2,1)S(1)}, u32[]{:S(2)}, u32[]{:S(2)}) collective-permute-start(bf16[2,32,1536]{2,1,0:T(8,128)(2,1)S(1)} %add_out.2.refs_0_.refs_12_), channel_id=1, source_target_pairs={{0,8},{4,12},{8,0},{12,4},{1,9},{5,13},{9,1},{13,5},{2,10},{6,14},... | collective-permute-start | bytes 589832 | tf_op jit(solution)/shard_map/ppermute | solution.py:26
  175.0 16.1 %collective-permute-start.31 = (bf16[2,32,1536]{2,1,0:T(8,128)(2,1)S(1)}, bf16[2,32,1536]{2,1,0:T(8,128)(2,1)S(1)}, u32[]{:S(2)}, u32[]{:S(2)}) collective-permute-start(bf16[2,32,1536]{2,1,0:T(8,128)(2,1)S(1)} %add_out.2.refs_0_.refs_12_), channel_id=1, source_target_pairs={{0,12},{4,8},{8,4},{12,0},{1,13},{5,9},{9,5},{13,1},{2,14},{6,10},... | collective-permute-start | bytes 589832 | tf_op jit(solution)/shard_map/ppermute | solution.py:26
  229.9 16.6 %collective-permute-start.38 = (bf16[2,32,1536]{2,1,0:T(8,128)(2,1)}, bf16[2,32,1536]{2,1,0:T(8,128)(2,1)S(1)}, u32[]{:S(2)}, u32[]{:S(2)}) collective-permute-start(bf16[2,32,1536]{2,1,0:T(8,128)(2,1)} %get-tuple-element.254), channel_id=1, source_target_pairs={{0,8},{4,12},{8,0},{12,4},{1,9},{5,13},{9,1},{13,5},{2,10},{6,14},... | collective-permute-start | bytes 589832 | tf_op jit(solution)/shard_map/ppermute | solution.py:26
  231.0 15.6 %collective-permute-start.39 = (bf16[2,32,1536]{2,1,0:T(8,128)(2,1)}, bf16[2,32,1536]{2,1,0:T(8,128)(2,1)S(1)}, u32[]{:S(2)}, u32[]{:S(2)}) collective-permute-start(bf16[2,32,1536]{2,1,0:T(8,128)(2,1)} %get-tuple-element.255), channel_id=1, source_target_pairs={{0,12},{4,8},{8,4},{12,0},{1,13},{5,9},{9,5},{13,1},{2,14},{6,10},... | collective-permute-start | bytes 589832 | tf_op jit(solution)/shard_map/ppermute | solution.py:26
  247.8 19.9 %collective-permute-start.43 = (bf16[768,3072]{1,0:T(8,128)(2,1)}, bf16[768,3072]{1,0:T(8,128)(2,1)}, u32[]{:S(2)}, u32[]{:S(2)}) collective-permute-start(bf16[768,3072]{1,0:T(8,128)(2,1)} %all-gather.8.cloned.1.call-done.refs_4_.refs_6_.refs_8_), channel_id=1, source_target_pairs={{0,16},{16,0},{1,17},{17,1},{2,18},{18,2},{3,19},{19,3},{4,20},{20... | collective-permute-start | bytes 14155784 | tf_op jit(solution)/shard_map/ppermute | solution.py:26
  250.6 17.1 %collective-permute-start.41 = (bf16[2,32,1536]{2,1,0:T(8,128)(2,1)S(1)}, bf16[2,32,1536]{2,1,0:T(8,128)(2,1)S(1)}, u32[]{:S(2)}, u32[]{:S(2)}) collective-permute-start(bf16[2,32,1536]{2,1,0:T(8,128)(2,1)S(1)} %get-tuple-element.257.refs_0_), channel_id=1, source_target_pairs={{0,8},{4,12},{8,0},{12,4},{1,9},{5,13},{9,1},{13,5},{2,10},{6,14},... | collective-permute-start | bytes 589832 | tf_op jit(solution)/shard_map/ppermute | solution.py:26
  251.6 16.1 %collective-permute-start.42 = (bf16[2,32,1536]{2,1,0:T(8,128)(2,1)S(1)}, bf16[2,32,1536]{2,1,0:T(8,128)(2,1)S(1)}, u32[]{:S(2)}, u32[]{:S(2)}) collective-permute-start(bf16[2,32,1536]{2,1,0:T(8,128)(2,1)S(1)} %get-tuple-element.257.refs_0_), channel_id=1, source_target_pairs={{0,12},{4,8},{8,4},{12,0},{1,13},{5,9},{9,5},{13,1},{2,14},{6,10},... | collective-permute-start | bytes 589832 | tf_op jit(solution)/shard_map/ppermute | solution.py:26
  277.0 32.5 %collective-permute-start.50 = (bf16[256,3072]{1,0:T(8,128)(2,1)}, bf16[256,3072]{1,0:T(8,128)(2,1)S(1)}, u32[]{:S(2)}, u32[]{:S(2)}) collective-permute-start(bf16[256,3072]{1,0:T(8,128)(2,1)} %get-tuple-element.276), channel_id=1, source_target_pairs={{0,16},{16,0},{1,17},{17,1},{2,18},{18,2},{3,19},{19,3},{4,20},{20... | collective-permute-start | bytes 4718600 | tf_op jit(solution)/shard_map/ppermute | solution.py:26
  286.8 22.8 %collective-permute-start.51 = (bf16[256,3072]{1,0:T(8,128)(2,1)}, bf16[256,3072]{1,0:T(8,128)(2,1)}, u32[]{:S(2)}, u32[]{:S(2)}) collective-permute-start(bf16[256,3072]{1,0:T(8,128)(2,1)} %get-tuple-element.277), channel_id=1, source_target_pairs={{0,16},{16,0},{1,17},{17,1},{2,18},{18,2},{3,19},{19,3},{4,20},{20... | collective-permute-start | bytes 4718600 | tf_op jit(solution)/shard_map/ppermute | solution.py:26
  290.8 17.3 %collective-permute-start.45 = (bf16[2,32,1536]{2,1,0:T(8,128)(2,1)}, bf16[2,32,1536]{2,1,0:T(8,128)(2,1)S(1)}, u32[]{:S(2)}, u32[]{:S(2)}) collective-permute-start(bf16[2,32,1536]{2,1,0:T(8,128)(2,1)} %get-tuple-element.268), channel_id=1, source_target_pairs={{0,8},{4,12},{8,0},{12,4},{1,9},{5,13},{9,1},{13,5},{2,10},{6,14},... | collective-permute-start | bytes 589832 | tf_op jit(solution)/shard_map/ppermute | solution.py:26
  291.8 16.3 %collective-permute-start.46 = (bf16[2,32,1536]{2,1,0:T(8,128)(2,1)}, bf16[2,32,1536]{2,1,0:T(8,128)(2,1)S(1)}, u32[]{:S(2)}, u32[]{:S(2)}) collective-permute-start(bf16[2,32,1536]{2,1,0:T(8,128)(2,1)} %get-tuple-element.269), channel_id=1, source_target_pairs={{0,12},{4,8},{8,4},{12,0},{1,13},{5,9},{9,5},{13,1},{2,14},{6,10},... | collective-permute-start | bytes 589832 | tf_op jit(solution)/shard_map/ppermute | solution.py:26
  319.1 134.4 %reduce-scatter.7.cloned.1.call-start = ((), (), s32[]{:S(2)}) async-start(), calls=%async_computation.8 | async-start | bytes 2211840 | tf_op jit(solution)/shard_map/reduce_scatter | solution.py:821
  323.4 17.2 %collective-permute-start.48 = (bf16[2,32,1536]{2,1,0:T(8,128)(2,1)S(1)}, bf16[2,32,1536]{2,1,0:T(8,128)(2,1)S(1)}, u32[]{:S(2)}, u32[]{:S(2)}) collective-permute-start(bf16[2,32,1536]{2,1,0:T(8,128)(2,1)S(1)} %get-tuple-element.285.refs_0_), channel_id=1, source_target_pairs={{0,8},{4,12},{8,0},{12,4},{1,9},{5,13},{9,1},{13,5},{2,10},{6,14},... | collective-permute-start | bytes 589832 | tf_op jit(solution)/shard_map/ppermute | solution.py:26
  324.4 16.2 %collective-permute-start.49 = (bf16[2,32,1536]{2,1,0:T(8,128)(2,1)S(1)}, bf16[2,32,1536]{2,1,0:T(8,128)(2,1)S(1)}, u32[]{:S(2)}, u32[]{:S(2)}) collective-permute-start(bf16[2,32,1536]{2,1,0:T(8,128)(2,1)S(1)} %get-tuple-element.285.refs_0_), channel_id=1, source_target_pairs={{0,12},{4,8},{8,4},{12,0},{1,13},{5,9},{9,5},{13,1},{2,14},{6,10},... | collective-permute-start | bytes 589832 | tf_op jit(solution)/shard_map/ppermute | solution.py:26
  362.2 30.0 %collective-permute-start.64 = (bf16[256,768]{1,0:T(8,128)(2,1)}, bf16[256,768]{1,0:T(8,128)(2,1)S(1)}, u32[]{:S(2)}, u32[]{:S(2)}) collective-permute-start(bf16[256,768]{1,0:T(8,128)(2,1)} %get-tuple-element.311), channel_id=1, source_target_pairs={{0,16},{16,0},{1,17},{17,1},{2,18},{18,2},{3,19},{19,3},{4,20},{20... | collective-permute-start | bytes 1179656 | tf_op jit(solution)/shard_map/ppermute | solution.py:26
  370.9 21.3 %collective-permute-start.65 = (bf16[256,768]{1,0:T(8,128)(2,1)}, bf16[256,768]{1,0:T(8,128)(2,1)S(1)}, u32[]{:S(2)}, u32[]{:S(2)}) collective-permute-start(bf16[256,768]{1,0:T(8,128)(2,1)} %get-tuple-element.318.refs_5_), channel_id=1, source_target_pairs={{0,16},{16,0},{1,17},{17,1},{2,18},{18,2},{3,19},{19,3},{4,20},{20... | collective-permute-start | bytes 1179656 | tf_op jit(solution)/shard_map/ppermute | solution.py:26
  372.7 17.3 %collective-permute-start.58 = (bf16[2,32,1536]{2,1,0:T(8,128)(2,1)}, bf16[2,32,1536]{2,1,0:T(8,128)(2,1)S(1)}, u32[]{:S(2)}, u32[]{:S(2)}) collective-permute-start(bf16[2,32,1536]{2,1,0:T(8,128)(2,1)} %get-tuple-element.306), channel_id=1, source_target_pairs={{0,8},{4,12},{8,0},{12,4},{1,9},{5,13},{9,1},{13,5},{2,10},{6,14},... | collective-permute-start | bytes 589832 | tf_op jit(solution)/shard_map/ppermute | solution.py:26
  374.0 16.1 %collective-permute-start.59 = (bf16[2,32,1536]{2,1,0:T(8,128)(2,1)}, bf16[2,32,1536]{2,1,0:T(8,128)(2,1)S(1)}, u32[]{:S(2)}, u32[]{:S(2)}) collective-permute-start(bf16[2,32,1536]{2,1,0:T(8,128)(2,1)} %get-tuple-element.307), channel_id=1, source_target_pairs={{0,12},{4,8},{8,4},{12,0},{1,13},{5,9},{9,5},{13,1},{2,14},{6,10},... | collective-permute-start | bytes 589832 | tf_op jit(solution)/shard_map/ppermute | solution.py:26
  397.4 155.4 %reduce-scatter.11.cloned.1.call-start = ((), (), s32[]{:S(2)}) async-start(), calls=%async_computation.10 | async-start | bytes 5898240 | tf_op jit(solution)/shard_map/reduce_scatter | solution.py:821
  398.6 22.5 %collective-permute-start.63 = (bf16[192,3072]{1,0:T(8,128)(2,1)S(1)}, bf16[192,3072]{1,0:T(8,128)(2,1)S(1)}, u32[]{:S(2)}, u32[]{:S(2)}) collective-permute-start(bf16[192,3072]{1,0:T(8,128)(2,1)S(1)} %copy-done.30), channel_id=1, source_target_pairs={{0,16},{1,17},{2,18},{3,19},{4,20},{5,21},{6,22},{7,23},{8,24},{9,... | collective-permute-start | bytes 3538952 | tf_op jit(solution)/shard_map/ppermute | solution.py:30
  404.0 17.0 %collective-permute-start.61 = (bf16[2,32,1536]{2,1,0:T(8,128)(2,1)S(1)}, bf16[2,32,1536]{2,1,0:T(8,128)(2,1)S(1)}, u32[]{:S(2)}, u32[]{:S(2)}) collective-permute-start(bf16[2,32,1536]{2,1,0:T(8,128)(2,1)S(1)} %get-tuple-element.321.refs_0_.refs_2_), channel_id=1, source_target_pairs={{0,8},{4,12},{8,0},{12,4},{1,9},{5,13},{9,1},{13,5},{2,10},{6,14},... | collective-permute-start | bytes 589832 | tf_op jit(solution)/shard_map/ppermute | solution.py:26
  404.6 16.5 %collective-permute-start.62 = (bf16[2,32,1536]{2,1,0:T(8,128)(2,1)S(1)}, bf16[2,32,1536]{2,1,0:T(8,128)(2,1)S(1)}, u32[]{:S(2)}, u32[]{:S(2)}) collective-permute-start(bf16[2,32,1536]{2,1,0:T(8,128)(2,1)S(1)} %get-tuple-element.321.refs_0_.refs_2_), channel_id=1, source_target_pairs={{0,12},{4,8},{8,4},{12,0},{1,13},{5,9},{9,5},{13,1},{2,14},{6,10},... | collective-permute-start | bytes 589832 | tf_op jit(solution)/shard_map/ppermute | solution.py:26
  406.5 47.0 %collective-permute-start.73 = (bf16[256,3072]{1,0:T(8,128)(2,1)}, bf16[256,3072]{1,0:T(8,128)(2,1)}, u32[]{:S(2)}, u32[]{:S(2)}) collective-permute-start(bf16[256,3072]{1,0:T(8,128)(2,1)} %get-tuple-element.338), channel_id=1, source_target_pairs={{0,16},{16,0},{1,17},{17,1},{2,18},{18,2},{3,19},{19,3},{4,20},{20... | collective-permute-start | bytes 4718600 | tf_op jit(solution)/shard_map/ppermute | solution.py:26
  431.2 22.3 %collective-permute-start.74 = (bf16[256,3072]{1,0:T(8,128)(2,1)}, bf16[256,3072]{1,0:T(8,128)(2,1)}, u32[]{:S(2)}, u32[]{:S(2)}) collective-permute-start(bf16[256,3072]{1,0:T(8,128)(2,1)} %get-tuple-element.339), channel_id=1, source_target_pairs={{0,16},{16,0},{1,17},{17,1},{2,18},{18,2},{3,19},{19,3},{4,20},{20... | collective-permute-start | bytes 4718600 | tf_op jit(solution)/shard_map/ppermute | solution.py:26
  434.8 17.3 %collective-permute-start.67 = (bf16[2,32,1536]{2,1,0:T(8,128)(2,1)}, bf16[2,32,1536]{2,1,0:T(8,128)(2,1)S(1)}, u32[]{:S(2)}, u32[]{:S(2)}) collective-permute-start(bf16[2,32,1536]{2,1,0:T(8,128)(2,1)} %get-tuple-element.329), channel_id=1, source_target_pairs={{0,8},{4,12},{8,0},{12,4},{1,9},{5,13},{9,1},{13,5},{2,10},{6,14},... | collective-permute-start | bytes 589832 | tf_op jit(solution)/shard_map/ppermute | solution.py:26
  435.4 16.8 %collective-permute-start.68 = (bf16[2,32,1536]{2,1,0:T(8,128)(2,1)}, bf16[2,32,1536]{2,1,0:T(8,128)(2,1)S(1)}, u32[]{:S(2)}, u32[]{:S(2)}) collective-permute-start(bf16[2,32,1536]{2,1,0:T(8,128)(2,1)} %get-tuple-element.330), channel_id=1, source_target_pairs={{0,12},{4,8},{8,4},{12,0},{1,13},{5,9},{9,5},{13,1},{2,14},{6,10},... | collective-permute-start | bytes 589832 | tf_op jit(solution)/shard_map/ppermute | solution.py:26
  462.1 109.5 %reduce-scatter.9.cloned.1.call-start = ((), (), s32[]{:S(2)}) async-start(), calls=%async_computation.9 | async-start | bytes 2211840 | tf_op jit(solution)/shard_map/reduce_scatter | solution.py:821
  463.0 22.7 %collective-permute-start.72 = (bf16[192,1152]{1,0:T(8,128)(2,1)S(1)}, bf16[192,1152]{1,0:T(8,128)(2,1)S(1)}, u32[]{:S(2)}, u32[]{:S(2)}) collective-permute-start(bf16[192,1152]{1,0:T(8,128)(2,1)S(1)} %copy-done.49), channel_id=1, source_target_pairs={{0,16},{1,17},{2,18},{3,19},{4,20},{5,21},{6,22},{7,23},{8,24},{9,... | collective-permute-start | bytes 1327112 | tf_op jit(solution)/shard_map/ppermute | solution.py:30
  468.6 17.1 %collective-permute-start.70 = (bf16[2,32,1536]{2,1,0:T(8,128)(2,1)S(1)}, bf16[2,32,1536]{2,1,0:T(8,128)(2,1)S(1)}, u32[]{:S(2)}, u32[]{:S(2)}) collective-permute-start(bf16[2,32,1536]{2,1,0:T(8,128)(2,1)S(1)} %get-tuple-element.347.refs_0_), channel_id=1, source_target_pairs={{0,8},{4,12},{8,0},{12,4},{1,9},{5,13},{9,1},{13,5},{2,10},{6,14},... | collective-permute-start | bytes 589832 | tf_op jit(solution)/shard_map/ppermute | solution.py:26
  469.2 16.5 %collective-permute-start.71 = (bf16[2,32,1536]{2,1,0:T(8,128)(2,1)S(1)}, bf16[2,32,1536]{2,1,0:T(8,128)(2,1)S(1)}, u32[]{:S(2)}, u32[]{:S(2)}) collective-permute-start(bf16[2,32,1536]{2,1,0:T(8,128)(2,1)S(1)} %get-tuple-element.347.refs_0_), channel_id=1, source_target_pairs={{0,12},{4,8},{8,4},{12,0},{1,13},{5,9},{9,5},{13,1},{2,14},{6,10},... | collective-permute-start | bytes 589832 | tf_op jit(solution)/shard_map/ppermute | solution.py:26
  500.9 19.2 %collective-permute-start.82 = (bf16[256,768]{1,0:T(8,128)(2,1)}, bf16[256,768]{1,0:T(8,128)(2,1)S(1)}, u32[]{:S(2)}, u32[]{:S(2)}) collective-permute-start(bf16[256,768]{1,0:T(8,128)(2,1)} %get-tuple-element.368), channel_id=1, source_target_pairs={{0,16},{16,0},{1,17},{17,1},{2,18},{18,2},{3,19},{19,3},{4,20},{20... | collective-permute-start | bytes 1179656 | tf_op jit(solution)/shard_map/ppermute | solution.py:26
  517.1 17.3 %collective-permute-start.80 = (bf16[2,32,1536]{2,1,0:T(8,128)(2,1)}, bf16[2,32,1536]{2,1,0:T(8,128)(2,1)S(1)}, u32[]{:S(2)}, u32[]{:S(2)}) collective-permute-start(bf16[2,32,1536]{2,1,0:T(8,128)(2,1)} %get-tuple-element.365), channel_id=1, source_target_pairs={{0,8},{4,12},{8,0},{12,4},{1,9},{5,13},{9,1},{13,5},{2,10},{6,14},... | collective-permute-start | bytes 589832 | tf_op jit(solution)/shard_map/ppermute | solution.py:26
  518.6 15.8 %collective-permute-start.81 = (bf16[2,32,1536]{2,1,0:T(8,128)(2,1)}, bf16[2,32,1536]{2,1,0:T(8,128)(2,1)S(1)}, u32[]{:S(2)}, u32[]{:S(2)}) collective-permute-start(bf16[2,32,1536]{2,1,0:T(8,128)(2,1)} %get-tuple-element.366), channel_id=1, source_target_pairs={{0,12},{4,8},{8,4},{12,0},{1,13},{5,9},{9,5},{13,1},{2,14},{6,10},... | collective-permute-start | bytes 589832 | tf_op jit(solution)/shard_map/ppermute | solution.py:26
  (147 other events, 1497.5 us)
Sparse Core Ops, SparseCore 0:
  49.3 67.9 all-gather.3
  119.7 34.2 all-gather.5
  170.6 64.3 all-gather.7
  319.2 60.1 reduce-scatter.4
  397.5 32.8 reduce-scatter.6
  462.2 58.0 reduce-scatter.10
  536.1 35.3 reduce-scatter.8

commit v5 on v4

--- a/solution.py
+++ b/solution.py
@@ -1234,7 +1234,7 @@
         last.append(both_0.first(both_of("0", gate)))
         return last[0]
 
-    on_last("0B4z", "0B5", last_grad)
+    on_last("0B4", "0B5", last_grad)
 
     gain_mine = []
 

time: 597 us -> 597 us (level)
  no operation moved by 1% of the time
where the time goes in v5:
time: 597 us; the launch traced here: 587 us
  waiting for transfers between devices  261 us (44%)
  starting transfers between devices  134 us (22%)
  Pallas kernels  128 us (21%)
  local copies, waits for them, and re-layouts  34.7 us (6%)
  between operations  15.9 us (3%)
  other arithmetic  12.3 us (2%)
    ppermute x91, waiting for transfers between devices, swap(): return lax.ppermute(value, axis, [(i, i ^ step) for i in range(count)])  249 us
    ppermute x91, starting transfers between devices, swap(): return lax.ppermute(value, axis, [(i, i ^ step) for i in range(count)])  128 us
    pallas_call x21, Pallas kernels, call(): pl.pallas_call(kernel, grid=(1,), in_specs=specs, out_specs=out_specs, ou...  71.1 us
    unnamed x193, local copies, waits for them, and re-layouts  25.5 us
    pallas_call x2, Pallas kernels, feed_back(): pl.pallas_call(kernel, grid=(count,), in_specs=[rows_spec] * heads + spec...  18.6 us
    pallas_call x2, Pallas kernels, feed(): pl.pallas_call(kernel, grid=(count,), in_specs=[rows_spec] * heads + spec...  17.3 us
    pallas_call x2, Pallas kernels, late_grad(): pl.pallas_call(kernel, grid=(3 * count,), in_specs=[side(0), side(0), sid...  16.9 us
  transfers between devices with their start and end apart: 102, of which 55 were waited for; matrix products, arithmetic and copies ran while one was open for 3% of the time, Pallas kernels for 16%

profile of v5, /device:TPU:0, one launch (start us, length us, event | category | flops | bytes accessed | tf_op | source)
XLA Modules:
  0.0 586.6 jit_solution(14528898369936772257)
XLA Ops:
  25.7 5.5 collective-permute-done.4.refs_1_
  34.7 5.7 collective-permute-done.5.refs_2_
  58.6 5.4 project.2
  71.8 7.1 %collective-permute-done.8.refs_2_.refs_10_ = bf16[2,128,384]{2,1,0:T(8,128)(2,1)S(1)} collective-permute-done((bf16[2,128,384]{2,1,0:T(8,128)(2,1)S(1)}, bf16[2,128,384]{2,1,0:T(8,128)(2,1)S(1)}, u32[]{:S(2)}, u32[]{:S(2)}) %collective-permute-start.8) | collective-permute-done | bytes 196640 | tf_op jit(solution)/shard_map/ppermute | solution.py:26
  83.9 6.8 %collective-permute-done.12.refs_2_ = bf16[2,32,1536]{2,1,0:T(8,128)(2,1)S(1)} collective-permute-done((bf16[2,32,1536]{2,1,0:T(8,128)(2,1)S(1)}, bf16[2,32,1536]{2,1,0:T(8,128)(2,1)S(1)}, u32[]{:S(2)}, u32[]{:S(2)}) %collective-permute-start.12) | collective-permute-done | bytes 196640 | tf_op jit(solution)/shard_map/ppermute | solution.py:26
  91.6 6.2 %attend.2 = (bf16[4,256,512]{2,1,0:T(8,128)(2,1)}, bf16[256,384]{1,0:T(8,128)(2,1)}, bf16[2,32,1536]{2,1,0:T(8,128)(2,1)}, bf16[2,32,1536]{2,1,0:T(8,128)(2,1)},...) custom-call(bf16[256,384]{1,0:T(8,128)(2,1)} %get-tuple-element.212.refs_0_.refs_8_, ...), custom_call_target="tpu_custom_call" | custom-call | flops 503316480 | bytes 4592640 | tf_op jit(solution)/shard_map/attend/pallas_call | solution.py:89
  102.2 5.4 collective-permute-done.18.refs_3_
  107.5 7.9 %collective-permute-done.19.refs_4_ = bf16[2,32,1536]{2,1,0:T(8,128)(2,1)S(1)} collective-permute-done((bf16[2,32,1536]{2,1,0:T(8,128)(2,1)}, bf16[2,32,1536]{2,1,0:T(8,128)(2,1)S(1)}, u32[]{:S(2)}, u32[]{:S(2)}) %collective-permute-start.19) | collective-permute-done | bytes 196640 | tf_op jit(solution)/shard_map/ppermute | solution.py:26
  124.0 6.9 %collective-permute-done.21.refs_1_ = bf16[2,32,1536]{2,1,0:T(8,128)(2,1)S(1)} collective-permute-done((bf16[2,32,1536]{2,1,0:T(8,128)(2,1)S(1)}, bf16[2,32,1536]{2,1,0:T(8,128)(2,1)S(1)}, u32[]{:S(2)}, u32[]{:S(2)}) %collective-permute-start.21) | collective-permute-done | bytes 196640 | tf_op jit(solution)/shard_map/ppermute | solution.py:26
  130.8 7.8 %collective-permute-done.22.refs_2_ = bf16[2,32,1536]{2,1,0:T(8,128)(2,1)S(1)} collective-permute-done((bf16[2,32,1536]{2,1,0:T(8,128)(2,1)S(1)}, bf16[2,32,1536]{2,1,0:T(8,128)(2,1)S(1)}, u32[]{:S(2)}, u32[]{:S(2)}) %collective-permute-start.22) | collective-permute-done | bytes 196640 | tf_op jit(solution)/shard_map/ppermute | solution.py:26
  139.4 8.8 %feed.2 = (bf16[256,1024]{1,0:T(8,128)(2,1)}, bf16[256,1024]{1,0:T(8,128)(2,1)}, bf16[256,1024]{1,0:T(8,128)(2,1)}, bf16[256,1536]{1,0:T(8,128)(2,1)}, bf16[256,...) custom-call(bf16[2,32,1536]{2,1,0:T(8,128)(2,1)} %copy-done.14, ...), custom_call_target="tpu_custom_call" | custom-call | flops 2415919104 | bytes 9437184 | tf_op jit(solution)/shard_map/feed/pallas_call | solution.py:335
  154.4 5.4 collective-permute-done.26.refs_2_
  159.8 9.6 %collective-permute-done.27.refs_3_ = bf16[2,32,1536]{2,1,0:T(8,128)(2,1)S(1)} collective-permute-done((bf16[2,32,1536]{2,1,0:T(8,128)(2,1)}, bf16[2,32,1536]{2,1,0:T(8,128)(2,1)S(1)}, u32[]{:S(2)}, u32[]{:S(2)}) %collective-permute-start.27) | collective-permute-done | bytes 196640 | tf_op jit(solution)/shard_map/ppermute | solution.py:26
  176.5 6.8 %collective-permute-done.29.refs_1_.refs_13_ = bf16[2,32,1536]{2,1,0:T(8,128)(2,1)S(1)} collective-permute-done((bf16[2,32,1536]{2,1,0:T(8,128)(2,1)S(1)}, bf16[2,32,1536]{2,1,0:T(8,128)(2,1)S(1)}, u32[]{:S(2)}, u32[]{:S(2)}) %collective-permute-start.29) | collective-permute-done | bytes 196640 | tf_op jit(solution)/shard_map/ppermute | solution.py:26
  183.2 7.9 %collective-permute-done.30.refs_2_.refs_14_ = bf16[2,32,1536]{2,1,0:T(8,128)(2,1)S(1)} collective-permute-done((bf16[2,32,1536]{2,1,0:T(8,128)(2,1)S(1)}, bf16[2,32,1536]{2,1,0:T(8,128)(2,1)S(1)}, u32[]{:S(2)}, u32[]{:S(2)}) %collective-permute-start.30) | collective-permute-done | bytes 196640 | tf_op jit(solution)/shard_map/ppermute | solution.py:26
  193.2 5.2 project.3
  204.4 4.9 collective-permute-done.33.refs_2_.refs_10_
  212.1 4.4 collective-permute-done.35.refs_4_.refs_12_
  217.1 6.2 %attend.3 = (bf16[4,256,512]{2,1,0:T(8,128)(2,1)}, bf16[256,384]{1,0:T(8,128)(2,1)}, bf16[2,32,1536]{2,1,0:T(8,128)(2,1)}, bf16[2,32,1536]{2,1,0:T(8,128)(2,1)},...) custom-call(bf16[256,384]{1,0:T(8,128)(2,1)} %get-tuple-element.245.refs_0_.refs_8_, ...), custom_call_target="tpu_custom_call" | custom-call | flops 503316480 | bytes 4592640 | tf_op jit(solution)/shard_map/attend/pallas_call | solution.py:89
  223.4 6.6 %collective-permute-start.37 = (bf16[2,32,1536]{2,1,0:T(8,128)(2,1)}, bf16[2,32,1536]{2,1,0:T(8,128)(2,1)S(1)}, u32[]{:S(2)}, u32[]{:S(2)}) collective-permute-start(bf16[2,32,1536]{2,1,0:T(8,128)(2,1)} %get-tuple-element.253), channel_id=1, source_target_pairs={{0,4},{4,0},{8,12},{12,8},{1,5},{5,1},{9,13},{13,9},{2,6},{6,2},{1... | collective-permute-start | bytes 589832 | tf_op jit(solution)/shard_map/ppermute | solution.py:26
  236.3 10.3 %collective-permute-done.38.refs_4_ = bf16[2,32,1536]{2,1,0:T(8,128)(2,1)S(1)} collective-permute-done((bf16[2,32,1536]{2,1,0:T(8,128)(2,1)}, bf16[2,32,1536]{2,1,0:T(8,128)(2,1)S(1)}, u32[]{:S(2)}, u32[]{:S(2)}) %collective-permute-start.38) | collective-permute-done | bytes 196640 | tf_op jit(solution)/shard_map/ppermute | solution.py:26
  253.0 6.8 %collective-permute-done.40.refs_1_ = bf16[2,32,1536]{2,1,0:T(8,128)(2,1)S(1)} collective-permute-done((bf16[2,32,1536]{2,1,0:T(8,128)(2,1)S(1)}, bf16[2,32,1536]{2,1,0:T(8,128)(2,1)S(1)}, u32[]{:S(2)}, u32[]{:S(2)}) %collective-permute-start.40) | collective-permute-done | bytes 196640 | tf_op jit(solution)/shard_map/ppermute | solution.py:26
  259.8 7.9 %collective-permute-done.41.refs_2_ = bf16[2,32,1536]{2,1,0:T(8,128)(2,1)S(1)} collective-permute-done((bf16[2,32,1536]{2,1,0:T(8,128)(2,1)S(1)}, bf16[2,32,1536]{2,1,0:T(8,128)(2,1)S(1)}, u32[]{:S(2)}, u32[]{:S(2)}) %collective-permute-start.41) | collective-permute-done | bytes 196640 | tf_op jit(solution)/shard_map/ppermute | solution.py:26
  268.5 8.5 %feed.3 = (bf16[256,1024]{1,0:T(8,128)(2,1)}, bf16[256,1024]{1,0:T(8,128)(2,1)}, bf16[256,1024]{1,0:T(8,128)(2,1)}, bf16[256,1536]{1,0:T(8,128)(2,1)}, bf16[256,...) custom-call(bf16[2,32,1536]{2,1,0:T(8,128)(2,1)} %copy-done.15, ...), custom_call_target="tpu_custom_call" | custom-call | flops 2415919104 | bytes 9437184 | tf_op jit(solution)/shard_map/feed/pallas_call | solution.py:335
  277.1 9.7 %feed_back.2 = (bf16[256,1024]{1,0:T(8,128)(2,1)}, bf16[256,1024]{1,0:T(8,128)(2,1)}, bf16[256,1536]{1,0:T(8,128)(2,1)}, bf16[256,3072]{1,0:T(8,128)(2,1)}, bf16...) custom-call(bf16[2,32,1536]{2,1,0:T(8,128)(2,1)} %copy-done.8, ...), custom_call_target="tpu_custom_call" | custom-call | flops 2415919104 | bytes 9437184 | tf_op jit(solution)/shard_map/feed_back/pallas_call | solution.py:408
  293.3 7.0 %collective-permute-done.44.refs_4_ = bf16[2,32,1536]{2,1,0:T(8,128)(2,1)S(1)} collective-permute-done((bf16[2,32,1536]{2,1,0:T(8,128)(2,1)}, bf16[2,32,1536]{2,1,0:T(8,128)(2,1)S(1)}, u32[]{:S(2)}, u32[]{:S(2)}) %collective-permute-start.44) | collective-permute-done | bytes 196640 | tf_op jit(solution)/shard_map/ppermute | solution.py:26
  300.3 7.9 %collective-permute-done.45.refs_5_ = bf16[2,32,1536]{2,1,0:T(8,128)(2,1)S(1)} collective-permute-done((bf16[2,32,1536]{2,1,0:T(8,128)(2,1)}, bf16[2,32,1536]{2,1,0:T(8,128)(2,1)S(1)}, u32[]{:S(2)}, u32[]{:S(2)}) %collective-permute-start.45) | collective-permute-done | bytes 196640 | tf_op jit(solution)/shard_map/ppermute | solution.py:26
  310.7 8.4 %late_grad.2 = bf16[768,3072]{1,0:T(8,128)(2,1)} custom-call(bf16[256,1536]{1,0:T(8,128)(2,1)} %get-tuple-element.278.refs_0_, bf16[256,1536]{1,0:T(8,128)(2,1)} %get-tuple-element.279.refs_1_, bf16[256,3072]{1,0:T(8,128)(2,1)} %copy-done.29, bf16[256,3072]{1,0:T(8,128)(2,1)} %collective-permute-done.51.refs_3_.refs_7_.refs_8_, ...), custom_call_target="tpu_custom_call" | custom-call | flops 2415919104 | bytes 4718592 | tf_op jit(solution)/shard_map/late_grad/pallas_call | solution.py:655
  325.8 4.8 collective-permute-done.47.refs_1_
  330.7 9.9 %collective-permute-done.48.refs_2_ = bf16[2,32,1536]{2,1,0:T(8,128)(2,1)S(1)} collective-permute-done((bf16[2,32,1536]{2,1,0:T(8,128)(2,1)S(1)}, bf16[2,32,1536]{2,1,0:T(8,128)(2,1)S(1)}, u32[]{:S(2)}, u32[]{:S(2)}) %collective-permute-start.48) | collective-permute-done | bytes 196640 | tf_op jit(solution)/shard_map/ppermute | solution.py:26
  341.3 9.0 %attend_back.2 = (bf16[256,1536]{1,0:T(8,128)(2,1)}, bf16[256,768]{1,0:T(8,128)(2,1)}, bf16[256,384]{1,0:T(8,128)(2,1)}, bf16[2,128,384]{2,1,0:T(8,128)(2,1)}, b...) custom-call(bf16[2,32,1536]{2,1,0:T(8,128)(2,1)} %copy-done.25, ...), custom_call_target="tpu_custom_call" | custom-call | flops 503316480 | bytes 8912896 | tf_op jit(solution)/shard_map/attend_back/pallas_call | solution.py:89
  357.7 4.5 collective-permute-done.52.refs_2_
  365.7 5.2 project_back.2
  375.4 6.6 %collective-permute-done.57.refs_4_ = bf16[2,32,1536]{2,1,0:T(8,128)(2,1)S(1)} collective-permute-done((bf16[2,32,1536]{2,1,0:T(8,128)(2,1)}, bf16[2,32,1536]{2,1,0:T(8,128)(2,1)S(1)}, u32[]{:S(2)}, u32[]{:S(2)}) %collective-permute-start.57) | collective-permute-done | bytes 196640 | tf_op jit(solution)/shard_map/ppermute | solution.py:26
  382.0 8.1 %collective-permute-done.58.refs_5_ = bf16[2,32,1536]{2,1,0:T(8,128)(2,1)S(1)} collective-permute-done((bf16[2,32,1536]{2,1,0:T(8,128)(2,1)}, bf16[2,32,1536]{2,1,0:T(8,128)(2,1)S(1)}, u32[]{:S(2)}, u32[]{:S(2)}) %collective-permute-start.58) | collective-permute-done | bytes 196640 | tf_op jit(solution)/shard_map/ppermute | solution.py:26
  406.5 4.6 collective-permute-done.60.refs_1_
  411.1 10.0 %collective-permute-done.61.refs_2_ = bf16[2,32,1536]{2,1,0:T(8,128)(2,1)S(1)} collective-permute-done((bf16[2,32,1536]{2,1,0:T(8,128)(2,1)S(1)}, bf16[2,32,1536]{2,1,0:T(8,128)(2,1)S(1)}, u32[]{:S(2)}, u32[]{:S(2)}) %collective-permute-start.61) | collective-permute-done | bytes 196640 | tf_op jit(solution)/shard_map/ppermute | solution.py:26
  422.2 8.9 %feed_back.3 = (bf16[256,1024]{1,0:T(8,128)(2,1)}, bf16[256,1024]{1,0:T(8,128)(2,1)}, bf16[256,1536]{1,0:T(8,128)(2,1)}, bf16[256,3072]{1,0:T(8,128)(2,1)}, bf16...) custom-call(bf16[2,32,1536]{2,1,0:T(8,128)(2,1)} %copy-done.10, ...), custom_call_target="tpu_custom_call" | custom-call | flops 2415919104 | bytes 9437184 | tf_op jit(solution)/shard_map/feed_back/pallas_call | solution.py:408
  437.3 6.8 %collective-permute-done.66.refs_4_ = bf16[2,32,1536]{2,1,0:T(8,128)(2,1)S(1)} collective-permute-done((bf16[2,32,1536]{2,1,0:T(8,128)(2,1)}, bf16[2,32,1536]{2,1,0:T(8,128)(2,1)S(1)}, u32[]{:S(2)}, u32[]{:S(2)}) %collective-permute-start.66) | collective-permute-done | bytes 196640 | tf_op jit(solution)/shard_map/ppermute | solution.py:26
  444.0 8.1 %collective-permute-done.67.refs_5_ = bf16[2,32,1536]{2,1,0:T(8,128)(2,1)S(1)} collective-permute-done((bf16[2,32,1536]{2,1,0:T(8,128)(2,1)}, bf16[2,32,1536]{2,1,0:T(8,128)(2,1)S(1)}, u32[]{:S(2)}, u32[]{:S(2)}) %collective-permute-start.67) | collective-permute-done | bytes 196640 | tf_op jit(solution)/shard_map/ppermute | solution.py:26
  453.5 8.5 %late_grad.3 = bf16[768,3072]{1,0:T(8,128)(2,1)} custom-call(bf16[256,1536]{1,0:T(8,128)(2,1)} %get-tuple-element.340.refs_0_, bf16[256,1536]{1,0:T(8,128)(2,1)} %get-tuple-element.341.refs_1_, bf16[256,3072]{1,0:T(8,128)(2,1)} %collective-permute-done.73.refs_2_.refs_9_.refs_3_.refs_6_, bf16[256,3072]{1,0:T(8,128)(2,1)} %collective-permute-done.74.refs_3_.refs_7_.refs_8_, ...), custom_call_target="tpu_custom_call" | custom-call | flops 2415919104 | bytes 4718592 | tf_op jit(solution)/shard_map/late_grad/pallas_call | solution.py:655
  471.1 4.7 collective-permute-done.69.refs_1_
  475.8 10.0 %collective-permute-done.70.refs_2_ = bf16[2,32,1536]{2,1,0:T(8,128)(2,1)S(1)} collective-permute-done((bf16[2,32,1536]{2,1,0:T(8,128)(2,1)S(1)}, bf16[2,32,1536]{2,1,0:T(8,128)(2,1)S(1)}, u32[]{:S(2)}, u32[]{:S(2)}) %collective-permute-start.70) | collective-permute-done | bytes 196640 | tf_op jit(solution)/shard_map/ppermute | solution.py:26
  486.6 8.8 %attend_back.3 = (bf16[256,1536]{1,0:T(8,128)(2,1)}, bf16[256,768]{1,0:T(8,128)(2,1)}, bf16[256,384]{1,0:T(8,128)(2,1)}, bf16[2,128,384]{2,1,0:T(8,128)(2,1)}, b...) custom-call(bf16[2,32,1536]{2,1,0:T(8,128)(2,1)} %copy-done.16, ...), custom_call_target="tpu_custom_call" | custom-call | flops 503316480 | bytes 8912896 | tf_op jit(solution)/shard_map/attend_back/pallas_call | solution.py:89
  506.6 5.2 project_back.3
  512.4 4.7 collective-permute-start.79
  526.8 7.7 %collective-permute-done.80.refs_5_ = bf16[2,32,1536]{2,1,0:T(8,128)(2,1)S(1)} collective-permute-done((bf16[2,32,1536]{2,1,0:T(8,128)(2,1)}, bf16[2,32,1536]{2,1,0:T(8,128)(2,1)S(1)}, u32[]{:S(2)}, u32[]{:S(2)}) %collective-permute-start.80) | collective-permute-done | bytes 196640 | tf_op jit(solution)/shard_map/ppermute | solution.py:26
  563.2 8.4 %reduce-scatter.9.cloned.1.call-done.refs_0_ = bf16[192,1152]{1,0:T(8,128)(2,1)} async-done(((bf16[768,1152]{1,0:T(8,128)(2,1)}), bf16[192,1152]{1,0:T(8,128)(2,1)}) %reduce-scatter.9.cloned.1.call-update) | async-done | bytes 442384 | tf_op jit(solution)/shard_map/reduce_scatter | solution.py:821
  (454 shorter events, 229.5 us)
Async XLA Ops:
  7.2 110.1 %all-gather.4.cloned.1.call-start = ((), (), s32[]{:S(2)}) async-start(), calls=%async_computation.4 | async-start | bytes 5898240 | tf_op jit(solution)/shard_map/all_gather | solution.py:807
  11.7 22.9 %collective-permute-start.1 = (bf16[2,32,1536]{2,1,0:T(8,128)(2,1)S(1)}, bf16[2,32,1536]{2,1,0:T(8,128)(2,1)}, u32[]{:S(2)}, u32[]{:S(2)}) collective-permute-start(bf16[2,32,1536]{2,1,0:T(8,128)(2,1)S(1)} %concatenate.45.refs_0_.refs_12_), channel_id=1, source_target_pairs={{0,8},{4,12},{8,0},{12,4},{1,9},{5,13},{9,1},{13,5},{2,10},{6,14},... | collective-permute-start | bytes 589832 | tf_op jit(solution)/shard_map/ppermute | solution.py:26
  14.3 20.3 %collective-permute-start.2 = (bf16[2,32,1536]{2,1,0:T(8,128)(2,1)S(1)}, bf16[2,32,1536]{2,1,0:T(8,128)(2,1)}, u32[]{:S(2)}, u32[]{:S(2)}) collective-permute-start(bf16[2,32,1536]{2,1,0:T(8,128)(2,1)S(1)} %concatenate.45.refs_0_.refs_12_), channel_id=1, source_target_pairs={{0,12},{4,8},{8,4},{12,0},{1,13},{5,9},{9,5},{13,1},{2,14},{6,10},... | collective-permute-start | bytes 589832 | tf_op jit(solution)/shard_map/ppermute | solution.py:26
  23.9 16.5 %collective-permute-start.5 = (bf16[192,896]{1,0:T(8,128)(2,1)S(1)}, bf16[192,896]{1,0:T(8,128)(2,1)}, u32[]{:S(2)}, u32[]{:S(2)}) collective-permute-start(bf16[192,896]{1,0:T(8,128)(2,1)S(1)} %get-tuple-element.207.refs_0_), channel_id=1, source_target_pairs={{0,2},{1,3},{2,0},{3,1},{4,6},{5,7},{6,4},{7,5},{8,10},{9,11},{10,... | collective-permute-start | bytes 1032200 | tf_op jit(solution)/shard_map/ppermute | solution.py:26
  49.2 121.2 %all-gather.6.cloned.1.call-start = ((), (), s32[]{:S(2)}) async-start(), calls=%async_computation.5 | async-start | bytes 2457600 | tf_op jit(solution)/shard_map/all_gather | solution.py:807
  67.2 23.5 %collective-permute-start.17 = (bf16[768,384]{1,0:T(8,128)(2,1)}, bf16[768,384]{1,0:T(8,128)(2,1)S(1)}, u32[]{:S(2)}, u32[]{:S(2)}) collective-permute-start(bf16[768,384]{1,0:T(8,128)(2,1)} %place.3.refs_8_.refs_4_), channel_id=1, source_target_pairs={{0,16},{16,0},{1,17},{17,1},{2,18},{18,2},{3,19},{19,3},{4,20},{20... | collective-permute-start | bytes 1769480 | tf_op jit(solution)/shard_map/ppermute | solution.py:26
  98.0 17.4 %collective-permute-start.19 = (bf16[2,32,1536]{2,1,0:T(8,128)(2,1)}, bf16[2,32,1536]{2,1,0:T(8,128)(2,1)S(1)}, u32[]{:S(2)}, u32[]{:S(2)}) collective-permute-start(bf16[2,32,1536]{2,1,0:T(8,128)(2,1)} %get-tuple-element.227), channel_id=1, source_target_pairs={{0,8},{4,12},{8,0},{12,4},{1,9},{5,13},{9,1},{13,5},{2,10},{6,14},... | collective-permute-start | bytes 589832 | tf_op jit(solution)/shard_map/ppermute | solution.py:26
  117.3 21.3 %collective-permute-start.25 = (bf16[768,3072]{1,0:T(8,128)(2,1)}, bf16[768,3072]{1,0:T(8,128)(2,1)}, u32[]{:S(2)}, u32[]{:S(2)}) collective-permute-start(bf16[768,3072]{1,0:T(8,128)(2,1)} %all-gather.4.cloned.1.call-done.refs_4_.refs_6_.refs_8_), channel_id=1, source_target_pairs={{0,16},{16,0},{1,17},{17,1},{2,18},{18,2},{3,19},{19,3},{4,20},{20... | collective-permute-start | bytes 14155784 | tf_op jit(solution)/shard_map/ppermute | solution.py:26
  118.1 129.6 %all-gather.8.cloned.1.call-start = ((), (), s32[]{:S(2)}) async-start(), calls=%async_computation.6 | async-start | bytes 5898240 | tf_op jit(solution)/shard_map/all_gather | solution.py:807
  121.5 17.1 %collective-permute-start.22 = (bf16[2,32,1536]{2,1,0:T(8,128)(2,1)S(1)}, bf16[2,32,1536]{2,1,0:T(8,128)(2,1)S(1)}, u32[]{:S(2)}, u32[]{:S(2)}) collective-permute-start(bf16[2,32,1536]{2,1,0:T(8,128)(2,1)S(1)} %get-tuple-element.230.refs_0_), channel_id=1, source_target_pairs={{0,8},{4,12},{8,0},{12,4},{1,9},{5,13},{9,1},{13,5},{2,10},{6,14},... | collective-permute-start | bytes 589832 | tf_op jit(solution)/shard_map/ppermute | solution.py:26
  122.6 16.1 %collective-permute-start.23 = (bf16[2,32,1536]{2,1,0:T(8,128)(2,1)S(1)}, bf16[2,32,1536]{2,1,0:T(8,128)(2,1)S(1)}, u32[]{:S(2)}, u32[]{:S(2)}) collective-permute-start(bf16[2,32,1536]{2,1,0:T(8,128)(2,1)S(1)} %get-tuple-element.230.refs_0_), channel_id=1, source_target_pairs={{0,12},{4,8},{8,4},{12,0},{1,13},{5,9},{9,5},{13,1},{2,14},{6,10},... | collective-permute-start | bytes 589832 | tf_op jit(solution)/shard_map/ppermute | solution.py:26
  151.9 17.4 %collective-permute-start.27 = (bf16[2,32,1536]{2,1,0:T(8,128)(2,1)}, bf16[2,32,1536]{2,1,0:T(8,128)(2,1)S(1)}, u32[]{:S(2)}, u32[]{:S(2)}) collective-permute-start(bf16[2,32,1536]{2,1,0:T(8,128)(2,1)} %get-tuple-element.240), channel_id=1, source_target_pairs={{0,8},{4,12},{8,0},{12,4},{1,9},{5,13},{9,1},{13,5},{2,10},{6,14},... | collective-permute-start | bytes 589832 | tf_op jit(solution)/shard_map/ppermute | solution.py:26
  153.0 16.3 %collective-permute-start.28 = (bf16[2,32,1536]{2,1,0:T(8,128)(2,1)}, bf16[2,32,1536]{2,1,0:T(8,128)(2,1)S(1)}, u32[]{:S(2)}, u32[]{:S(2)}) collective-permute-start(bf16[2,32,1536]{2,1,0:T(8,128)(2,1)} %get-tuple-element.241), channel_id=1, source_target_pairs={{0,12},{4,8},{8,4},{12,0},{1,13},{5,9},{9,5},{13,1},{2,14},{6,10},... | collective-permute-start | bytes 589832 | tf_op jit(solution)/shard_map/ppermute | solution.py:26
  170.4 221.7 %reduce-scatter.5.cloned.1.call-start = ((), (), s32[]{:S(2)}) async-start(), calls=%async_computation.7 | async-start | bytes 5898240 | tf_op jit(solution)/shard_map/reduce_scatter | solution.py:821
  170.8 20.3 %collective-permute-start.32 = (bf16[768,1280]{1,0:T(8,128)(2,1)}, bf16[768,1280]{1,0:T(8,128)(2,1)S(1)}, u32[]{:S(2)}, u32[]{:S(2)}) collective-permute-start(bf16[768,1280]{1,0:T(8,128)(2,1)} %all-gather.6.cloned.1.call-done.refs_4_.refs_6_.refs_8_.refs_5_.refs_7_), channel_id=1, source_target_pairs={{0,16},{16,0},{1,17},{17,1},{2,18},{18,2},{3,19},{19,3},{4,20},{20... | collective-permute-start | bytes 5898248 | tf_op jit(solution)/shard_map/ppermute | solution.py:26
  174.0 17.1 %collective-permute-start.30 = (bf16[2,32,1536]{2,1,0:T(8,128)(2,1)S(1)}, bf16[2,32,1536]{2,1,0:T(8,128)(2,1)S(1)}, u32[]{:S(2)}, u32[]{:S(2)}) collective-permute-start(bf16[2,32,1536]{2,1,0:T(8,128)(2,1)S(1)} %add_out.2.refs_0_.refs_12_), channel_id=1, source_target_pairs={{0,8},{4,12},{8,0},{12,4},{1,9},{5,13},{9,1},{13,5},{2,10},{6,14},... | collective-permute-start | bytes 589832 | tf_op jit(solution)/shard_map/ppermute | solution.py:26
  175.0 16.1 %collective-permute-start.31 = (bf16[2,32,1536]{2,1,0:T(8,128)(2,1)S(1)}, bf16[2,32,1536]{2,1,0:T(8,128)(2,1)S(1)}, u32[]{:S(2)}, u32[]{:S(2)}) collective-permute-start(bf16[2,32,1536]{2,1,0:T(8,128)(2,1)S(1)} %add_out.2.refs_0_.refs_12_), channel_id=1, source_target_pairs={{0,12},{4,8},{8,4},{12,0},{1,13},{5,9},{9,5},{13,1},{2,14},{6,10},... | collective-permute-start | bytes 589832 | tf_op jit(solution)/shard_map/ppermute | solution.py:26
  229.9 16.6 %collective-permute-start.38 = (bf16[2,32,1536]{2,1,0:T(8,128)(2,1)}, bf16[2,32,1536]{2,1,0:T(8,128)(2,1)S(1)}, u32[]{:S(2)}, u32[]{:S(2)}) collective-permute-start(bf16[2,32,1536]{2,1,0:T(8,128)(2,1)} %get-tuple-element.254), channel_id=1, source_target_pairs={{0,8},{4,12},{8,0},{12,4},{1,9},{5,13},{9,1},{13,5},{2,10},{6,14},... | collective-permute-start | bytes 589832 | tf_op jit(solution)/shard_map/ppermute | solution.py:26
  231.0 15.6 %collective-permute-start.39 = (bf16[2,32,1536]{2,1,0:T(8,128)(2,1)}, bf16[2,32,1536]{2,1,0:T(8,128)(2,1)S(1)}, u32[]{:S(2)}, u32[]{:S(2)}) collective-permute-start(bf16[2,32,1536]{2,1,0:T(8,128)(2,1)} %get-tuple-element.255), channel_id=1, source_target_pairs={{0,12},{4,8},{8,4},{12,0},{1,13},{5,9},{9,5},{13,1},{2,14},{6,10},... | collective-permute-start | bytes 589832 | tf_op jit(solution)/shard_map/ppermute | solution.py:26
  247.8 19.9 %collective-permute-start.43 = (bf16[768,3072]{1,0:T(8,128)(2,1)}, bf16[768,3072]{1,0:T(8,128)(2,1)}, u32[]{:S(2)}, u32[]{:S(2)}) collective-permute-start(bf16[768,3072]{1,0:T(8,128)(2,1)} %all-gather.8.cloned.1.call-done.refs_4_.refs_6_.refs_8_), channel_id=1, source_target_pairs={{0,16},{16,0},{1,17},{17,1},{2,18},{18,2},{3,19},{19,3},{4,20},{20... | collective-permute-start | bytes 14155784 | tf_op jit(solution)/shard_map/ppermute | solution.py:26
  250.6 17.1 %collective-permute-start.41 = (bf16[2,32,1536]{2,1,0:T(8,128)(2,1)S(1)}, bf16[2,32,1536]{2,1,0:T(8,128)(2,1)S(1)}, u32[]{:S(2)}, u32[]{:S(2)}) collective-permute-start(bf16[2,32,1536]{2,1,0:T(8,128)(2,1)S(1)} %get-tuple-element.257.refs_0_), channel_id=1, source_target_pairs={{0,8},{4,12},{8,0},{12,4},{1,9},{5,13},{9,1},{13,5},{2,10},{6,14},... | collective-permute-start | bytes 589832 | tf_op jit(solution)/shard_map/ppermute | solution.py:26
  251.6 16.1 %collective-permute-start.42 = (bf16[2,32,1536]{2,1,0:T(8,128)(2,1)S(1)}, bf16[2,32,1536]{2,1,0:T(8,128)(2,1)S(1)}, u32[]{:S(2)}, u32[]{:S(2)}) collective-permute-start(bf16[2,32,1536]{2,1,0:T(8,128)(2,1)S(1)} %get-tuple-element.257.refs_0_), channel_id=1, source_target_pairs={{0,12},{4,8},{8,4},{12,0},{1,13},{5,9},{9,5},{13,1},{2,14},{6,10},... | collective-permute-start | bytes 589832 | tf_op jit(solution)/shard_map/ppermute | solution.py:26
  277.0 32.5 %collective-permute-start.50 = (bf16[256,3072]{1,0:T(8,128)(2,1)}, bf16[256,3072]{1,0:T(8,128)(2,1)S(1)}, u32[]{:S(2)}, u32[]{:S(2)}) collective-permute-start(bf16[256,3072]{1,0:T(8,128)(2,1)} %get-tuple-element.276), channel_id=1, source_target_pairs={{0,16},{16,0},{1,17},{17,1},{2,18},{18,2},{3,19},{19,3},{4,20},{20... | collective-permute-start | bytes 4718600 | tf_op jit(solution)/shard_map/ppermute | solution.py:26
  286.8 22.8 %collective-permute-start.51 = (bf16[256,3072]{1,0:T(8,128)(2,1)}, bf16[256,3072]{1,0:T(8,128)(2,1)}, u32[]{:S(2)}, u32[]{:S(2)}) collective-permute-start(bf16[256,3072]{1,0:T(8,128)(2,1)} %get-tuple-element.277), channel_id=1, source_target_pairs={{0,16},{16,0},{1,17},{17,1},{2,18},{18,2},{3,19},{19,3},{4,20},{20... | collective-permute-start | bytes 4718600 | tf_op jit(solution)/shard_map/ppermute | solution.py:26
  290.8 17.3 %collective-permute-start.45 = (bf16[2,32,1536]{2,1,0:T(8,128)(2,1)}, bf16[2,32,1536]{2,1,0:T(8,128)(2,1)S(1)}, u32[]{:S(2)}, u32[]{:S(2)}) collective-permute-start(bf16[2,32,1536]{2,1,0:T(8,128)(2,1)} %get-tuple-element.268), channel_id=1, source_target_pairs={{0,8},{4,12},{8,0},{12,4},{1,9},{5,13},{9,1},{13,5},{2,10},{6,14},... | collective-permute-start | bytes 589832 | tf_op jit(solution)/shard_map/ppermute | solution.py:26
  291.8 16.3 %collective-permute-start.46 = (bf16[2,32,1536]{2,1,0:T(8,128)(2,1)}, bf16[2,32,1536]{2,1,0:T(8,128)(2,1)S(1)}, u32[]{:S(2)}, u32[]{:S(2)}) collective-permute-start(bf16[2,32,1536]{2,1,0:T(8,128)(2,1)} %get-tuple-element.269), channel_id=1, source_target_pairs={{0,12},{4,8},{8,4},{12,0},{1,13},{5,9},{9,5},{13,1},{2,14},{6,10},... | collective-permute-start | bytes 589832 | tf_op jit(solution)/shard_map/ppermute | solution.py:26
  319.1 134.4 %reduce-scatter.7.cloned.1.call-start = ((), (), s32[]{:S(2)}) async-start(), calls=%async_computation.8 | async-start | bytes 2211840 | tf_op jit(solution)/shard_map/reduce_scatter | solution.py:821
  323.4 17.2 %collective-permute-start.48 = (bf16[2,32,1536]{2,1,0:T(8,128)(2,1)S(1)}, bf16[2,32,1536]{2,1,0:T(8,128)(2,1)S(1)}, u32[]{:S(2)}, u32[]{:S(2)}) collective-permute-start(bf16[2,32,1536]{2,1,0:T(8,128)(2,1)S(1)} %get-tuple-element.285.refs_0_), channel_id=1, source_target_pairs={{0,8},{4,12},{8,0},{12,4},{1,9},{5,13},{9,1},{13,5},{2,10},{6,14},... | collective-permute-start | bytes 589832 | tf_op jit(solution)/shard_map/ppermute | solution.py:26
  324.4 16.2 %collective-permute-start.49 = (bf16[2,32,1536]{2,1,0:T(8,128)(2,1)S(1)}, bf16[2,32,1536]{2,1,0:T(8,128)(2,1)S(1)}, u32[]{:S(2)}, u32[]{:S(2)}) collective-permute-start(bf16[2,32,1536]{2,1,0:T(8,128)(2,1)S(1)} %get-tuple-element.285.refs_0_), channel_id=1, source_target_pairs={{0,12},{4,8},{8,4},{12,0},{1,13},{5,9},{9,5},{13,1},{2,14},{6,10},... | collective-permute-start | bytes 589832 | tf_op jit(solution)/shard_map/ppermute | solution.py:26
  362.2 30.0 %collective-permute-start.64 = (bf16[256,768]{1,0:T(8,128)(2,1)}, bf16[256,768]{1,0:T(8,128)(2,1)S(1)}, u32[]{:S(2)}, u32[]{:S(2)}) collective-permute-start(bf16[256,768]{1,0:T(8,128)(2,1)} %get-tuple-element.311), channel_id=1, source_target_pairs={{0,16},{16,0},{1,17},{17,1},{2,18},{18,2},{3,19},{19,3},{4,20},{20... | collective-permute-start | bytes 1179656 | tf_op jit(solution)/shard_map/ppermute | solution.py:26
  370.9 21.3 %collective-permute-start.65 = (bf16[256,768]{1,0:T(8,128)(2,1)}, bf16[256,768]{1,0:T(8,128)(2,1)S(1)}, u32[]{:S(2)}, u32[]{:S(2)}) collective-permute-start(bf16[256,768]{1,0:T(8,128)(2,1)} %get-tuple-element.318.refs_5_), channel_id=1, source_target_pairs={{0,16},{16,0},{1,17},{17,1},{2,18},{18,2},{3,19},{19,3},{4,20},{20... | collective-permute-start | bytes 1179656 | tf_op jit(solution)/shard_map/ppermute | solution.py:26
  372.7 17.3 %collective-permute-start.58 = (bf16[2,32,1536]{2,1,0:T(8,128)(2,1)}, bf16[2,32,1536]{2,1,0:T(8,128)(2,1)S(1)}, u32[]{:S(2)}, u32[]{:S(2)}) collective-permute-start(bf16[2,32,1536]{2,1,0:T(8,128)(2,1)} %get-tuple-element.306), channel_id=1, source_target_pairs={{0,8},{4,12},{8,0},{12,4},{1,9},{5,13},{9,1},{13,5},{2,10},{6,14},... | collective-permute-start | bytes 589832 | tf_op jit(solution)/shard_map/ppermute | solution.py:26
  374.0 16.1 %collective-permute-start.59 = (bf16[2,32,1536]{2,1,0:T(8,128)(2,1)}, bf16[2,32,1536]{2,1,0:T(8,128)(2,1)S(1)}, u32[]{:S(2)}, u32[]{:S(2)}) collective-permute-start(bf16[2,32,1536]{2,1,0:T(8,128)(2,1)} %get-tuple-element.307), channel_id=1, source_target_pairs={{0,12},{4,8},{8,4},{12,0},{1,13},{5,9},{9,5},{13,1},{2,14},{6,10},... | collective-permute-start | bytes 589832 | tf_op jit(solution)/shard_map/ppermute | solution.py:26
  397.4 155.4 %reduce-scatter.11.cloned.1.call-start = ((), (), s32[]{:S(2)}) async-start(), calls=%async_computation.10 | async-start | bytes 5898240 | tf_op jit(solution)/shard_map/reduce_scatter | solution.py:821
  398.6 22.5 %collective-permute-start.63 = (bf16[192,3072]{1,0:T(8,128)(2,1)S(1)}, bf16[192,3072]{1,0:T(8,128)(2,1)S(1)}, u32[]{:S(2)}, u32[]{:S(2)}) collective-permute-start(bf16[192,3072]{1,0:T(8,128)(2,1)S(1)} %copy-done.30), channel_id=1, source_target_pairs={{0,16},{1,17},{2,18},{3,19},{4,20},{5,21},{6,22},{7,23},{8,24},{9,... | collective-permute-start | bytes 3538952 | tf_op jit(solution)/shard_map/ppermute | solution.py:30
  404.0 17.0 %collective-permute-start.61 = (bf16[2,32,1536]{2,1,0:T(8,128)(2,1)S(1)}, bf16[2,32,1536]{2,1,0:T(8,128)(2,1)S(1)}, u32[]{:S(2)}, u32[]{:S(2)}) collective-permute-start(bf16[2,32,1536]{2,1,0:T(8,128)(2,1)S(1)} %get-tuple-element.321.refs_0_.refs_2_), channel_id=1, source_target_pairs={{0,8},{4,12},{8,0},{12,4},{1,9},{5,13},{9,1},{13,5},{2,10},{6,14},... | collective-permute-start | bytes 589832 | tf_op jit(solution)/shard_map/ppermute | solution.py:26
  404.6 16.5 %collective-permute-start.62 = (bf16[2,32,1536]{2,1,0:T(8,128)(2,1)S(1)}, bf16[2,32,1536]{2,1,0:T(8,128)(2,1)S(1)}, u32[]{:S(2)}, u32[]{:S(2)}) collective-permute-start(bf16[2,32,1536]{2,1,0:T(8,128)(2,1)S(1)} %get-tuple-element.321.refs_0_.refs_2_), channel_id=1, source_target_pairs={{0,12},{4,8},{8,4},{12,0},{1,13},{5,9},{9,5},{13,1},{2,14},{6,10},... | collective-permute-start | bytes 589832 | tf_op jit(solution)/shard_map/ppermute | solution.py:26
  406.5 47.0 %collective-permute-start.73 = (bf16[256,3072]{1,0:T(8,128)(2,1)}, bf16[256,3072]{1,0:T(8,128)(2,1)}, u32[]{:S(2)}, u32[]{:S(2)}) collective-permute-start(bf16[256,3072]{1,0:T(8,128)(2,1)} %get-tuple-element.338), channel_id=1, source_target_pairs={{0,16},{16,0},{1,17},{17,1},{2,18},{18,2},{3,19},{19,3},{4,20},{20... | collective-permute-start | bytes 4718600 | tf_op jit(solution)/shard_map/ppermute | solution.py:26
  431.2 22.3 %collective-permute-start.74 = (bf16[256,3072]{1,0:T(8,128)(2,1)}, bf16[256,3072]{1,0:T(8,128)(2,1)}, u32[]{:S(2)}, u32[]{:S(2)}) collective-permute-start(bf16[256,3072]{1,0:T(8,128)(2,1)} %get-tuple-element.339), channel_id=1, source_target_pairs={{0,16},{16,0},{1,17},{17,1},{2,18},{18,2},{3,19},{19,3},{4,20},{20... | collective-permute-start | bytes 4718600 | tf_op jit(solution)/shard_map/ppermute | solution.py:26
  434.8 17.3 %collective-permute-start.67 = (bf16[2,32,1536]{2,1,0:T(8,128)(2,1)}, bf16[2,32,1536]{2,1,0:T(8,128)(2,1)S(1)}, u32[]{:S(2)}, u32[]{:S(2)}) collective-permute-start(bf16[2,32,1536]{2,1,0:T(8,128)(2,1)} %get-tuple-element.329), channel_id=1, source_target_pairs={{0,8},{4,12},{8,0},{12,4},{1,9},{5,13},{9,1},{13,5},{2,10},{6,14},... | collective-permute-start | bytes 589832 | tf_op jit(solution)/shard_map/ppermute | solution.py:26
  435.4 16.8 %collective-permute-start.68 = (bf16[2,32,1536]{2,1,0:T(8,128)(2,1)}, bf16[2,32,1536]{2,1,0:T(8,128)(2,1)S(1)}, u32[]{:S(2)}, u32[]{:S(2)}) collective-permute-start(bf16[2,32,1536]{2,1,0:T(8,128)(2,1)} %get-tuple-element.330), channel_id=1, source_target_pairs={{0,12},{4,8},{8,4},{12,0},{1,13},{5,9},{9,5},{13,1},{2,14},{6,10},... | collective-permute-start | bytes 589832 | tf_op jit(solution)/shard_map/ppermute | solution.py:26
  462.1 109.5 %reduce-scatter.9.cloned.1.call-start = ((), (), s32[]{:S(2)}) async-start(), calls=%async_computation.9 | async-start | bytes 2211840 | tf_op jit(solution)/shard_map/reduce_scatter | solution.py:821
  463.0 22.7 %collective-permute-start.72 = (bf16[192,1152]{1,0:T(8,128)(2,1)S(1)}, bf16[192,1152]{1,0:T(8,128)(2,1)S(1)}, u32[]{:S(2)}, u32[]{:S(2)}) collective-permute-start(bf16[192,1152]{1,0:T(8,128)(2,1)S(1)} %copy-done.49), channel_id=1, source_target_pairs={{0,16},{1,17},{2,18},{3,19},{4,20},{5,21},{6,22},{7,23},{8,24},{9,... | collective-permute-start | bytes 1327112 | tf_op jit(solution)/shard_map/ppermute | solution.py:30
  468.6 17.1 %collective-permute-start.70 = (bf16[2,32,1536]{2,1,0:T(8,128)(2,1)S(1)}, bf16[2,32,1536]{2,1,0:T(8,128)(2,1)S(1)}, u32[]{:S(2)}, u32[]{:S(2)}) collective-permute-start(bf16[2,32,1536]{2,1,0:T(8,128)(2,1)S(1)} %get-tuple-element.347.refs_0_), channel_id=1, source_target_pairs={{0,8},{4,12},{8,0},{12,4},{1,9},{5,13},{9,1},{13,5},{2,10},{6,14},... | collective-permute-start | bytes 589832 | tf_op jit(solution)/shard_map/ppermute | solution.py:26
  469.2 16.5 %collective-permute-start.71 = (bf16[2,32,1536]{2,1,0:T(8,128)(2,1)S(1)}, bf16[2,32,1536]{2,1,0:T(8,128)(2,1)S(1)}, u32[]{:S(2)}, u32[]{:S(2)}) collective-permute-start(bf16[2,32,1536]{2,1,0:T(8,128)(2,1)S(1)} %get-tuple-element.347.refs_0_), channel_id=1, source_target_pairs={{0,12},{4,8},{8,4},{12,0},{1,13},{5,9},{9,5},{13,1},{2,14},{6,10},... | collective-permute-start | bytes 589832 | tf_op jit(solution)/shard_map/ppermute | solution.py:26
  500.9 19.2 %collective-permute-start.82 = (bf16[256,768]{1,0:T(8,128)(2,1)}, bf16[256,768]{1,0:T(8,128)(2,1)S(1)}, u32[]{:S(2)}, u32[]{:S(2)}) collective-permute-start(bf16[256,768]{1,0:T(8,128)(2,1)} %get-tuple-element.368), channel_id=1, source_target_pairs={{0,16},{16,0},{1,17},{17,1},{2,18},{18,2},{3,19},{19,3},{4,20},{20... | collective-permute-start | bytes 1179656 | tf_op jit(solution)/shard_map/ppermute | solution.py:26
  517.1 17.3 %collective-permute-start.80 = (bf16[2,32,1536]{2,1,0:T(8,128)(2,1)}, bf16[2,32,1536]{2,1,0:T(8,128)(2,1)S(1)}, u32[]{:S(2)}, u32[]{:S(2)}) collective-permute-start(bf16[2,32,1536]{2,1,0:T(8,128)(2,1)} %get-tuple-element.365), channel_id=1, source_target_pairs={{0,8},{4,12},{8,0},{12,4},{1,9},{5,13},{9,1},{13,5},{2,10},{6,14},... | collective-permute-start | bytes 589832 | tf_op jit(solution)/shard_map/ppermute | solution.py:26
  518.6 15.8 %collective-permute-start.81 = (bf16[2,32,1536]{2,1,0:T(8,128)(2,1)}, bf16[2,32,1536]{2,1,0:T(8,128)(2,1)S(1)}, u32[]{:S(2)}, u32[]{:S(2)}) collective-permute-start(bf16[2,32,1536]{2,1,0:T(8,128)(2,1)} %get-tuple-element.366), channel_id=1, source_target_pairs={{0,12},{4,8},{8,4},{12,0},{1,13},{5,9},{9,5},{13,1},{2,14},{6,10},... | collective-permute-start | bytes 589832 | tf_op jit(solution)/shard_map/ppermute | solution.py:26
  (147 other events, 1496.8 us)
Sparse Core Ops, SparseCore 0:
  49.3 67.9 all-gather.3
  119.7 34.2 all-gather.5
  170.6 64.3 all-gather.7
  319.2 60.1 reduce-scatter.4
  397.5 32.8 reduce-scatter.6
  462.2 58.0 reduce-scatter.10
  536.1 35.3 reduce-scatter.8
